TPU v7x, 32 devices: a whole 2x2x4 slice. The times are simulated.
32 devices in a mesh: tm: 8 (over y, x, core), space: 4 (over z).
Axes of the slice: x: 2, y: 2, z: 4, core: 2. Of those that a mesh axis runs over, the one named last changes fastest.
Arguments:
- frames_in: bfloat16 [64, 32, 64, 256], P('tm', 'space'), may hold values from -6 to 6
- cotangent: bfloat16 [64, 32, 64, 256], P('tm', 'space'), may hold values from -6 to 6
- spatial: bfloat16 [3, 3, 256, 256], replicated, may hold values from -0.125 to 0.125
- temporal: bfloat16 [3, 256, 256], replicated, may hold values from -0.375 to 0.375
- norm_gain: float32 [256], replicated, may hold values from 0.5 to 2
- norm_shift: float32 [256], replicated, may hold values from -3 to 3
- clip_frames: int32 [2], replicated, may hold values from 8 to 48, as said below
- dilation: int32 [2], replicated, may hold values from 1 to 8, as said below
Outputs:
- out_frames: bfloat16 [64, 32, 64, 256], P('tm', 'space')
- in_grad: bfloat16 [64, 32, 64, 256], P('tm', 'space')
- spatial_grad: float32 [3, 3, 256, 256], replicated
- temporal_grad: float32 [3, 256, 256], replicated
Inputs may be any that keep to these rules, and one draw needn't show every extreme that they name: `clip_frames`: the two clips are packed in order from slot 0 and fill at least 56 and at most 64 slots together; one of them has exactly 48 frames. One of the two clips has dilation 8.
All inputs are finite; a program needn't handle non-finite values.
Results may differ from a plain program's by a relative error of at most 0.0055.
Values may be sent and summed in bfloat16 or wider, within the bound.
No kernel may reach another device: no remote copies, remote signals or barrier semaphores. Data moves between devices by JAX's collectives and lax.ppermute only.
A program may use at most 128 MiB of HBM per device.

v0:
```python
import functools

import jax
import jax.numpy as jnp
from jax import lax
from jax.experimental import pallas as pl
from jax.experimental.pallas import tpu as pltpu
from jax.sharding import PartitionSpec as P

GROUPS = 32
NORM_EPS = 1e-05
BF16 = jnp.bfloat16
F32 = jnp.float32
MIB = 2**20


def call(kernel, name, operands, out_shape, flops=0, moved=0, scratch=(), grant=14):
    vmem = pl.BlockSpec(memory_space=pltpu.VMEM)
    smem = pl.BlockSpec(memory_space=pltpu.SMEM)
    return pl.pallas_call(
        kernel,
        in_specs=[smem if x.dtype == jnp.int32 else vmem for x in operands],
        out_specs=jax.tree.map(lambda _: vmem, out_shape),
        out_shape=out_shape,
        scratch_shapes=list(scratch),
        compiler_params=pltpu.CompilerParams(vmem_limit_bytes=grant * MIB),
        cost_estimate=pl.CostEstimate(flops=int(flops), bytes_accessed=int(moved), transcendentals=0),
        name=name,
    )(*operands)


def dot(a, b):
    return jnp.dot(a, b, preferred_element_type=F32)


def dot_rows(a, b):
    return lax.dot_general(a, b, (((0,), (0,)), ((), ())), preferred_element_type=F32)


def group_total(row, group_size):
    channels = row.shape[-1]
    lane = lax.broadcasted_iota(jnp.int32, row.shape, 1)
    step = 1
    while step < group_size:
        up = pltpu.roll(row, channels - step, axis=1)
        down = pltpu.roll(row, step, axis=1)
        row = row + jnp.where((lane & step) == 0, up, down)
        step *= 2
    return row


def frame_stats(part_refs, f, entries, group_size):
    total = part_refs[0][f]
    for ref in part_refs[1:]:
        total = total + ref[f]
    return group_total(total, group_size) / entries


def sigmoid(x):
    return 0.5 * jnp.tanh(0.5 * x) + 0.5


def mean_and_inv(part_refs, f, entries, group_size):
    both = frame_stats(part_refs, f, entries, group_size)
    mean = both[0:1]
    inv = lax.rsqrt(both[1:2] - mean * mean + NORM_EPS)
    return mean, inv


def column_sums(first, second):
    return jnp.concatenate(
        [jnp.sum(first, axis=0, keepdims=True), jnp.sum(second, axis=0, keepdims=True)], axis=0
    )


def put_windows(above, mid, below, lhs_ref, at, order):
    width, (pixels, channels) = above.shape[0], mid.shape
    first, mid_at, last = (slice(k * channels, (k + 1) * channels) for k in order)
    lhs_ref[at : at + width, first] = above
    lhs_ref[at + width : at + pixels, first] = mid[: pixels - width]
    lhs_ref[at : at + pixels, mid_at] = mid
    lhs_ref[at : at + pixels - width, last] = mid[width:]
    lhs_ref[at + pixels - width : at + pixels, last] = below


def from_left(y, width):
    col = lax.broadcasted_iota(jnp.int32, y.shape, 0) & (width - 1)
    return jnp.where(col == 0, 0.0, pltpu.roll(y, 1, axis=0))


def from_right(y, width):
    col = lax.broadcasted_iota(jnp.int32, y.shape, 0) & (width - 1)
    return jnp.where(col == width - 1, 0.0, pltpu.roll(y, y.shape[0] - 1, axis=0))


def slot_sources(clip_ref, dil_ref, local, frames):
    slot = lax.axis_index("tm") * frames + local
    start1 = clip_ref[0]
    filled = start1 + clip_ref[1]
    in_first = slot < start1
    d = jnp.where(in_first, dil_ref[0], dil_ref[1])
    low = jnp.where(in_first, 0, start1)
    high = jnp.where(in_first, start1, filled)
    used = slot < filled
    later, earlier = local + d, local - d
    later_live = used & (slot + d < high)
    earlier_live = used & (slot - d >= low)
    later_which = jnp.where(later_live, jnp.where(later < frames, 1, 2), 0)
    earlier_which = jnp.where(earlier_live, jnp.where(earlier >= 0, 1, 2), 0)
    return (later, later_which), (earlier, earlier_which), used


def gather_taps(clip_ref, dil_ref, local, own, nxt, prv, corner, cat_ref, at, up_slot):
    frames, pixels, channels = own.shape
    later, earlier, used = slot_sources(clip_ref, dil_ref, local, frames)
    me, half = lax.axis_index("tm"), frames // 2

    def put(slot, ref, index):
        cat_ref[pl.ds(at, pixels), slot * channels : (slot + 1) * channels] = ref[index]

    def clear(slot):
        cat_ref[pl.ds(at, pixels), slot * channels : (slot + 1) * channels] = jnp.zeros((pixels, channels), BF16)

    for slot, (index, which), other, shift, turn in (
        (up_slot, later, nxt, -frames, 3),
        (2 - up_slot, earlier, prv, frames, 4),
    ):
        beyond = which == 2
        there = jnp.clip(index + shift, 0, frames - 1)
        pl.when(which == 1)(functools.partial(put, slot, own, jnp.clip(index, 0, frames - 1)))
        pl.when(which == 0)(functools.partial(clear, slot))
        if corner:
            by_corner = beyond & (me == turn)
            low, high = by_corner & (there < half), by_corner & (there >= half)
            pl.when(low)(functools.partial(put, slot, corner[0], jnp.minimum(there, half - 1)))
            pl.when(high)(functools.partial(put, slot, corner[1], jnp.maximum(there - half, 0)))
            beyond = beyond & (me != turn)
        pl.when(beyond)(functools.partial(put, slot, other, there))
    pl.when(used)(functools.partial(put, 1, own, local))
    pl.when(jnp.logical_not(used))(functools.partial(clear, 1))


def loop(count, body):
    def step(k, carry):
        body(k)
        return carry

    lax.fori_loop(0, count, step, 0)


def conv_kernel(x_ref, above_ref, below_ref, w_ref, out_ref, sums_ref, lhs_ref):
    frames, rows, width, channels = x_ref.shape
    pixels = rows * width

    def body(pair):
        for b in range(2):
            f = 2 * pair + b
            mid = x_ref[f].reshape(pixels, channels)
            put_windows(above_ref[f, 0], mid, below_ref[f, 0], lhs_ref, b * pixels, (0, 1, 2))
        lhs = lhs_ref[...]
        y = [dot(lhs, w_ref[:, j].reshape(3 * channels, channels)) for j in range(3)]
        out = y[1] + from_left(y[0], width) + from_right(y[2], width)
        for b in range(2):
            one = out[b * pixels : (b + 1) * pixels]
            out_ref[2 * pair + b] = one
            sums_ref[2 * pair + b] = column_sums(one, one * one)

    loop(frames // 2, body)


def act_kernel(n, entries, group_size, clip_ref, *refs):
    parts, (conv_ref, gain_ref, shift_ref, act_ref, normed_ref, slope_ref) = refs[:n], refs[n:]
    frames = conv_ref.shape[0]
    first = lax.axis_index("tm") * frames
    filled = clip_ref[0] + clip_ref[1]

    def body(f):
        mean, inv = mean_and_inv(parts, f, entries, group_size)
        normed = (conv_ref[f] - mean) * inv
        shaped = normed * gain_ref[...] + shift_ref[...]
        sig = sigmoid(shaped)
        act_ref[f] = jnp.where(first + f < filled, shaped * sig, 0.0).astype(BF16)
        normed_ref[f] = normed.astype(BF16)
        slope_ref[f] = (sig * (1.0 + shaped * (1.0 - sig)) * gain_ref[...]).astype(BF16)

    loop(frames, body)


def turn_kernel(x_ref, above_ref, below_ref, xt_ref, lhs_ref):
    frames, rows, width, channels = x_ref.shape
    pixels = rows * width

    def body(f):
        mid = x_ref[f].reshape(pixels, channels)
        put_windows(above_ref[f, 0], mid, below_ref[f, 0], lhs_ref, 0, (0, 1, 2))
        lanes = pl.ds(pl.multiple_of(f * pixels, pixels), pixels)
        for i in range(3):
            block = slice(i * channels, (i + 1) * channels)
            xt_ref[block, lanes] = lhs_ref[:, block].T

    loop(frames, body)


def turn_weights_kernel(spatial_ref, temporal_ref, back_ref, out_ref):
    channels = spatial_ref.shape[-1]
    for i in range(3):
        rows = slice(i * channels, (i + 1) * channels)
        out_ref[rows] = temporal_ref[i].T
        for j in range(3):
            back_ref[j, rows] = spatial_ref[i, j].T


def grad_act_kernel(corners, clip_ref, dil_ref, own, nxt, prv, *refs):
    corner, (tw_ref, normed_ref, slope_ref, ga_ref, cat_ref, sums_ref) = refs[:corners], refs[corners:]
    frames, pixels, _ = own.shape

    def body(pair):
        rows = pl.ds(pl.multiple_of(2 * pair * pixels, 2 * pixels), 2 * pixels)
        for b in range(2):
            at = pl.multiple_of((2 * pair + b) * pixels, pixels)
            gather_taps(clip_ref, dil_ref, 2 * pair + b, own, nxt, prv, corner, cat_ref, at, 0)
        grad_act = dot(cat_ref[rows], tw_ref[...]).astype(BF16)
        for b in range(2):
            f = 2 * pair + b
            one = grad_act[b * pixels : (b + 1) * pixels]
            ga_ref[f] = one
            gn = one.astype(F32) * slope_ref[f].astype(F32)
            sums_ref[f] = column_sums(gn, gn * normed_ref[f].astype(F32))

    loop(frames // 2, body)


def temporal_grad_kernel(act_ref, cat_ref, out_ref):
    frames, pixels, channels = act_ref.shape
    out_ref[...] = dot_rows(act_ref[...].reshape(frames * pixels, channels), cat_ref[...])


def norm_back_kernel(n, m, entries, group_size, normed_ref, slope_ref, ga_ref, *refs):
    parts, grad_parts = refs[:n], refs[n : n + m]
    g_ref, first_ref, last_ref, moved_ref = refs[n + m :]
    _, pixels, channels = normed_ref.shape
    width = first_ref.shape[2]

    def body(f):
        _, inv = mean_and_inv(parts, f, entries, group_size)
        means = frame_stats(grad_parts, f, entries, group_size)
        gn = ga_ref[f].astype(F32) * slope_ref[f].astype(F32)
        wide = inv * (gn - means[0:1] - normed_ref[f].astype(F32) * means[1:2])
        grad = wide.astype(BF16)
        g_ref[f] = grad
        first_ref[f, 0] = grad[:width]
        last_ref[f, 0] = grad[pixels - width :]
        here = pl.ds(pl.multiple_of(f * pixels, pixels), pixels)
        moved_ref[here, :channels] = from_right(wide, width).astype(BF16)
        moved_ref[here, channels : 2 * channels] = grad
        moved_ref[here, 2 * channels :] = from_left(wide, width).astype(BF16)

    loop(normed_ref.shape[0], body)


def weight_grad_kernel(xt_ref, moved_ref, temporal_ref, send_ref, keep_ref, acc_ref):
    channels = temporal_ref.shape[0]
    for j in range(3):
        lanes = slice(j * channels, (j + 1) * channels)
        acc_ref[: 3 * channels, lanes] = dot(xt_ref[...], moved_ref[:, lanes])
    acc_ref[3 * channels :, :] = temporal_ref[...]

    chips, depth, block, _ = keep_ref.shape
    half = chips * depth * block
    core = lax.axis_index("tm") & 1

    def hand_out(kept, sent):
        for p in range(chips):
            for z in range(depth):
                at = (p * depth + z) * block
                keep_ref[p, z] = acc_ref[kept + at : kept + at + block]
                send_ref[p, z] = acc_ref[sent + at : sent + at + block].astype(BF16)

    pl.when(core == 0)(functools.partial(hand_out, 0, half))
    pl.when(core == 1)(functools.partial(hand_out, half, 0))


def conv_back_kernel(g_ref, above_ref, below_ref, cot_ref, w_ref, out_ref, lhs_ref):
    frames, rows, width, channels = cot_ref.shape
    pixels = rows * width

    def body(pair):
        for b in range(2):
            f = 2 * pair + b
            put_windows(above_ref[f, 0], g_ref[f], below_ref[f, 0], lhs_ref, b * pixels, (2, 1, 0))
        lhs = lhs_ref[...]
        z = [dot(lhs, w_ref[j]) for j in range(3)]
        out = z[1] + from_right(z[0], width) + from_left(z[2], width)
        for b in range(2):
            one = out[b * pixels : (b + 1) * pixels].reshape(rows, width, channels)
            out_ref[2 * pair + b] = (one + cot_ref[2 * pair + b].astype(F32)).astype(BF16)

    loop(frames // 2, body)


def out_kernel(corners, clip_ref, dil_ref, own, nxt, prv, *refs):
    corner, (tw_ref, x_ref, out_ref, cat_ref) = refs[:corners], refs[corners:]
    frames, rows, width, channels = x_ref.shape
    pixels = rows * width

    def body(pair):
        for b in range(2):
            gather_taps(clip_ref, dil_ref, 2 * pair + b, own, nxt, prv, corner, cat_ref, b * pixels, 2)
        temporal_out = dot(cat_ref[...], tw_ref[...]).astype(BF16).astype(F32)
        for b in range(2):
            one = temporal_out[b * pixels : (b + 1) * pixels].reshape(rows, width, channels)
            out_ref[2 * pair + b] = (x_ref[2 * pair + b].astype(F32) + one).astype(BF16)

    loop(frames // 2, body)


def core_sum_kernel(keep_ref, got_ref, own_ref, *send_refs):
    chip = lax.axis_index("tm") >> 1
    own_ref[...] = keep_ref[chip] + got_ref[chip].astype(F32)
    for s, ref in enumerate(send_refs, 1):
        ref[...] = (keep_ref[chip ^ s] + got_ref[chip ^ s].astype(F32)).astype(BF16)


def sum_kernel(count, own_ref, *refs):
    total = own_ref[...]
    for ref in refs[:count]:
        total = total + ref[...].astype(F32)
    refs[count][...] = total.astype(BF16)


def sum_split_kernel(count, own_ref, *refs):
    got, (mine_ref, *send_refs) = refs[:count], refs[count:]
    deep = lax.axis_index("space")

    def block(k):
        total = own_ref[k]
        for ref in got:
            total = total + ref[k].astype(F32)
        return total

    mine_ref[...] = block(deep)
    for s, ref in enumerate(send_refs, 1):
        ref[...] = block(deep ^ s).astype(BF16)


def place_kernel(axis, shift, *refs):
    me = lax.axis_index(axis) >> shift
    for s, ref in enumerate(refs[:-1]):
        refs[-1][me ^ s] = ref[...]


def finish_kernel(mine_ref, got_ref, spatial_ref, temporal_ref):
    chips, depth, block, _ = mine_ref.shape
    channels = spatial_ref.shape[-1]

    def write(pair):
        for c in range(2):
            for p in range(chips):
                for z in range(depth):
                    row = ((c * chips + p) * depth + z) * block
                    values = pair[c][p, z].astype(F32)
                    i, at = row // channels, row % channels
                    for k in range(3):
                        lanes = values[:, k * channels : (k + 1) * channels]
                        if i < 3:
                            spatial_ref[i, k, at : at + block] = lanes
                        else:
                            temporal_ref[k, at : at + block] = lanes

    core = lax.axis_index("tm") & 1
    pl.when(core == 0)(functools.partial(write, (mine_ref, got_ref)))
    pl.when(core == 1)(functools.partial(write, (got_ref, mine_ref)))


def neighbours(axis, low, high):
    size = lax.axis_size(axis)
    up = [(i, i + 1) for i in range(size - 1)]
    down = [(j, i) for i, j in up]
    return lax.ppermute(high, axis, up), lax.ppermute(low, axis, down)


def near_frames(x, corner):
    pairs = [(i, i + 1) for i in range(lax.axis_size("tm") - 1) if corner or i != 3]
    return lax.ppermute(x, "tm", [(j, i) for i, j in pairs]), lax.ppermute(x, "tm", pairs)


def spread_sums(part, axis):
    size = lax.axis_size(axis)
    step, got = 1, None
    while step < size:
        if got is not None:
            part = part + got
        got = lax.ppermute(part, axis, [(i, i ^ step) for i in range(size)])
        step *= 2
    return [part, got]


def per_device(frames_in, cotangent, spatial, temporal, norm_gain, norm_shift, clip_frames, dilation):
    frames, rows, width, channels = frames_in.shape
    pixels = rows * width
    n, tm = lax.axis_size("space"), lax.axis_size("tm")
    chips = tm // 2
    group_size = channels // GROUPS
    entries = float(rows * n * width * group_size)
    gain, shift = norm_gain[None], norm_shift[None]
    big = frames * pixels * channels
    shape = jax.ShapeDtypeStruct
    per_px = (frames, pixels, channels)
    windows = pltpu.VMEM((2 * pixels, 3 * channels), BF16)

    first, last = frames_in[:, :1], frames_in[:, rows - 1 :]
    first, last, cot = lax.optimization_barrier((first, last, cotangent.reshape(per_px)))
    above, below = neighbours("space", first, last)
    by_corner = tm == 8
    cot_around = list(near_frames(cot, not by_corner))

    conv_out, sums = call(
        conv_kernel, "conv_forward", [frames_in, above, below, spatial],
        [shape(per_px, F32), shape((frames, 2, channels), F32)],
        18 * big * channels, 8 * big, [windows], 18,
    )
    if by_corner:
        sums, late = lax.optimization_barrier((sums, cot))
        relayed = lax.ppermute(late[frames // 2 :], "tm", [(3, 7), (4, 0)])
        cot_around.append(lax.ppermute(late[: frames // 2], "tm", [(3, 4), (4, 3)]))
    parts = spread_sums(sums, "space")
    x_turned = call(
        turn_kernel, "turned", [frames_in, above, below], shape((3 * channels, frames * pixels), BF16),
        0, 8 * big, [pltpu.VMEM((pixels, 3 * channels), BF16)],
    )
    back_weights, back_taps = call(
        turn_weights_kernel, "turn_weights", [spatial, temporal],
        [shape((3, 3 * channels, channels), BF16), shape((3 * channels, channels), BF16)], 0, big,
    )
    x_turned, back_weights, back_taps, *parts = lax.optimization_barrier((x_turned, back_weights, back_taps, *parts))
    if by_corner:
        relayed, *parts = lax.optimization_barrier((relayed, *parts))
        cot_around.append(lax.ppermute(relayed, "tm", [(7, 4), (0, 3)]))
    corners = len(cot_around) - 2
    act, normed, slope = call(
        functools.partial(act_kernel, len(parts), entries, group_size), "activation",
        [clip_frames, *parts, conv_out, gain, shift],
        [shape(per_px, BF16)] * 3, 10 * big, 10 * big,
    )
    act_sent, *cot_around[:2] = lax.optimization_barrier((act, *cot_around[:2]))
    act_around = near_frames(act_sent, True)

    grad_act, cot_cat, grad_sums = call(
        functools.partial(grad_act_kernel, corners), "grad_activation",
        [clip_frames, dilation, cot, *cot_around, back_taps, normed, slope],
        [shape(per_px, BF16), shape((frames * pixels, 3 * channels), BF16), shape((frames, 2, channels), F32)],
        6 * big * channels, 16 * big,
    )
    grad_parts = spread_sums(grad_sums, "space")
    temporal_part = call(
        temporal_grad_kernel, "temporal_grad", [act, cot_cat],
        shape((channels, 3 * channels), F32), 6 * big * channels, 8 * big,
    )
    lanes = 3 * channels
    grad_conv, first_rows, last_rows, moved = call(
        functools.partial(norm_back_kernel, len(parts), len(grad_parts), entries, group_size), "norm_backward",
        [normed, slope, grad_act, *parts, *grad_parts],
        [shape(per_px, BF16)] + [shape((frames, 1, width, channels), BF16)] * 2
        + [shape((frames * pixels, lanes), BF16)],
        0, 12 * big,
    )
    grad_above, grad_below = neighbours("space", first_rows, last_rows)
    block = 2 * channels // (chips * n)
    send, keep = call(
        weight_grad_kernel, "weight_grad", [x_turned, moved, temporal_part],
        [shape((chips, n, block, lanes), BF16), shape((chips, n, block, lanes), F32)],
        18 * big * channels, 12 * big, [pltpu.VMEM((4 * channels, lanes), F32)], 20,
    )

    def other_chip(s):
        return [(i, i ^ (2 * s)) for i in range(tm)]

    def other_plane(s):
        return [(i, i ^ s) for i in range(n)]

    other_core = [(i, i ^ 1) for i in range(tm)]
    got = lax.ppermute(send, "tm", other_core)
    own, *sends = call(
        core_sum_kernel, "core_sum", [keep, got],
        [shape((n, block, lanes), F32)] + [shape((n, block, lanes), BF16)] * (chips - 1), 0, 4 * big,
    )
    gots = [lax.ppermute(x, "tm", other_chip(s)) for s, x in enumerate(sends, 1)]

    in_grad = call(
        conv_back_kernel, "conv_backward", [grad_conv, grad_above, grad_below, cotangent, back_weights],
        shape(frames_in.shape, BF16), 18 * big * channels, 8 * big, [windows], 20,
    )
    own, in_grad = lax.optimization_barrier((own, in_grad))

    own, *sends = call(
        functools.partial(sum_split_kernel, chips - 1), "plane_sum", [own, *gots],
        [shape((block, lanes), F32)] + [shape((block, lanes), BF16)] * (n - 1), 0, big,
    )
    gots = [lax.ppermute(x, "space", other_plane(s)) for s, x in enumerate(sends, 1)]
    own = call(
        functools.partial(sum_kernel, n - 1), "line_sum", [own, *gots], shape((block, lanes), BF16), 0, big
    )
    gots = [lax.ppermute(own, "space", other_plane(s)) for s in range(1, n)]
    own = call(
        functools.partial(place_kernel, "space", 0), "line_place", [own, *gots], shape((n, block, lanes), BF16), 0, big
    )
    gots = [lax.ppermute(own, "tm", other_chip(s)) for s in range(1, chips)]

    out_frames = call(
        functools.partial(out_kernel, 0), "temporal_forward",
        [clip_frames, dilation, act, *act_around, temporal.reshape(3 * channels, channels), frames_in],
        shape(frames_in.shape, BF16), 6 * big * channels, 10 * big, [windows],
    )
    own, out_frames = lax.optimization_barrier((own, out_frames))

    own = call(
        functools.partial(place_kernel, "tm", 1), "plane_place", [own, *gots], shape((chips, n, block, lanes), BF16), 0, big
    )
    got = lax.ppermute(own, "tm", other_core)
    spatial_grad, temporal_grad = call(
        finish_kernel, "finish", [own, got], [shape(spatial.shape, F32), shape(temporal.shape, F32)], 0, 4 * big
    )
    return (out_frames, in_grad, spatial_grad, temporal_grad)


def solution(mesh):
    tiles = P("tm", "space", None, None)
    return jax.shard_map(
        per_device,
        mesh=mesh,
        in_specs=(tiles, tiles, P(), P(), P(), P(), P(), P()),
        out_specs=(tiles, tiles, P(), P()),
        check_vma=False,
    )
```

profile of v0, /device:TPU:0, one launch (start us, length us, event | category | flops | bytes accessed | tf_op | source)
XLA Modules:
  0.0 138.8 jit_solution(3855769943424045358)
XLA Ops:
  0.6 1.1 fusion.1
  1.7 4.9 %collective-permute-start = (bf16[8,1,64,256]{3,2,1,0:T(8,128)(2,1)S(1)}, bf16[8,1,64,256]{3,2,1,0:T(8,128)(2,1)S(1)}, u32[]{:S(2)}, u32[]{:S(2)}) collective-permute-start(bf16[8,1,64,256]{3,2,1,0:T(8,128)(2,1)S(1)} %get-tuple-element.50), channel_id=1, source_target_pairs={{0,1},{1,2},{2,3},{4,5},{5,6},{6,7},{8,9},{9,10},{10,11},{12,13},{... | collective-permute-start | bytes 786440 | tf_op jit(solution)/shard_map/ppermute | solution.py:379
  6.7 1.3 collective-permute-start.1
  8.0 1.6 %collective-permute-start.6 = (bf16[8,512,256]{2,1,0:T(8,128)(2,1)}, bf16[8,512,256]{2,1,0:T(8,128)(2,1)S(1)}, u32[]{:S(2)}, u32[]{:S(2)}) collective-permute-start(bf16[8,512,256]{2,1,0:T(8,128)(2,1)} %bitcast.4), channel_id=1, source_target_pairs={{0,4},{4,8},{8,12},{16,20},{20,24},{24,28},{1,5},{5,9},{9,13},{17,... | collective-permute-start | bytes 6291464 | tf_op jit(solution)/shard_map/ppermute | solution.py:384
  9.6 1.3 collective-permute-start.5
  10.9 1.3 collective-permute-done.above_ref
  12.2 4.1 %collective-permute-done.1.below_ref = bf16[8,1,64,256]{3,2,1,0:T(8,128)(2,1)S(1)} collective-permute-done((bf16[8,1,64,256]{3,2,1,0:T(8,128)(2,1)S(1)}, bf16[8,1,64,256]{3,2,1,0:T(8,128)(2,1)S(1)}, u32[]{:S(2)}, u32[]{:S(2)}) %collective-permute-start.1) | collective-permute-done | bytes 262176 | tf_op jit(solution)/shard_map/ppermute | solution.py:379
  16.3 1.6 %copy-done = bf16[8,8,64,256]{3,2,1,0:T(8,128)(2,1)S(1)} copy-done((bf16[8,8,64,256]{3,2,1,0:T(8,128)(2,1)S(1)}, bf16[8,8,64,256]{3,2,1,0:T(8,128)(2,1)}, u32[]{:S(2)}) %copy-start) | copy-done | bytes 2097176
  17.9 1.3 copy-done.4
  19.2 5.6 %conv_forward.1 = (f32[8,512,256]{2,1,0:T(8,128)S(1)}, f32[8,2,256]{2,1,0:T(2,128)S(1)}) custom-call(bf16[8,8,64,256]{3,2,1,0:T(8,128)(2,1)S(1)} %copy-done, bf16[8,1,64,256]{3,2,1,0:T(8,128)(2,1)S(1)} %collective-permute-done.above_ref, bf16[8,1,64,256]{3,2,1,0:T(8,128)(2,1)S(1)} %collective-permute-done.1.below_ref, bf16[3,3,256,256]{3,2,1,0:T(8,128)(2,1)S(1)} %copy-done.4), custom_call_target="tpu_custom_call" | custom-call | flops 4831838208 | bytes 8388608 | tf_op jit(solution)/shard_map/conv_forward/pallas_call | solution.py:20
  24.8 0.0 copy-start.3
  24.8 0.0 copy-start.1
  24.8 0.1 fusion
  25.0 1.4 %collective-permute-start.4 = (bf16[4,512,256]{2,1,0:T(8,128)(2,1)S(1)}, bf16[4,512,256]{2,1,0:T(8,128)(2,1)S(1)}, u32[]{:S(2)}, u32[]{:S(2)}) collective-permute-start(bf16[4,512,256]{2,1,0:T(8,128)(2,1)S(1)} %get-tuple-element.97), channel_id=1, source_target_pairs={{12,28},{16,0},{13,29},{17,1},{14,30},{18,2},{15,31},{19,3}} | collective-permute-start | bytes 3145736 | tf_op jit(solution)/shard_map/ppermute | solution.py:424
  26.4 1.6 %collective-permute-start.2 = (f32[8,2,256]{2,1,0:T(2,128)S(1)}, f32[8,2,256]{2,1,0:T(2,128)S(1)}, u32[]{:S(2)}, u32[]{:S(2)}) collective-permute-start(f32[8,2,256]{2,1,0:T(2,128)S(1)} %get-tuple-element.56), channel_id=1, source_target_pairs={{0,1},{1,0},{2,3},{3,2},{4,5},{5,4},{6,7},{7,6},{8,9},{9,8},{10,11... | collective-permute-start | bytes 49160 | tf_op jit(solution)/shard_map/ppermute | solution.py:393
  28.1 2.2 %collective-permute-done.2 = f32[8,2,256]{2,1,0:T(2,128)S(1)} collective-permute-done((f32[8,2,256]{2,1,0:T(2,128)S(1)}, f32[8,2,256]{2,1,0:T(2,128)S(1)}, u32[]{:S(2)}, u32[]{:S(2)}) %collective-permute-start.2) | collective-permute-done | bytes 16416 | tf_op jit(solution)/shard_map/ppermute | solution.py:393
  30.2 2.6 %collective-permute-start.3 = (f32[8,2,256]{2,1,0:T(2,128)S(1)}, f32[8,2,256]{2,1,0:T(2,128)S(1)}, u32[]{:S(2)}, u32[]{:S(2)}) collective-permute-start(f32[8,2,256]{2,1,0:T(2,128)S(1)} %add.6.refs_0_), channel_id=1, source_target_pairs={{0,2},{1,3},{2,0},{3,1},{4,6},{5,7},{6,4},{7,5},{8,10},{9,11},{10,... | collective-permute-start | bytes 49160 | tf_op jit(solution)/shard_map/ppermute | solution.py:393
  32.9 0.5 turn_weights.1
  33.3 0.0 copy-start.5
  33.4 0.0 copy-start.7
  33.4 0.0 copy-start.8
  33.4 0.9 collective-permute-start.7
  34.3 2.2 %turned.1.xt_ref = bf16[768,4096]{1,0:T(8,128)(2,1)S(1)} custom-call(bf16[8,8,64,256]{3,2,1,0:T(8,128)(2,1)S(1)} %copy-done.1, bf16[8,1,64,256]{3,2,1,0:T(8,128)(2,1)S(1)} %collective-permute-done.above_ref, bf16[8,1,64,256]{3,2,1,0:T(8,128)(2,1)S(1)} %collective-permute-done.1.below_ref), custom_call_target="tpu_custom_call" | custom-call | bytes 8388608 | tf_op jit(solution)/shard_map/turned/pallas_call | solution.py:20
  36.4 5.4 %collective-permute-done.4 = bf16[4,512,256]{2,1,0:T(8,128)(2,1)S(1)} collective-permute-done((bf16[4,512,256]{2,1,0:T(8,128)(2,1)S(1)}, bf16[4,512,256]{2,1,0:T(8,128)(2,1)S(1)}, u32[]{:S(2)}, u32[]{:S(2)}) %collective-permute-start.4) | collective-permute-done | bytes 1048608 | tf_op jit(solution)/shard_map/ppermute | solution.py:424
  41.8 1.7 %collective-permute-start.8 = (bf16[4,512,256]{2,1,0:T(8,128)(2,1)S(1)}, bf16[4,512,256]{2,1,0:T(8,128)(2,1)S(1)}, u32[]{:S(2)}, u32[]{:S(2)}) collective-permute-start(bf16[4,512,256]{2,1,0:T(8,128)(2,1)S(1)} %collective-permute-done.4), channel_id=1, source_target_pairs={{28,16},{0,12},{29,17},{1,13},{30,18},{2,14},{31,19},{3,15}} | collective-permute-start | bytes 3145736 | tf_op jit(solution)/shard_map/ppermute | solution.py:438
  43.5 6.1 %activation.1 = (bf16[8,512,256]{2,1,0:T(8,128)(2,1)S(1)}, bf16[8,512,256]{2,1,0:T(8,128)(2,1)S(1)}, bf16[8,512,256]{2,1,0:T(8,128)(2,1)S(1)}) custom-call(s32[2]{0:T(128)S(1)} %copy-done.5, f32[8,2,256]{2,1,0:T(2,128)S(1)} %add.6.refs_0_, f32[8,2,256]{2,1,0:T(2,128)S(1)} %collective-permute-done.3.refs_1_, f32[8,512,256]{2,1,0:T(8,128)S(1)} %get-tuple-element.63.refs_2_, ...), custom_call_target="tpu_custom_call" | custom-call | flops 10485760 | bytes 10485760 | tf_op jit(solution)/shard_map/activation/pallas_call | solution.py:20
  49.7 1.4 %collective-permute-start.24 = (bf16[8,512,256]{2,1,0:T(8,128)(2,1)S(1)}, bf16[8,512,256]{2,1,0:T(8,128)(2,1)S(1)}, u32[]{:S(2)}, u32[]{:S(2)}) collective-permute-start(bf16[8,512,256]{2,1,0:T(8,128)(2,1)S(1)} %get-tuple-element.90.act_ref.own), channel_id=1, source_target_pairs={{0,4},{4,8},{8,12},{12,16},{16,20},{20,24},{24,28},{1,5},{5,9},{9,... | collective-permute-start | bytes 6291464 | tf_op jit(solution)/shard_map/ppermute | solution.py:384
  51.1 1.3 collective-permute-start.23
  52.4 12.2 %collective-permute-done.8.refs_1_ = bf16[4,512,256]{2,1,0:T(8,128)(2,1)S(1)} collective-permute-done((bf16[4,512,256]{2,1,0:T(8,128)(2,1)S(1)}, bf16[4,512,256]{2,1,0:T(8,128)(2,1)S(1)}, u32[]{:S(2)}, u32[]{:S(2)}) %collective-permute-start.8) | collective-permute-done | bytes 1048608 | tf_op jit(solution)/shard_map/ppermute | solution.py:438
  64.7 4.2 %grad_activation.1 = (bf16[8,512,256]{2,1,0:T(8,128)(2,1)S(1)}, bf16[4096,768]{1,0:T(8,128)(2,1)S(1)}, f32[8,2,256]{2,1,0:T(2,128)S(1)}) custom-call(s32[2]{0:T(128)S(1)} %copy-done.5, s32[2]{0:T(128)S(1)} %copy-done.6, bf16[8,512,256]{2,1,0:T(8,128)(2,1)S(1)} %bitcast.7, bf16[8,512,256]{2,1,0:T(8,128)(2,1)S(1)} %collective-permute-done.5.nxt, ...), custom_call_target="tpu_custom_call" | custom-call | flops 1610612736 | bytes 16777216 | tf_op jit(solution)/shard_map/grad_activation/pallas_call | solution.py:20
  68.8 2.5 %collective-permute-start.9 = (f32[8,2,256]{2,1,0:T(2,128)S(1)}, f32[8,2,256]{2,1,0:T(2,128)S(1)}, u32[]{:S(2)}, u32[]{:S(2)}) collective-permute-start(f32[8,2,256]{2,1,0:T(2,128)S(1)} %get-tuple-element.72), channel_id=1, source_target_pairs={{0,1},{1,0},{2,3},{3,2},{4,5},{5,4},{6,7},{7,6},{8,9},{9,8},{10,11... | collective-permute-start | bytes 49160 | tf_op jit(solution)/shard_map/ppermute | solution.py:393
  71.4 1.7 %collective-permute-done.9 = f32[8,2,256]{2,1,0:T(2,128)S(1)} collective-permute-done((f32[8,2,256]{2,1,0:T(2,128)S(1)}, f32[8,2,256]{2,1,0:T(2,128)S(1)}, u32[]{:S(2)}, u32[]{:S(2)}) %collective-permute-start.9) | collective-permute-done | bytes 16416 | tf_op jit(solution)/shard_map/ppermute | solution.py:393
  73.1 3.1 %collective-permute-start.10 = (f32[8,2,256]{2,1,0:T(2,128)S(1)}, f32[8,2,256]{2,1,0:T(2,128)S(1)}, u32[]{:S(2)}, u32[]{:S(2)}) collective-permute-start(f32[8,2,256]{2,1,0:T(2,128)S(1)} %add.7.refs_2_), channel_id=1, source_target_pairs={{0,2},{1,3},{2,0},{3,1},{4,6},{5,7},{6,4},{7,5},{8,10},{9,11},{10,... | collective-permute-start | bytes 49160 | tf_op jit(solution)/shard_map/ppermute | solution.py:393
  76.2 1.9 %temporal_grad.1.temporal_ref = f32[256,768]{1,0:T(8,128)S(1)} custom-call(bf16[8,512,256]{2,1,0:T(8,128)(2,1)S(1)} %get-tuple-element.90.act_ref.own, bf16[4096,768]{1,0:T(8,128)(2,1)S(1)} %get-tuple-element.74.cat_ref), custom_call_target="tpu_custom_call" | custom-call | flops 1610612736 | bytes 8388608 | tf_op jit(solution)/shard_map/temporal_grad/pallas_call | solution.py:20
  78.1 4.6 %norm_backward.1 = (bf16[8,512,256]{2,1,0:T(8,128)(2,1)S(1)}, bf16[8,1,64,256]{3,2,1,0:T(8,128)(2,1)S(1)}, bf16[8,1,64,256]{3,2,1,0:T(8,128)(2,1)S(1)}, bf16[4096,768]{1,0:T(8,128)(2,1)S(1)}) custom-call(bf16[8,512,256]{2,1,0:T(8,128)(2,1)S(1)} %get-tuple-element.64.refs_3_.normed_ref, bf16[8,512,256]{2,1,0:T(8,128)(2,1)S(1)} %get-tuple-element.65.refs_4_.slope_ref, ...), custom_call_target="tpu_custom_call" | custom-call | bytes 12582912 | tf_op jit(solution)/shard_map/norm_backward/pallas_call | solution.py:20
  82.7 5.2 %weight_grad.1 = (bf16[4,4,32,768]{3,2,1,0:T(8,128)(2,1)S(1)}, f32[4,4,32,768]{3,2,1,0:T(8,128)S(1)}) custom-call(bf16[768,4096]{1,0:T(8,128)(2,1)S(1)} %turned.1.xt_ref, bf16[4096,768]{1,0:T(8,128)(2,1)S(1)} %get-tuple-element.73.moved_ref, f32[256,768]{1,0:T(8,128)S(1)} %temporal_grad.1.temporal_ref), custom_call_target="tpu_custom_call" | custom-call | flops 4831838208 | bytes 12582912 | tf_op jit(solution)/shard_map/weight_grad/pallas_call | solution.py:20
  87.9 0.1 collective-permute-start.11
  88.0 3.6 %collective-permute-start.12 = (bf16[8,1,64,256]{3,2,1,0:T(8,128)(2,1)S(1)}, bf16[8,1,64,256]{3,2,1,0:T(8,128)(2,1)S(1)}, u32[]{:S(2)}, u32[]{:S(2)}) collective-permute-start(bf16[8,1,64,256]{3,2,1,0:T(8,128)(2,1)S(1)} %get-tuple-element.79), channel_id=1, source_target_pairs={{0,1},{1,2},{2,3},{4,5},{5,6},{6,7},{8,9},{9,10},{10,11},{12,13},{... | collective-permute-start | bytes 786440 | tf_op jit(solution)/shard_map/ppermute | solution.py:379
  91.6 1.5 %collective-permute-start.13 = (bf16[8,1,64,256]{3,2,1,0:T(8,128)(2,1)S(1)}, bf16[8,1,64,256]{3,2,1,0:T(8,128)(2,1)S(1)}, u32[]{:S(2)}, u32[]{:S(2)}) collective-permute-start(bf16[8,1,64,256]{3,2,1,0:T(8,128)(2,1)S(1)} %get-tuple-element.80), channel_id=1, source_target_pairs={{1,0},{2,1},{3,2},{5,4},{6,5},{7,6},{9,8},{10,9},{11,10},{13,12},{... | collective-permute-start | bytes 786440 | tf_op jit(solution)/shard_map/ppermute | solution.py:379
  93.1 0.1 core_sum.1
  93.3 0.6 collective-permute-start.14
  93.9 3.9 %collective-permute-done.12.above_ref = bf16[8,1,64,256]{3,2,1,0:T(8,128)(2,1)S(1)} collective-permute-done((bf16[8,1,64,256]{3,2,1,0:T(8,128)(2,1)S(1)}, bf16[8,1,64,256]{3,2,1,0:T(8,128)(2,1)S(1)}, u32[]{:S(2)}, u32[]{:S(2)}) %collective-permute-start.12) | collective-permute-done | bytes 262176 | tf_op jit(solution)/shard_map/ppermute | solution.py:379
  97.8 4.1 %collective-permute-done.13.below_ref = bf16[8,1,64,256]{3,2,1,0:T(8,128)(2,1)S(1)} collective-permute-done((bf16[8,1,64,256]{3,2,1,0:T(8,128)(2,1)S(1)}, bf16[8,1,64,256]{3,2,1,0:T(8,128)(2,1)S(1)}, u32[]{:S(2)}, u32[]{:S(2)}) %collective-permute-start.13) | collective-permute-done | bytes 262176 | tf_op jit(solution)/shard_map/ppermute | solution.py:379
  101.9 6.9 %conv_backward.1 = bf16[8,8,64,256]{3,2,1,0:T(8,128)(2,1)} custom-call(bf16[8,512,256]{2,1,0:T(8,128)(2,1)S(1)} %get-tuple-element.78.g_ref, bf16[8,1,64,256]{3,2,1,0:T(8,128)(2,1)S(1)} %collective-permute-done.12.above_ref, bf16[8,1,64,256]{3,2,1,0:T(8,128)(2,1)S(1)} %collective-permute-done.13.below_ref, bf16[8,8,64,256]{3,2,1,0:T(8,128)(2,1)S(1)} %copy-done.2, ...), custom_call_target="tpu_custom_call" | custom-call | flops 4831838208 | bytes 8388608 | tf_op jit(solution)/shard_map/conv_backward/pallas_call | solution.py:20
  108.9 0.1 collective-permute-done.16.refs_2_
  109.0 0.1 plane_sum.1
  109.1 2.1 %collective-permute-start.17 = (bf16[32,768]{1,0:T(8,128)(2,1)S(1)}, bf16[32,768]{1,0:T(8,128)(2,1)S(1)}, u32[]{:S(2)}, u32[]{:S(2)}) collective-permute-start(bf16[32,768]{1,0:T(8,128)(2,1)S(1)} %get-tuple-element.87), channel_id=1, source_target_pairs={{0,1},{1,0},{2,3},{3,2},{4,5},{5,4},{6,7},{7,6},{8,9},{9,8},{10,11... | collective-permute-start | bytes 147464 | tf_op jit(solution)/shard_map/ppermute | solution.py:499
  111.2 1.5 %collective-permute-start.18 = (bf16[32,768]{1,0:T(8,128)(2,1)S(1)}, bf16[32,768]{1,0:T(8,128)(2,1)S(1)}, u32[]{:S(2)}, u32[]{:S(2)}) collective-permute-start(bf16[32,768]{1,0:T(8,128)(2,1)S(1)} %get-tuple-element.88), channel_id=1, source_target_pairs={{0,2},{1,3},{2,0},{3,1},{4,6},{5,7},{6,4},{7,5},{8,10},{9,11},{10,... | collective-permute-start | bytes 147464 | tf_op jit(solution)/shard_map/ppermute | solution.py:499
  112.7 1.0 collective-permute-start.19
  113.6 3.5 %collective-permute-done.18.refs_1_ = bf16[32,768]{1,0:T(8,128)(2,1)S(1)} collective-permute-done((bf16[32,768]{1,0:T(8,128)(2,1)S(1)}, bf16[32,768]{1,0:T(8,128)(2,1)S(1)}, u32[]{:S(2)}, u32[]{:S(2)}) %collective-permute-start.18) | collective-permute-done | bytes 49184 | tf_op jit(solution)/shard_map/ppermute | solution.py:499
  117.1 1.5 %collective-permute-done.19.refs_2_ = bf16[32,768]{1,0:T(8,128)(2,1)S(1)} collective-permute-done((bf16[32,768]{1,0:T(8,128)(2,1)S(1)}, bf16[32,768]{1,0:T(8,128)(2,1)S(1)}, u32[]{:S(2)}, u32[]{:S(2)}) %collective-permute-start.19) | collective-permute-done | bytes 49184 | tf_op jit(solution)/shard_map/ppermute | solution.py:499
  118.7 1.0 collective-permute-start.22
  119.7 0.4 collective-permute-start.21
  120.1 3.1 %collective-permute-start.20 = (bf16[32,768]{1,0:T(8,128)(2,1)S(1)}, bf16[32,768]{1,0:T(8,128)(2,1)S(1)}, u32[]{:S(2)}, u32[]{:S(2)}) collective-permute-start(bf16[32,768]{1,0:T(8,128)(2,1)S(1)} %line_sum.1.refs_0_), channel_id=1, source_target_pairs={{0,1},{1,0},{2,3},{3,2},{4,5},{5,4},{6,7},{7,6},{8,9},{9,8},{10,11... | collective-permute-start | bytes 147464 | tf_op jit(solution)/shard_map/ppermute | solution.py:503
  123.2 1.5 %collective-permute-done.22.refs_3_ = bf16[32,768]{1,0:T(8,128)(2,1)S(1)} collective-permute-done((bf16[32,768]{1,0:T(8,128)(2,1)S(1)}, bf16[32,768]{1,0:T(8,128)(2,1)S(1)}, u32[]{:S(2)}, u32[]{:S(2)}) %collective-permute-start.22) | collective-permute-done | bytes 49184 | tf_op jit(solution)/shard_map/ppermute | solution.py:503
  124.7 1.0 collective-permute-done.21.refs_2_
  125.7 1.8 %collective-permute-start.27 = (bf16[4,32,768]{2,1,0:T(8,128)(2,1)S(1)}, bf16[4,32,768]{2,1,0:T(8,128)(2,1)S(1)}, u32[]{:S(2)}, u32[]{:S(2)}) collective-permute-start(bf16[4,32,768]{2,1,0:T(8,128)(2,1)S(1)} %line_place.1.refs_0_), channel_id=1, source_target_pairs={{0,24},{4,28},{8,16},{12,20},{16,8},{20,12},{24,0},{28,4},{1,25},{... | collective-permute-start | bytes 589832 | tf_op jit(solution)/shard_map/ppermute | solution.py:507
  127.5 1.7 %collective-permute-start.25 = (bf16[4,32,768]{2,1,0:T(8,128)(2,1)S(1)}, bf16[4,32,768]{2,1,0:T(8,128)(2,1)S(1)}, u32[]{:S(2)}, u32[]{:S(2)}) collective-permute-start(bf16[4,32,768]{2,1,0:T(8,128)(2,1)S(1)} %line_place.1.refs_0_), channel_id=1, source_target_pairs={{0,8},{4,12},{8,0},{12,4},{16,24},{20,28},{24,16},{28,20},{1,9},{5... | collective-permute-start | bytes 589832 | tf_op jit(solution)/shard_map/ppermute | solution.py:507
  129.3 5.0 %temporal_forward.1 = bf16[8,8,64,256]{3,2,1,0:T(8,128)(2,1)} custom-call(s32[2]{0:T(128)S(1)} %copy-done.5, s32[2]{0:T(128)S(1)} %copy-done.6, bf16[8,512,256]{2,1,0:T(8,128)(2,1)S(1)} %get-tuple-element.90.act_ref.own, bf16[8,512,256]{2,1,0:T(8,128)(2,1)S(1)} %collective-permute-done.23.nxt, bf16[8,512,256]{2,1,0:T(8,128)(2,1)S(1)} %collective-permute-done.24.prv, ...), custom_call_target="tpu_custom_call" | custom-call | flops 1610612736 | bytes 10485760 | tf_op jit(solution)/shard_map/temporal_forward/pallas_call | solution.py:20
  134.3 0.2 collective-permute-done.26.refs_2_
  134.5 0.1 plane_place.1.mine_ref
  134.6 0.1 collective-permute-start.28
  134.6 2.3 %collective-permute-done.28.got_ref = bf16[4,4,32,768]{3,2,1,0:T(8,128)(2,1)S(1)} collective-permute-done((bf16[4,4,32,768]{3,2,1,0:T(8,128)(2,1)S(1)}, bf16[4,4,32,768]{3,2,1,0:T(8,128)(2,1)S(1)}, u32[]{:S(2)}, u32[]{:S(2)}) %collective-permute-start.28) | collective-permute-done | bytes 786464 | tf_op jit(solution)/shard_map/ppermute | solution.py:519
  136.9 1.9 %finish.1 = (f32[3,3,256,256]{3,2,1,0:T(8,128)}, f32[3,256,256]{2,1,0:T(8,128)}) custom-call(bf16[4,4,32,768]{3,2,1,0:T(8,128)(2,1)S(1)} %plane_place.1.mine_ref, bf16[4,4,32,768]{3,2,1,0:T(8,128)(2,1)S(1)} %collective-permute-done.28.got_ref), custom_call_target="tpu_custom_call" | custom-call | bytes 4194304 | tf_op jit(solution)/shard_map/finish/pallas_call | solution.py:20
  (32 shorter events, 0.1 us)
Async XLA Ops:
  1.7 10.5 %collective-permute-start = (bf16[8,1,64,256]{3,2,1,0:T(8,128)(2,1)S(1)}, bf16[8,1,64,256]{3,2,1,0:T(8,128)(2,1)S(1)}, u32[]{:S(2)}, u32[]{:S(2)}) collective-permute-start(bf16[8,1,64,256]{3,2,1,0:T(8,128)(2,1)S(1)} %get-tuple-element.50), channel_id=1, source_target_pairs={{0,1},{1,2},{2,3},{4,5},{5,6},{6,7},{8,9},{9,10},{10,11},{12,13},{... | collective-permute-start | bytes 786440 | tf_op jit(solution)/shard_map/ppermute | solution.py:379
  6.7 9.7 %collective-permute-start.1 = (bf16[8,1,64,256]{3,2,1,0:T(8,128)(2,1)S(1)}, bf16[8,1,64,256]{3,2,1,0:T(8,128)(2,1)S(1)}, u32[]{:S(2)}, u32[]{:S(2)}) collective-permute-start(bf16[8,1,64,256]{3,2,1,0:T(8,128)(2,1)S(1)} %get-tuple-element.51), channel_id=1, source_target_pairs={{1,0},{2,1},{3,2},{5,4},{6,5},{7,6},{9,8},{10,9},{11,10},{13,12},{... | collective-permute-start | bytes 786440 | tf_op jit(solution)/shard_map/ppermute | solution.py:379
  8.0 41.7 %collective-permute-start.6 = (bf16[8,512,256]{2,1,0:T(8,128)(2,1)}, bf16[8,512,256]{2,1,0:T(8,128)(2,1)S(1)}, u32[]{:S(2)}, u32[]{:S(2)}) collective-permute-start(bf16[8,512,256]{2,1,0:T(8,128)(2,1)} %bitcast.4), channel_id=1, source_target_pairs={{0,4},{4,8},{8,12},{16,20},{20,24},{24,28},{1,5},{5,9},{9,13},{17,... | collective-permute-start | bytes 6291464 | tf_op jit(solution)/shard_map/ppermute | solution.py:384
  9.6 40.1 %collective-permute-start.5 = (bf16[8,512,256]{2,1,0:T(8,128)(2,1)}, bf16[8,512,256]{2,1,0:T(8,128)(2,1)S(1)}, u32[]{:S(2)}, u32[]{:S(2)}) collective-permute-start(bf16[8,512,256]{2,1,0:T(8,128)(2,1)} %bitcast.5), channel_id=1, source_target_pairs={{4,0},{8,4},{12,8},{20,16},{24,20},{28,24},{5,1},{9,5},{13,9},{21,... | collective-permute-start | bytes 6291464 | tf_op jit(solution)/shard_map/ppermute | solution.py:384
  16.3 1.6 %copy-start = (bf16[8,8,64,256]{3,2,1,0:T(8,128)(2,1)S(1)}, bf16[8,8,64,256]{3,2,1,0:T(8,128)(2,1)}, u32[]{:S(2)}) copy-start(bf16[8,8,64,256]{3,2,1,0:T(8,128)(2,1)} %refs_1_.1) | copy-start | bytes 6291460
  17.9 1.3 copy-start.4
  19.2 5.6 %copy-start.2 = (bf16[8,8,64,256]{3,2,1,0:T(8,128)(2,1)S(1)}, bf16[8,8,64,256]{3,2,1,0:T(8,128)(2,1)}, u32[]{:S(2)}) copy-start(bf16[8,8,64,256]{3,2,1,0:T(8,128)(2,1)} %cot_ref.1) | copy-start | bytes 6291460
  24.8 8.1 %copy-start.3 = (bf16[3,256,256]{2,1,0:T(8,128)(2,1)S(1)}, bf16[3,256,256]{2,1,0:T(8,128)(2,1)}, u32[]{:S(2)}) copy-start(bf16[3,256,256]{2,1,0:T(8,128)(2,1)} %temporal_ref.1) | copy-start | bytes 1179652
  24.8 9.4 %copy-start.1 = (bf16[8,8,64,256]{3,2,1,0:T(8,128)(2,1)S(1)}, bf16[8,8,64,256]{3,2,1,0:T(8,128)(2,1)}, u32[]{:S(2)}) copy-start(bf16[8,8,64,256]{3,2,1,0:T(8,128)(2,1)} %refs_1_.1) | copy-start | bytes 6291460
  25.0 16.8 %collective-permute-start.4 = (bf16[4,512,256]{2,1,0:T(8,128)(2,1)S(1)}, bf16[4,512,256]{2,1,0:T(8,128)(2,1)S(1)}, u32[]{:S(2)}, u32[]{:S(2)}) collective-permute-start(bf16[4,512,256]{2,1,0:T(8,128)(2,1)S(1)} %get-tuple-element.97), channel_id=1, source_target_pairs={{12,28},{16,0},{13,29},{17,1},{14,30},{18,2},{15,31},{19,3}} | collective-permute-start | bytes 3145736 | tf_op jit(solution)/shard_map/ppermute | solution.py:424
  26.4 3.8 %collective-permute-start.2 = (f32[8,2,256]{2,1,0:T(2,128)S(1)}, f32[8,2,256]{2,1,0:T(2,128)S(1)}, u32[]{:S(2)}, u32[]{:S(2)}) collective-permute-start(f32[8,2,256]{2,1,0:T(2,128)S(1)} %get-tuple-element.56), channel_id=1, source_target_pairs={{0,1},{1,0},{2,3},{3,2},{4,5},{5,4},{6,7},{7,6},{8,9},{9,8},{10,11... | collective-permute-start | bytes 49160 | tf_op jit(solution)/shard_map/ppermute | solution.py:393
  30.2 6.2 %collective-permute-start.3 = (f32[8,2,256]{2,1,0:T(2,128)S(1)}, f32[8,2,256]{2,1,0:T(2,128)S(1)}, u32[]{:S(2)}, u32[]{:S(2)}) collective-permute-start(f32[8,2,256]{2,1,0:T(2,128)S(1)} %add.6.refs_0_), channel_id=1, source_target_pairs={{0,2},{1,3},{2,0},{3,1},{4,6},{5,7},{6,4},{7,5},{8,10},{9,11},{10,... | collective-permute-start | bytes 49160 | tf_op jit(solution)/shard_map/ppermute | solution.py:393
  33.3 10.2 %copy-start.5 = (s32[2]{0:T(128)S(1)}, s32[2]{0:T(128)}, u32[]{:S(2)}) copy-start(s32[2]{0:T(128)} %clip_ref.5) | copy-start | bytes 28
  33.4 10.2 %copy-start.7 = (f32[256]{0:T(256)S(1)}, f32[256]{0:T(256)}, u32[]{:S(2)}) copy-start(f32[256]{0:T(256)} %param.12) | copy-start | bytes 3076
  33.4 10.2 %copy-start.8 = (f32[256]{0:T(256)S(1)}, f32[256]{0:T(256)}, u32[]{:S(2)}) copy-start(f32[256]{0:T(256)} %param.13) | copy-start | bytes 3076
  33.4 19.0 %collective-permute-start.7 = (bf16[4,512,256]{2,1,0:T(8,128)(2,1)S(1)}, bf16[4,512,256]{2,1,0:T(8,128)(2,1)S(1)}, u32[]{:S(2)}, u32[]{:S(2)}) collective-permute-start(bf16[4,512,256]{2,1,0:T(8,128)(2,1)S(1)} %get-tuple-element.96), channel_id=1, source_target_pairs={{12,16},{16,12},{13,17},{17,13},{14,18},{18,14},{15,19},{19,15}} | collective-permute-start | bytes 3145736 | tf_op jit(solution)/shard_map/ppermute | solution.py:425
  41.8 22.9 %collective-permute-start.8 = (bf16[4,512,256]{2,1,0:T(8,128)(2,1)S(1)}, bf16[4,512,256]{2,1,0:T(8,128)(2,1)S(1)}, u32[]{:S(2)}, u32[]{:S(2)}) collective-permute-start(bf16[4,512,256]{2,1,0:T(8,128)(2,1)S(1)} %collective-permute-done.4), channel_id=1, source_target_pairs={{28,16},{0,12},{29,17},{1,13},{30,18},{2,14},{31,19},{3,15}} | collective-permute-start | bytes 3145736 | tf_op jit(solution)/shard_map/ppermute | solution.py:438
  43.5 21.1 %copy-start.6 = (s32[2]{0:T(128)S(1)}, s32[2]{0:T(128)}, u32[]{:S(2)}) copy-start(s32[2]{0:T(128)} %dil_ref.3) | copy-start | bytes 28
  49.7 79.6 %collective-permute-start.24 = (bf16[8,512,256]{2,1,0:T(8,128)(2,1)S(1)}, bf16[8,512,256]{2,1,0:T(8,128)(2,1)S(1)}, u32[]{:S(2)}, u32[]{:S(2)}) collective-permute-start(bf16[8,512,256]{2,1,0:T(8,128)(2,1)S(1)} %get-tuple-element.90.act_ref.own), channel_id=1, source_target_pairs={{0,4},{4,8},{8,12},{12,16},{16,20},{20,24},{24,28},{1,5},{5,9},{9,... | collective-permute-start | bytes 6291464 | tf_op jit(solution)/shard_map/ppermute | solution.py:384
  51.1 78.2 %collective-permute-start.23 = (bf16[8,512,256]{2,1,0:T(8,128)(2,1)S(1)}, bf16[8,512,256]{2,1,0:T(8,128)(2,1)S(1)}, u32[]{:S(2)}, u32[]{:S(2)}) collective-permute-start(bf16[8,512,256]{2,1,0:T(8,128)(2,1)S(1)} %get-tuple-element.90.act_ref.own), channel_id=1, source_target_pairs={{4,0},{8,4},{12,8},{16,12},{20,16},{24,20},{28,24},{5,1},{9,5},{13... | collective-permute-start | bytes 6291464 | tf_op jit(solution)/shard_map/ppermute | solution.py:384
  68.8 4.3 %collective-permute-start.9 = (f32[8,2,256]{2,1,0:T(2,128)S(1)}, f32[8,2,256]{2,1,0:T(2,128)S(1)}, u32[]{:S(2)}, u32[]{:S(2)}) collective-permute-start(f32[8,2,256]{2,1,0:T(2,128)S(1)} %get-tuple-element.72), channel_id=1, source_target_pairs={{0,1},{1,0},{2,3},{3,2},{4,5},{5,4},{6,7},{7,6},{8,9},{9,8},{10,11... | collective-permute-start | bytes 49160 | tf_op jit(solution)/shard_map/ppermute | solution.py:393
  73.1 5.0 %collective-permute-start.10 = (f32[8,2,256]{2,1,0:T(2,128)S(1)}, f32[8,2,256]{2,1,0:T(2,128)S(1)}, u32[]{:S(2)}, u32[]{:S(2)}) collective-permute-start(f32[8,2,256]{2,1,0:T(2,128)S(1)} %add.7.refs_2_), channel_id=1, source_target_pairs={{0,2},{1,3},{2,0},{3,1},{4,6},{5,7},{6,4},{7,5},{8,10},{9,11},{10,... | collective-permute-start | bytes 49160 | tf_op jit(solution)/shard_map/ppermute | solution.py:393
  87.9 5.2 %collective-permute-start.11 = (bf16[4,4,32,768]{3,2,1,0:T(8,128)(2,1)S(1)}, bf16[4,4,32,768]{3,2,1,0:T(8,128)(2,1)S(1)}, u32[]{:S(2)}, u32[]{:S(2)}) collective-permute-start(bf16[4,4,32,768]{3,2,1,0:T(8,128)(2,1)S(1)} %get-tuple-element.76), channel_id=1, source_target_pairs={{0,4},{4,0},{8,12},{12,8},{16,20},{20,16},{24,28},{28,24},{1,5},{5... | collective-permute-start | bytes 2359304 | tf_op jit(solution)/shard_map/ppermute | solution.py:482
  88.0 9.8 %collective-permute-start.12 = (bf16[8,1,64,256]{3,2,1,0:T(8,128)(2,1)S(1)}, bf16[8,1,64,256]{3,2,1,0:T(8,128)(2,1)S(1)}, u32[]{:S(2)}, u32[]{:S(2)}) collective-permute-start(bf16[8,1,64,256]{3,2,1,0:T(8,128)(2,1)S(1)} %get-tuple-element.79), channel_id=1, source_target_pairs={{0,1},{1,2},{2,3},{4,5},{5,6},{6,7},{8,9},{9,10},{10,11},{12,13},{... | collective-permute-start | bytes 786440 | tf_op jit(solution)/shard_map/ppermute | solution.py:379
  91.6 10.3 %collective-permute-start.13 = (bf16[8,1,64,256]{3,2,1,0:T(8,128)(2,1)S(1)}, bf16[8,1,64,256]{3,2,1,0:T(8,128)(2,1)S(1)}, u32[]{:S(2)}, u32[]{:S(2)}) collective-permute-start(bf16[8,1,64,256]{3,2,1,0:T(8,128)(2,1)S(1)} %get-tuple-element.80), channel_id=1, source_target_pairs={{1,0},{2,1},{3,2},{5,4},{6,5},{7,6},{9,8},{10,9},{11,10},{13,12},{... | collective-permute-start | bytes 786440 | tf_op jit(solution)/shard_map/ppermute | solution.py:379
  93.3 15.6 %collective-permute-start.14 = (bf16[4,32,768]{2,1,0:T(8,128)(2,1)S(1)}, bf16[4,32,768]{2,1,0:T(8,128)(2,1)S(1)}, u32[]{:S(2)}, u32[]{:S(2)}) collective-permute-start(bf16[4,32,768]{2,1,0:T(8,128)(2,1)S(1)} %get-tuple-element.83), channel_id=1, source_target_pairs={{0,8},{4,12},{8,0},{12,4},{16,24},{20,28},{24,16},{28,20},{1,9},{5... | collective-permute-start | bytes 589832 | tf_op jit(solution)/shard_map/ppermute | solution.py:487
  97.8 11.1 %collective-permute-start.15 = (bf16[4,32,768]{2,1,0:T(8,128)(2,1)S(1)}, bf16[4,32,768]{2,1,0:T(8,128)(2,1)S(1)}, u32[]{:S(2)}, u32[]{:S(2)}) collective-permute-start(bf16[4,32,768]{2,1,0:T(8,128)(2,1)S(1)} %get-tuple-element.84), channel_id=1, source_target_pairs={{0,16},{4,20},{8,24},{12,28},{16,0},{20,4},{24,8},{28,12},{1,17},{... | collective-permute-start | bytes 589832 | tf_op jit(solution)/shard_map/ppermute | solution.py:487
  101.9 7.1 %collective-permute-start.16 = (bf16[4,32,768]{2,1,0:T(8,128)(2,1)S(1)}, bf16[4,32,768]{2,1,0:T(8,128)(2,1)S(1)}, u32[]{:S(2)}, u32[]{:S(2)}) collective-permute-start(bf16[4,32,768]{2,1,0:T(8,128)(2,1)S(1)} %get-tuple-element.85), channel_id=1, source_target_pairs={{0,24},{4,28},{8,16},{12,20},{16,8},{20,12},{24,0},{28,4},{1,25},{... | collective-permute-start | bytes 589832 | tf_op jit(solution)/shard_map/ppermute | solution.py:487
  109.1 4.5 %collective-permute-start.17 = (bf16[32,768]{1,0:T(8,128)(2,1)S(1)}, bf16[32,768]{1,0:T(8,128)(2,1)S(1)}, u32[]{:S(2)}, u32[]{:S(2)}) collective-permute-start(bf16[32,768]{1,0:T(8,128)(2,1)S(1)} %get-tuple-element.87), channel_id=1, source_target_pairs={{0,1},{1,0},{2,3},{3,2},{4,5},{5,4},{6,7},{7,6},{8,9},{9,8},{10,11... | collective-permute-start | bytes 147464 | tf_op jit(solution)/shard_map/ppermute | solution.py:499
  111.2 6.0 %collective-permute-start.18 = (bf16[32,768]{1,0:T(8,128)(2,1)S(1)}, bf16[32,768]{1,0:T(8,128)(2,1)S(1)}, u32[]{:S(2)}, u32[]{:S(2)}) collective-permute-start(bf16[32,768]{1,0:T(8,128)(2,1)S(1)} %get-tuple-element.88), channel_id=1, source_target_pairs={{0,2},{1,3},{2,0},{3,1},{4,6},{5,7},{6,4},{7,5},{8,10},{9,11},{10,... | collective-permute-start | bytes 147464 | tf_op jit(solution)/shard_map/ppermute | solution.py:499
  112.7 6.0 %collective-permute-start.19 = (bf16[32,768]{1,0:T(8,128)(2,1)S(1)}, bf16[32,768]{1,0:T(8,128)(2,1)S(1)}, u32[]{:S(2)}, u32[]{:S(2)}) collective-permute-start(bf16[32,768]{1,0:T(8,128)(2,1)S(1)} %get-tuple-element.89), channel_id=1, source_target_pairs={{0,3},{1,2},{2,1},{3,0},{4,7},{5,6},{6,5},{7,4},{8,11},{9,10},{10,... | collective-permute-start | bytes 147464 | tf_op jit(solution)/shard_map/ppermute | solution.py:499
  118.7 6.0 %collective-permute-start.22 = (bf16[32,768]{1,0:T(8,128)(2,1)S(1)}, bf16[32,768]{1,0:T(8,128)(2,1)S(1)}, u32[]{:S(2)}, u32[]{:S(2)}) collective-permute-start(bf16[32,768]{1,0:T(8,128)(2,1)S(1)} %line_sum.1.refs_0_), channel_id=1, source_target_pairs={{0,3},{1,2},{2,1},{3,0},{4,7},{5,6},{6,5},{7,4},{8,11},{9,10},{10,... | collective-permute-start | bytes 147464 | tf_op jit(solution)/shard_map/ppermute | solution.py:503
  119.7 6.0 %collective-permute-start.21 = (bf16[32,768]{1,0:T(8,128)(2,1)S(1)}, bf16[32,768]{1,0:T(8,128)(2,1)S(1)}, u32[]{:S(2)}, u32[]{:S(2)}) collective-permute-start(bf16[32,768]{1,0:T(8,128)(2,1)S(1)} %line_sum.1.refs_0_), channel_id=1, source_target_pairs={{0,2},{1,3},{2,0},{3,1},{4,6},{5,7},{6,4},{7,5},{8,10},{9,11},{10,... | collective-permute-start | bytes 147464 | tf_op jit(solution)/shard_map/ppermute | solution.py:503
  120.1 5.6 %collective-permute-start.20 = (bf16[32,768]{1,0:T(8,128)(2,1)S(1)}, bf16[32,768]{1,0:T(8,128)(2,1)S(1)}, u32[]{:S(2)}, u32[]{:S(2)}) collective-permute-start(bf16[32,768]{1,0:T(8,128)(2,1)S(1)} %line_sum.1.refs_0_), channel_id=1, source_target_pairs={{0,1},{1,0},{2,3},{3,2},{4,5},{5,4},{6,7},{7,6},{8,9},{9,8},{10,11... | collective-permute-start | bytes 147464 | tf_op jit(solution)/shard_map/ppermute | solution.py:503
  125.7 8.5 %collective-permute-start.27 = (bf16[4,32,768]{2,1,0:T(8,128)(2,1)S(1)}, bf16[4,32,768]{2,1,0:T(8,128)(2,1)S(1)}, u32[]{:S(2)}, u32[]{:S(2)}) collective-permute-start(bf16[4,32,768]{2,1,0:T(8,128)(2,1)S(1)} %line_place.1.refs_0_), channel_id=1, source_target_pairs={{0,24},{4,28},{8,16},{12,20},{16,8},{20,12},{24,0},{28,4},{1,25},{... | collective-permute-start | bytes 589832 | tf_op jit(solution)/shard_map/ppermute | solution.py:507
  127.5 6.9 %collective-permute-start.26 = (bf16[4,32,768]{2,1,0:T(8,128)(2,1)S(1)}, bf16[4,32,768]{2,1,0:T(8,128)(2,1)S(1)}, u32[]{:S(2)}, u32[]{:S(2)}) collective-permute-start(bf16[4,32,768]{2,1,0:T(8,128)(2,1)S(1)} %line_place.1.refs_0_), channel_id=1, source_target_pairs={{0,16},{4,20},{8,24},{12,28},{16,0},{20,4},{24,8},{28,12},{1,17},{... | collective-permute-start | bytes 589832 | tf_op jit(solution)/shard_map/ppermute | solution.py:507
  127.5 6.9 %collective-permute-start.25 = (bf16[4,32,768]{2,1,0:T(8,128)(2,1)S(1)}, bf16[4,32,768]{2,1,0:T(8,128)(2,1)S(1)}, u32[]{:S(2)}, u32[]{:S(2)}) collective-permute-start(bf16[4,32,768]{2,1,0:T(8,128)(2,1)S(1)} %line_place.1.refs_0_), channel_id=1, source_target_pairs={{0,8},{4,12},{8,0},{12,4},{16,24},{20,28},{24,16},{28,20},{1,9},{5... | collective-permute-start | bytes 589832 | tf_op jit(solution)/shard_map/ppermute | solution.py:507
  134.6 2.4 %collective-permute-start.28 = (bf16[4,4,32,768]{3,2,1,0:T(8,128)(2,1)S(1)}, bf16[4,4,32,768]{3,2,1,0:T(8,128)(2,1)S(1)}, u32[]{:S(2)}, u32[]{:S(2)}) collective-permute-start(bf16[4,4,32,768]{3,2,1,0:T(8,128)(2,1)S(1)} %plane_place.1.mine_ref), channel_id=1, source_target_pairs={{0,4},{4,0},{8,12},{12,8},{16,20},{20,16},{24,28},{28,24},{1,5},{5... | collective-permute-start | bytes 2359304 | tf_op jit(solution)/shard_map/ppermute | solution.py:519
where the time goes:
time: 139 us
  waiting for transfers between devices  45.2 us (33%)
  starting transfers between devices  44.2 us (32%)
  Pallas kernels  44.2 us (32%)
  local copies, waits for them, and re-layouts  4.12 us (3%)
    pallas_call x16, Pallas kernels, call(): pl.pallas_call(kernel, in_specs=[smem if x.dtype == jnp.int32 else vmem f...  44.2 us
    ppermute x4, waiting for transfers between devices, neighbours(): return (lax.ppermute(high, axis, up), lax.ppermute(low, axis, down))  13.5 us
    ppermute x1, waiting for transfers between devices, per_device(): cot_around.append(lax.ppermute(relayed, 'tm', [(7, 4), (0, 3)]))  12.2 us
    ppermute x4, starting transfers between devices, neighbours(): return (lax.ppermute(high, axis, up), lax.ppermute(low, axis, down))  11.4 us
    ppermute x4, starting transfers between devices, spread_sums(): got = lax.ppermute(part, axis, [(i, i ^ step) for i in range(size)])  9.92 us
    ppermute x1, waiting for transfers between devices, per_device(): relayed = lax.ppermute(late[frames // 2:], 'tm', [(3, 7), (4, 0)])  5.37 us
    ppermute x3, waiting for transfers between devices, per_device(): lax.ppermute(x, 'space', other_plane(s))  5.02 us
    ppermute x3, starting transfers between devices, per_device(): lax.ppermute(x, 'space', other_plane(s))  4.54 us
  transfers between devices with their start and end apart: 29, of which 15 were waited for; matrix products, arithmetic and copies ran while one was open for 0% of the time, Pallas kernels for 30%

commit v1 on v0

--- a/solution.py
+++ b/solution.py
@@ -54,10 +54,6 @@
     for ref in part_refs[1:]:
         total = total + ref[f]
     return group_total(total, group_size) / entries
-
-
-def sigmoid(x):
-    return 0.5 * jnp.tanh(0.5 * x) + 0.5
 
 
 def mean_and_inv(part_refs, f, entries, group_size):
@@ -110,10 +106,9 @@
     return (later, later_which), (earlier, earlier_which), used
 
 
-def gather_taps(clip_ref, dil_ref, local, own, nxt, prv, corner, cat_ref, at, up_slot):
+def gather_taps(clip_ref, dil_ref, local, own, nxt, prv, cat_ref, at, up_slot):
     frames, pixels, channels = own.shape
     later, earlier, used = slot_sources(clip_ref, dil_ref, local, frames)
-    me, half = lax.axis_index("tm"), frames // 2
 
     def put(slot, ref, index):
         cat_ref[pl.ds(at, pixels), slot * channels : (slot + 1) * channels] = ref[index]
@@ -121,21 +116,13 @@
     def clear(slot):
         cat_ref[pl.ds(at, pixels), slot * channels : (slot + 1) * channels] = jnp.zeros((pixels, channels), BF16)
 
-    for slot, (index, which), other, shift, turn in (
-        (up_slot, later, nxt, -frames, 3),
-        (2 - up_slot, earlier, prv, frames, 4),
+    for slot, (index, which), other, shift in (
+        (up_slot, later, nxt, -frames),
+        (2 - up_slot, earlier, prv, frames),
     ):
-        beyond = which == 2
-        there = jnp.clip(index + shift, 0, frames - 1)
+        pl.when(which == 0)(functools.partial(clear, slot))
         pl.when(which == 1)(functools.partial(put, slot, own, jnp.clip(index, 0, frames - 1)))
-        pl.when(which == 0)(functools.partial(clear, slot))
-        if corner:
-            by_corner = beyond & (me == turn)
-            low, high = by_corner & (there < half), by_corner & (there >= half)
-            pl.when(low)(functools.partial(put, slot, corner[0], jnp.minimum(there, half - 1)))
-            pl.when(high)(functools.partial(put, slot, corner[1], jnp.maximum(there - half, 0)))
-            beyond = beyond & (me != turn)
-        pl.when(beyond)(functools.partial(put, slot, other, there))
+        pl.when(which == 2)(functools.partial(put, slot, other, jnp.clip(index + shift, 0, frames - 1)))
     pl.when(used)(functools.partial(put, 1, own, local))
     pl.when(jnp.logical_not(used))(functools.partial(clear, 1))
 
@@ -173,15 +160,17 @@
     frames = conv_ref.shape[0]
     first = lax.axis_index("tm") * frames
     filled = clip_ref[0] + clip_ref[1]
+    half_gain, half_shift = 0.5 * gain_ref[...], 0.5 * shift_ref[...]
 
     def body(f):
         mean, inv = mean_and_inv(parts, f, entries, group_size)
         normed = (conv_ref[f] - mean) * inv
-        shaped = normed * gain_ref[...] + shift_ref[...]
-        sig = sigmoid(shaped)
-        act_ref[f] = jnp.where(first + f < filled, shaped * sig, 0.0).astype(BF16)
+        h = normed * half_gain + half_shift
+        t = jnp.tanh(h)
+        rise = 1.0 + t
+        act_ref[f] = jnp.where(first + f < filled, h * rise, 0.0).astype(BF16)
         normed_ref[f] = normed.astype(BF16)
-        slope_ref[f] = (sig * (1.0 + shaped * (1.0 - sig)) * gain_ref[...]).astype(BF16)
+        slope_ref[f] = (rise * (1.0 + h * (1.0 - t)) * half_gain).astype(BF16)
 
     loop(frames, body)
 
@@ -210,15 +199,16 @@
             back_ref[j, rows] = spatial_ref[i, j].T
 
 
-def grad_act_kernel(corners, clip_ref, dil_ref, own, nxt, prv, *refs):
-    corner, (tw_ref, normed_ref, slope_ref, ga_ref, cat_ref, sums_ref) = refs[:corners], refs[corners:]
+def grad_act_kernel(
+    clip_ref, dil_ref, own, nxt, prv, tw_ref, normed_ref, slope_ref, ga_ref, cat_ref, sums_ref
+):
     frames, pixels, _ = own.shape
 
     def body(pair):
         rows = pl.ds(pl.multiple_of(2 * pair * pixels, 2 * pixels), 2 * pixels)
         for b in range(2):
             at = pl.multiple_of((2 * pair + b) * pixels, pixels)
-            gather_taps(clip_ref, dil_ref, 2 * pair + b, own, nxt, prv, corner, cat_ref, at, 0)
+            gather_taps(clip_ref, dil_ref, 2 * pair + b, own, nxt, prv, cat_ref, at, 0)
         grad_act = dot(cat_ref[rows], tw_ref[...]).astype(BF16)
         for b in range(2):
             f = 2 * pair + b
@@ -258,11 +248,15 @@
     loop(normed_ref.shape[0], body)
 
 
-def weight_grad_kernel(xt_ref, moved_ref, temporal_ref, send_ref, keep_ref, acc_ref):
+def weight_part_kernel(xt_ref, moved_ref, out_ref):
+    out_ref[...] = dot(xt_ref[...], moved_ref[:, : out_ref.shape[1]])
+
+
+def weight_grad_kernel(xt_ref, moved_ref, part_ref, temporal_ref, send_ref, keep_ref, acc_ref):
     channels = temporal_ref.shape[0]
-    for j in range(3):
-        lanes = slice(j * channels, (j + 1) * channels)
-        acc_ref[: 3 * channels, lanes] = dot(xt_ref[...], moved_ref[:, lanes])
+    done = part_ref.shape[1]
+    acc_ref[: 3 * channels, done:] = dot(xt_ref[...], moved_ref[:, done:])
+    acc_ref[: 3 * channels, :done] = part_ref[...]
     acc_ref[3 * channels :, :] = temporal_ref[...]
 
     chips, depth, block, _ = keep_ref.shape
@@ -298,14 +292,13 @@
     loop(frames // 2, body)
 
 
-def out_kernel(corners, clip_ref, dil_ref, own, nxt, prv, *refs):
-    corner, (tw_ref, x_ref, out_ref, cat_ref) = refs[:corners], refs[corners:]
+def out_kernel(clip_ref, dil_ref, own, nxt, prv, tw_ref, x_ref, out_ref, cat_ref):
     frames, rows, width, channels = x_ref.shape
     pixels = rows * width
 
     def body(pair):
         for b in range(2):
-            gather_taps(clip_ref, dil_ref, 2 * pair + b, own, nxt, prv, corner, cat_ref, b * pixels, 2)
+            gather_taps(clip_ref, dil_ref, 2 * pair + b, own, nxt, prv, cat_ref, b * pixels, 2)
         temporal_out = dot(cat_ref[...], tw_ref[...]).astype(BF16).astype(F32)
         for b in range(2):
             one = temporal_out[b * pixels : (b + 1) * pixels].reshape(rows, width, channels)
@@ -379,11 +372,6 @@
     return lax.ppermute(high, axis, up), lax.ppermute(low, axis, down)
 
 
-def near_frames(x, corner):
-    pairs = [(i, i + 1) for i in range(lax.axis_size("tm") - 1) if corner or i != 3]
-    return lax.ppermute(x, "tm", [(j, i) for i, j in pairs]), lax.ppermute(x, "tm", pairs)
-
-
 def spread_sums(part, axis):
     size = lax.axis_size(axis)
     step, got = 1, None
@@ -408,46 +396,37 @@
     per_px = (frames, pixels, channels)
     windows = pltpu.VMEM((2 * pixels, 3 * channels), BF16)
 
-    first, last = frames_in[:, :1], frames_in[:, rows - 1 :]
-    first, last, cot = lax.optimization_barrier((first, last, cotangent.reshape(per_px)))
-    above, below = neighbours("space", first, last)
-    by_corner = tm == 8
-    cot_around = list(near_frames(cot, not by_corner))
-
+    cot = cotangent.reshape(per_px)
+    cot_prev, cot_next = neighbours("tm", cot, cot)
+    above, below = neighbours("space", frames_in[:, :1], frames_in[:, rows - 1 :])
+
+    back_weights, back_taps = call(
+        turn_weights_kernel, "turn_weights", [spatial, temporal],
+        [shape((3, 3 * channels, channels), BF16), shape((3 * channels, channels), BF16)], 0, big,
+    )
+    above, back_weights, back_taps = lax.optimization_barrier((above, back_weights, back_taps))
     conv_out, sums = call(
         conv_kernel, "conv_forward", [frames_in, above, below, spatial],
         [shape(per_px, F32), shape((frames, 2, channels), F32)],
         18 * big * channels, 8 * big, [windows], 18,
     )
-    if by_corner:
-        sums, late = lax.optimization_barrier((sums, cot))
-        relayed = lax.ppermute(late[frames // 2 :], "tm", [(3, 7), (4, 0)])
-        cot_around.append(lax.ppermute(late[: frames // 2], "tm", [(3, 4), (4, 3)]))
     parts = spread_sums(sums, "space")
     x_turned = call(
         turn_kernel, "turned", [frames_in, above, below], shape((3 * channels, frames * pixels), BF16),
         0, 8 * big, [pltpu.VMEM((pixels, 3 * channels), BF16)],
     )
-    back_weights, back_taps = call(
-        turn_weights_kernel, "turn_weights", [spatial, temporal],
-        [shape((3, 3 * channels, channels), BF16), shape((3 * channels, channels), BF16)], 0, big,
-    )
-    x_turned, back_weights, back_taps, *parts = lax.optimization_barrier((x_turned, back_weights, back_taps, *parts))
-    if by_corner:
-        relayed, *parts = lax.optimization_barrier((relayed, *parts))
-        cot_around.append(lax.ppermute(relayed, "tm", [(7, 4), (0, 3)]))
-    corners = len(cot_around) - 2
+    x_turned, *parts = lax.optimization_barrier((x_turned, *parts))
     act, normed, slope = call(
         functools.partial(act_kernel, len(parts), entries, group_size), "activation",
         [clip_frames, *parts, conv_out, gain, shift],
         [shape(per_px, BF16)] * 3, 10 * big, 10 * big,
     )
-    act_sent, *cot_around[:2] = lax.optimization_barrier((act, *cot_around[:2]))
-    act_around = near_frames(act_sent, True)
+    act_sent, cot_prev, cot_next = lax.optimization_barrier((act, cot_prev, cot_next))
+    act_prev, act_next = neighbours("tm", act_sent, act_sent)
 
     grad_act, cot_cat, grad_sums = call(
-        functools.partial(grad_act_kernel, corners), "grad_activation",
-        [clip_frames, dilation, cot, *cot_around, back_taps, normed, slope],
+        grad_act_kernel, "grad_activation",
+        [clip_frames, dilation, cot, cot_next, cot_prev, back_taps, normed, slope],
         [shape(per_px, BF16), shape((frames * pixels, 3 * channels), BF16), shape((frames, 2, channels), F32)],
         6 * big * channels, 16 * big,
     )
@@ -465,11 +444,16 @@
         0, 12 * big,
     )
     grad_above, grad_below = neighbours("space", first_rows, last_rows)
+    part = call(
+        weight_part_kernel, "weight_part", [x_turned, moved], shape((lanes, 2 * channels), F32),
+        12 * big * channels, 8 * big,
+    )
+    moved, grad_above, grad_below = lax.optimization_barrier((moved, grad_above, grad_below))
     block = 2 * channels // (chips * n)
     send, keep = call(
-        weight_grad_kernel, "weight_grad", [x_turned, moved, temporal_part],
+        weight_grad_kernel, "weight_grad", [x_turned, moved, part, temporal_part],
         [shape((chips, n, block, lanes), BF16), shape((chips, n, block, lanes), F32)],
-        18 * big * channels, 12 * big, [pltpu.VMEM((4 * channels, lanes), F32)], 20,
+        6 * big * channels, 8 * big, [pltpu.VMEM((4 * channels, lanes), F32)], 20,
     )
 
     def other_chip(s):
@@ -507,8 +491,8 @@
     gots = [lax.ppermute(own, "tm", other_chip(s)) for s in range(1, chips)]
 
     out_frames = call(
-        functools.partial(out_kernel, 0), "temporal_forward",
-        [clip_frames, dilation, act, *act_around, temporal.reshape(3 * channels, channels), frames_in],
+        out_kernel, "temporal_forward",
+        [clip_frames, dilation, act, act_next, act_prev, temporal.reshape(3 * channels, channels), frames_in],
         shape(frames_in.shape, BF16), 6 * big * channels, 10 * big, [windows],
     )
     own, out_frames = lax.optimization_barrier((own, out_frames))

time: 139 us -> 142 us (1.022)
  starting transfers between devices: 44.2 us -> 57.7 us
  waiting for transfers between devices: 45.2 us -> 34.3 us
    ppermute x7 -> x0, waiting for transfers between devices: 17.6 us -> none  [the longest x1 12.2 us: per_device(): cot_around.append(lax.ppermute(relayed, 'tm', [(7, 4), (0, 3)]))]
    ppermute x4 -> x8, starting transfers between devices: 11.4 us -> 23.8 us  [neighbours(): return (lax.ppermute(high, axis, up), lax.ppermute(low, axis, down))]
    ppermute x7 -> x0, starting transfers between devices: 9.56 us -> none  [the longest x2 3.02 us: near_frames(): lax.ppermute(x, 'tm', pairs)]
    ppermute x3, starting transfers between devices: 0.65 us -> 8.83 us  [per_device(): lax.ppermute(x, 'tm', other_chip(s))]
    ppermute x3, waiting for transfers between devices: 0.14 us -> 4.4 us  [per_device(): lax.ppermute(x, 'tm', other_chip(s))]
    ppermute x3, starting transfers between devices: 3.55 us -> 7.44 us  [per_device(): gots = [lax.ppermute(own, 'tm', other_chip(s)) for s in range(1, chips)]]
    ppermute x1, waiting for transfers between devices: 0.01 us -> 2.27 us  [per_device(): got = lax.ppermute(send, 'tm', other_core)]
    ppermute x4 -> x8, waiting for transfers between devices: 13.5 us -> 11.6 us  [neighbours(): return (lax.ppermute(high, axis, up), lax.ppermute(low, axis, down))]
  transfers between devices with their start and end apart: 29 -> 26, of which waited for: 15 -> 15; matrix products, arithmetic and copies ran while one was open for 0% -> 1% of each run, Pallas kernels for 30% -> 30%
where the time goes in v1:
time: 142 us
  starting transfers between devices  57.7 us (41%)
  Pallas kernels  44 us (31%)
  waiting for transfers between devices  34.3 us (24%)
  local copies, waits for them, and re-layouts  4.65 us (3%)
    pallas_call x17, Pallas kernels, call(): pl.pallas_call(kernel, in_specs=[smem if x.dtype == jnp.int32 else vmem f...  44 us
    ppermute x8, starting transfers between devices, neighbours(): return (lax.ppermute(high, axis, up), lax.ppermute(low, axis, down))  23.8 us
    ppermute x8, waiting for transfers between devices, neighbours(): return (lax.ppermute(high, axis, up), lax.ppermute(low, axis, down))  11.6 us
    ppermute x3, starting transfers between devices, per_device(): lax.ppermute(x, 'tm', other_chip(s))  8.83 us
    ppermute x4, starting transfers between devices, spread_sums(): got = lax.ppermute(part, axis, [(i, i ^ step) for i in range(size)])  8.57 us
    ppermute x3, starting transfers between devices, per_device(): gots = [lax.ppermute(own, 'tm', other_chip(s)) for s in range(1, chips)]  7.44 us
    ppermute x3, waiting for transfers between devices, per_device(): lax.ppermute(x, 'space', other_plane(s))  5.66 us
    ppermute x4, waiting for transfers between devices, spread_sums(): got = lax.ppermute(part, axis, [(i, i ^ step) for i in range(size)])  4.52 us
  transfers between devices with their start and end apart: 26, of which 15 were waited for; matrix products, arithmetic and copies ran while one was open for 1% of the time, Pallas kernels for 30%

profile of v1, /device:TPU:0, one launch (start us, length us, event | category | flops | bytes accessed | tf_op | source)
XLA Modules:
  0.0 141.7 jit_solution(6426565720571185416)
XLA Ops:
  0.6 1.4 %collective-permute-start.5 = (bf16[8,512,256]{2,1,0:T(8,128)(2,1)}, bf16[8,512,256]{2,1,0:T(8,128)(2,1)S(1)}, u32[]{:S(2)}, u32[]{:S(2)}) collective-permute-start(bf16[8,512,256]{2,1,0:T(8,128)(2,1)} %bitcast.4), channel_id=1, source_target_pairs={{4,0},{8,4},{12,8},{16,12},{20,16},{24,20},{28,24},{5,1},{9,5},{13... | collective-permute-start | bytes 6291464 | tf_op jit(solution)/shard_map/ppermute | solution.py:372
  2.1 3.2 %collective-permute-start.4 = (bf16[8,512,256]{2,1,0:T(8,128)(2,1)}, bf16[8,512,256]{2,1,0:T(8,128)(2,1)S(1)}, u32[]{:S(2)}, u32[]{:S(2)}) collective-permute-start(bf16[8,512,256]{2,1,0:T(8,128)(2,1)} %bitcast.5), channel_id=1, source_target_pairs={{0,4},{4,8},{8,12},{12,16},{16,20},{20,24},{24,28},{1,5},{5,9},{9,... | collective-permute-start | bytes 6291464 | tf_op jit(solution)/shard_map/ppermute | solution.py:372
  5.2 1.1 fusion
  6.3 4.9 %collective-permute-start = (bf16[8,1,64,256]{3,2,1,0:T(8,128)(2,1)S(1)}, bf16[8,1,64,256]{3,2,1,0:T(8,128)(2,1)S(1)}, u32[]{:S(2)}, u32[]{:S(2)}) collective-permute-start(bf16[8,1,64,256]{3,2,1,0:T(8,128)(2,1)S(1)} %get-tuple-element.89), channel_id=1, source_target_pairs={{0,1},{1,2},{2,3},{4,5},{5,6},{6,7},{8,9},{9,10},{10,11},{12,13},{... | collective-permute-start | bytes 786440 | tf_op jit(solution)/shard_map/ppermute | solution.py:372
  11.3 1.3 collective-permute-start.1
  12.6 0.0 copy-start.2
  12.6 1.0 copy-done.2
  13.6 1.3 copy-done.4
  14.9 0.5 turn_weights.1
  15.3 2.6 %collective-permute-done.above_ref = bf16[8,1,64,256]{3,2,1,0:T(8,128)(2,1)S(1)} collective-permute-done((bf16[8,1,64,256]{3,2,1,0:T(8,128)(2,1)S(1)}, bf16[8,1,64,256]{3,2,1,0:T(8,128)(2,1)S(1)}, u32[]{:S(2)}, u32[]{:S(2)}) %collective-permute-start) | collective-permute-done | bytes 262176 | tf_op jit(solution)/shard_map/ppermute | solution.py:372
  17.9 4.1 %collective-permute-done.1.below_ref = bf16[8,1,64,256]{3,2,1,0:T(8,128)(2,1)S(1)} collective-permute-done((bf16[8,1,64,256]{3,2,1,0:T(8,128)(2,1)S(1)}, bf16[8,1,64,256]{3,2,1,0:T(8,128)(2,1)S(1)}, u32[]{:S(2)}, u32[]{:S(2)}) %collective-permute-start.1) | collective-permute-done | bytes 262176 | tf_op jit(solution)/shard_map/ppermute | solution.py:372
  22.1 1.3 copy-done.5
  23.4 5.6 %conv_forward.1 = (f32[8,512,256]{2,1,0:T(8,128)S(1)}, f32[8,2,256]{2,1,0:T(2,128)S(1)}) custom-call(bf16[8,8,64,256]{3,2,1,0:T(8,128)(2,1)S(1)} %copy-done, bf16[8,1,64,256]{3,2,1,0:T(8,128)(2,1)S(1)} %collective-permute-done.above_ref, bf16[8,1,64,256]{3,2,1,0:T(8,128)(2,1)S(1)} %collective-permute-done.1.below_ref, bf16[3,3,256,256]{3,2,1,0:T(8,128)(2,1)S(1)} %copy-done.5), custom_call_target="tpu_custom_call" | custom-call | flops 4831838208 | bytes 8388608 | tf_op jit(solution)/shard_map/conv_forward/pallas_call | solution.py:20
  29.0 1.6 %collective-permute-start.2 = (f32[8,2,256]{2,1,0:T(2,128)S(1)}, f32[8,2,256]{2,1,0:T(2,128)S(1)}, u32[]{:S(2)}, u32[]{:S(2)}) collective-permute-start(f32[8,2,256]{2,1,0:T(2,128)S(1)} %get-tuple-element.49), channel_id=1, source_target_pairs={{0,1},{1,0},{2,3},{3,2},{4,5},{5,4},{6,7},{7,6},{8,9},{9,8},{10,11... | collective-permute-start | bytes 49160 | tf_op jit(solution)/shard_map/ppermute | solution.py:381
  30.6 2.2 %collective-permute-done.2 = f32[8,2,256]{2,1,0:T(2,128)S(1)} collective-permute-done((f32[8,2,256]{2,1,0:T(2,128)S(1)}, f32[8,2,256]{2,1,0:T(2,128)S(1)}, u32[]{:S(2)}, u32[]{:S(2)}) %collective-permute-start.2) | collective-permute-done | bytes 16416 | tf_op jit(solution)/shard_map/ppermute | solution.py:381
  32.8 0.0 copy-start.6
  32.8 0.0 copy-start.8
  32.8 0.0 copy-start.9
  32.9 2.6 %collective-permute-start.3 = (f32[8,2,256]{2,1,0:T(2,128)S(1)}, f32[8,2,256]{2,1,0:T(2,128)S(1)}, u32[]{:S(2)}, u32[]{:S(2)}) collective-permute-start(f32[8,2,256]{2,1,0:T(2,128)S(1)} %add.6.refs_0_), channel_id=1, source_target_pairs={{0,2},{1,3},{2,0},{3,1},{4,6},{5,7},{6,4},{7,5},{8,10},{9,11},{10,... | collective-permute-start | bytes 49160 | tf_op jit(solution)/shard_map/ppermute | solution.py:381
  35.5 2.2 %turned.1.xt_ref = bf16[768,4096]{1,0:T(8,128)(2,1)S(1)} custom-call(bf16[8,8,64,256]{3,2,1,0:T(8,128)(2,1)S(1)} %copy-done, bf16[8,1,64,256]{3,2,1,0:T(8,128)(2,1)S(1)} %collective-permute-done.above_ref, bf16[8,1,64,256]{3,2,1,0:T(8,128)(2,1)S(1)} %collective-permute-done.1.below_ref), custom_call_target="tpu_custom_call" | custom-call | bytes 8388608 | tf_op jit(solution)/shard_map/turned/pallas_call | solution.py:20
  37.7 0.0 copy-start.1
  37.7 0.0 copy-start.7
  37.7 5.7 %activation.1 = (bf16[8,512,256]{2,1,0:T(8,128)(2,1)S(1)}, bf16[8,512,256]{2,1,0:T(8,128)(2,1)S(1)}, bf16[8,512,256]{2,1,0:T(8,128)(2,1)S(1)}) custom-call(s32[2]{0:T(128)S(1)} %copy-done.6, f32[8,2,256]{2,1,0:T(2,128)S(1)} %add.6.refs_0_, f32[8,2,256]{2,1,0:T(2,128)S(1)} %collective-permute-done.3.refs_1_, f32[8,512,256]{2,1,0:T(8,128)S(1)} %get-tuple-element.53.refs_2_, ...), custom_call_target="tpu_custom_call" | custom-call | flops 10485760 | bytes 10485760 | tf_op jit(solution)/shard_map/activation/pallas_call | solution.py:20
  43.5 6.9 %collective-permute-start.21 = (bf16[8,512,256]{2,1,0:T(8,128)(2,1)S(1)}, bf16[8,512,256]{2,1,0:T(8,128)(2,1)S(1)}, u32[]{:S(2)}, u32[]{:S(2)}) collective-permute-start(bf16[8,512,256]{2,1,0:T(8,128)(2,1)S(1)} %get-tuple-element.82.act_ref.own), channel_id=1, source_target_pairs={{0,4},{4,8},{8,12},{12,16},{16,20},{20,24},{24,28},{1,5},{5,9},{9,... | collective-permute-start | bytes 6291464 | tf_op jit(solution)/shard_map/ppermute | solution.py:372
  50.4 1.3 collective-permute-start.20
  51.7 3.9 %grad_activation.1 = (bf16[8,512,256]{2,1,0:T(8,128)(2,1)S(1)}, bf16[4096,768]{1,0:T(8,128)(2,1)S(1)}, f32[8,2,256]{2,1,0:T(2,128)S(1)}) custom-call(s32[2]{0:T(128)S(1)} %copy-done.6, s32[2]{0:T(128)S(1)} %copy-done.7, bf16[8,512,256]{2,1,0:T(8,128)(2,1)S(1)} %bitcast.6, bf16[8,512,256]{2,1,0:T(8,128)(2,1)S(1)} %collective-permute-done.5.nxt, ...), custom_call_target="tpu_custom_call" | custom-call | flops 1610612736 | bytes 16777216 | tf_op jit(solution)/shard_map/grad_activation/pallas_call | solution.py:20
  55.6 1.6 %collective-permute-start.6 = (f32[8,2,256]{2,1,0:T(2,128)S(1)}, f32[8,2,256]{2,1,0:T(2,128)S(1)}, u32[]{:S(2)}, u32[]{:S(2)}) collective-permute-start(f32[8,2,256]{2,1,0:T(2,128)S(1)} %get-tuple-element.61), channel_id=1, source_target_pairs={{0,1},{1,0},{2,3},{3,2},{4,5},{5,4},{6,7},{7,6},{8,9},{9,8},{10,11... | collective-permute-start | bytes 49160 | tf_op jit(solution)/shard_map/ppermute | solution.py:381
  57.3 2.2 %collective-permute-done.6 = f32[8,2,256]{2,1,0:T(2,128)S(1)} collective-permute-done((f32[8,2,256]{2,1,0:T(2,128)S(1)}, f32[8,2,256]{2,1,0:T(2,128)S(1)}, u32[]{:S(2)}, u32[]{:S(2)}) %collective-permute-start.6) | collective-permute-done | bytes 16416 | tf_op jit(solution)/shard_map/ppermute | solution.py:381
  59.5 2.7 %collective-permute-start.7 = (f32[8,2,256]{2,1,0:T(2,128)S(1)}, f32[8,2,256]{2,1,0:T(2,128)S(1)}, u32[]{:S(2)}, u32[]{:S(2)}) collective-permute-start(f32[8,2,256]{2,1,0:T(2,128)S(1)} %add.7.refs_2_), channel_id=1, source_target_pairs={{0,2},{1,3},{2,0},{3,1},{4,6},{5,7},{6,4},{7,5},{8,10},{9,11},{10,... | collective-permute-start | bytes 49160 | tf_op jit(solution)/shard_map/ppermute | solution.py:381
  62.1 1.9 %temporal_grad.1.temporal_ref = f32[256,768]{1,0:T(8,128)S(1)} custom-call(bf16[8,512,256]{2,1,0:T(8,128)(2,1)S(1)} %get-tuple-element.82.act_ref.own, bf16[4096,768]{1,0:T(8,128)(2,1)S(1)} %get-tuple-element.66.cat_ref), custom_call_target="tpu_custom_call" | custom-call | flops 1610612736 | bytes 8388608 | tf_op jit(solution)/shard_map/temporal_grad/pallas_call | solution.py:20
  64.0 0.2 collective-permute-done.7.refs_3_
  64.2 4.6 %norm_backward.1 = (bf16[8,512,256]{2,1,0:T(8,128)(2,1)S(1)}, bf16[8,1,64,256]{3,2,1,0:T(8,128)(2,1)S(1)}, bf16[8,1,64,256]{3,2,1,0:T(8,128)(2,1)S(1)}, bf16[4096,768]{1,0:T(8,128)(2,1)S(1)}) custom-call(bf16[8,512,256]{2,1,0:T(8,128)(2,1)S(1)} %get-tuple-element.54.normed_ref, bf16[8,512,256]{2,1,0:T(8,128)(2,1)S(1)} %get-tuple-element.55.slope_ref, ...), custom_call_target="tpu_custom_call" | custom-call | bytes 12582912 | tf_op jit(solution)/shard_map/norm_backward/pallas_call | solution.py:20
  68.8 3.5 %collective-permute-start.8 = (bf16[8,1,64,256]{3,2,1,0:T(8,128)(2,1)S(1)}, bf16[8,1,64,256]{3,2,1,0:T(8,128)(2,1)S(1)}, u32[]{:S(2)}, u32[]{:S(2)}) collective-permute-start(bf16[8,1,64,256]{3,2,1,0:T(8,128)(2,1)S(1)} %get-tuple-element.63), channel_id=1, source_target_pairs={{0,1},{1,2},{2,3},{4,5},{5,6},{6,7},{8,9},{9,10},{10,11},{12,13},{... | collective-permute-start | bytes 786440 | tf_op jit(solution)/shard_map/ppermute | solution.py:372
  72.3 1.3 collective-permute-start.9
  73.6 3.4 %weight_part.1.part_ref = f32[768,512]{1,0:T(8,128)S(1)} custom-call(bf16[768,4096]{1,0:T(8,128)(2,1)S(1)} %turned.1.xt_ref, bf16[4096,768]{1,0:T(8,128)(2,1)S(1)} %get-tuple-element.65.moved_ref), custom_call_target="tpu_custom_call" | custom-call | flops 3221225472 | bytes 8388608 | tf_op jit(solution)/shard_map/weight_part/pallas_call | solution.py:20
  77.0 0.7 collective-permute-done.8.above_ref
  77.6 4.1 %collective-permute-done.9.below_ref = bf16[8,1,64,256]{3,2,1,0:T(8,128)(2,1)S(1)} collective-permute-done((bf16[8,1,64,256]{3,2,1,0:T(8,128)(2,1)S(1)}, bf16[8,1,64,256]{3,2,1,0:T(8,128)(2,1)S(1)}, u32[]{:S(2)}, u32[]{:S(2)}) %collective-permute-start.9) | collective-permute-done | bytes 262176 | tf_op jit(solution)/shard_map/ppermute | solution.py:372
  81.8 2.2 %weight_grad.1 = (bf16[4,4,32,768]{3,2,1,0:T(8,128)(2,1)S(1)}, f32[4,4,32,768]{3,2,1,0:T(8,128)S(1)}) custom-call(bf16[768,4096]{1,0:T(8,128)(2,1)S(1)} %turned.1.xt_ref, bf16[4096,768]{1,0:T(8,128)(2,1)S(1)} %get-tuple-element.65.moved_ref, f32[768,512]{1,0:T(8,128)S(1)} %weight_part.1.part_ref, f32[256,768]{1,0:T(8,128)S(1)} %temporal_grad.1.temporal_ref), custom_call_target="tpu_custom_call" | custom-call | flops 1610612736 | bytes 8388608 | tf_op jit(solution)/shard_map/weight_grad/pallas_call | solution.py:20
  84.0 0.1 collective-permute-start.10
  84.1 2.3 %collective-permute-done.10.got_ref = bf16[4,4,32,768]{3,2,1,0:T(8,128)(2,1)S(1)} collective-permute-done((bf16[4,4,32,768]{3,2,1,0:T(8,128)(2,1)S(1)}, bf16[4,4,32,768]{3,2,1,0:T(8,128)(2,1)S(1)}, u32[]{:S(2)}, u32[]{:S(2)}) %collective-permute-start.10) | collective-permute-done | bytes 786464 | tf_op jit(solution)/shard_map/ppermute | solution.py:466
  86.3 0.1 core_sum.1
  86.5 6.0 %collective-permute-start.11 = (bf16[4,32,768]{2,1,0:T(8,128)(2,1)S(1)}, bf16[4,32,768]{2,1,0:T(8,128)(2,1)S(1)}, u32[]{:S(2)}, u32[]{:S(2)}) collective-permute-start(bf16[4,32,768]{2,1,0:T(8,128)(2,1)S(1)} %get-tuple-element.75), channel_id=1, source_target_pairs={{0,8},{4,12},{8,0},{12,4},{16,24},{20,28},{24,16},{28,20},{1,9},{5... | collective-permute-start | bytes 589832 | tf_op jit(solution)/shard_map/ppermute | solution.py:471
  92.4 1.9 %collective-permute-start.12 = (bf16[4,32,768]{2,1,0:T(8,128)(2,1)S(1)}, bf16[4,32,768]{2,1,0:T(8,128)(2,1)S(1)}, u32[]{:S(2)}, u32[]{:S(2)}) collective-permute-start(bf16[4,32,768]{2,1,0:T(8,128)(2,1)S(1)} %get-tuple-element.76), channel_id=1, source_target_pairs={{0,16},{4,20},{8,24},{12,28},{16,0},{20,4},{24,8},{28,12},{1,17},{... | collective-permute-start | bytes 589832 | tf_op jit(solution)/shard_map/ppermute | solution.py:471
  94.4 0.9 collective-permute-start.13
  95.3 7.0 %conv_backward.1 = bf16[8,8,64,256]{3,2,1,0:T(8,128)(2,1)} custom-call(bf16[8,512,256]{2,1,0:T(8,128)(2,1)S(1)} %get-tuple-element.70.g_ref, bf16[8,1,64,256]{3,2,1,0:T(8,128)(2,1)S(1)} %collective-permute-done.8.above_ref, bf16[8,1,64,256]{3,2,1,0:T(8,128)(2,1)S(1)} %collective-permute-done.9.below_ref, bf16[8,8,64,256]{3,2,1,0:T(8,128)(2,1)S(1)} %copy-done.1, ...), custom_call_target="tpu_custom_call" | custom-call | flops 4831838208 | bytes 8388608 | tf_op jit(solution)/shard_map/conv_backward/pallas_call | solution.py:20
  102.3 4.4 %collective-permute-done.11.refs_0_ = bf16[4,32,768]{2,1,0:T(8,128)(2,1)S(1)} collective-permute-done((bf16[4,32,768]{2,1,0:T(8,128)(2,1)S(1)}, bf16[4,32,768]{2,1,0:T(8,128)(2,1)S(1)}, u32[]{:S(2)}, u32[]{:S(2)}) %collective-permute-start.11) | collective-permute-done | bytes 196640 | tf_op jit(solution)/shard_map/ppermute | solution.py:471
  106.7 0.1 plane_sum.1
  106.8 1.7 %collective-permute-start.14 = (bf16[32,768]{1,0:T(8,128)(2,1)S(1)}, bf16[32,768]{1,0:T(8,128)(2,1)S(1)}, u32[]{:S(2)}, u32[]{:S(2)}) collective-permute-start(bf16[32,768]{1,0:T(8,128)(2,1)S(1)} %get-tuple-element.79), channel_id=1, source_target_pairs={{0,1},{1,0},{2,3},{3,2},{4,5},{5,4},{6,7},{7,6},{8,9},{9,8},{10,11... | collective-permute-start | bytes 147464 | tf_op jit(solution)/shard_map/ppermute | solution.py:483
  108.4 2.6 %collective-permute-start.15 = (bf16[32,768]{1,0:T(8,128)(2,1)S(1)}, bf16[32,768]{1,0:T(8,128)(2,1)S(1)}, u32[]{:S(2)}, u32[]{:S(2)}) collective-permute-start(bf16[32,768]{1,0:T(8,128)(2,1)S(1)} %get-tuple-element.80), channel_id=1, source_target_pairs={{0,2},{1,3},{2,0},{3,1},{4,6},{5,7},{6,4},{7,5},{8,10},{9,11},{10,... | collective-permute-start | bytes 147464 | tf_op jit(solution)/shard_map/ppermute | solution.py:483
  111.0 0.2 collective-permute-start.16
  111.2 3.3 %collective-permute-done.15.refs_1_ = bf16[32,768]{1,0:T(8,128)(2,1)S(1)} collective-permute-done((bf16[32,768]{1,0:T(8,128)(2,1)S(1)}, bf16[32,768]{1,0:T(8,128)(2,1)S(1)}, u32[]{:S(2)}, u32[]{:S(2)}) %collective-permute-start.15) | collective-permute-done | bytes 49184 | tf_op jit(solution)/shard_map/ppermute | solution.py:483
  114.5 2.4 %collective-permute-done.16.refs_2_ = bf16[32,768]{1,0:T(8,128)(2,1)S(1)} collective-permute-done((bf16[32,768]{1,0:T(8,128)(2,1)S(1)}, bf16[32,768]{1,0:T(8,128)(2,1)S(1)}, u32[]{:S(2)}, u32[]{:S(2)}) %collective-permute-start.16) | collective-permute-done | bytes 49184 | tf_op jit(solution)/shard_map/ppermute | solution.py:483
  116.9 1.3 collective-permute-start.19
  118.3 3.1 %collective-permute-start.17 = (bf16[32,768]{1,0:T(8,128)(2,1)S(1)}, bf16[32,768]{1,0:T(8,128)(2,1)S(1)}, u32[]{:S(2)}, u32[]{:S(2)}) collective-permute-start(bf16[32,768]{1,0:T(8,128)(2,1)S(1)} %line_sum.1.refs_0_), channel_id=1, source_target_pairs={{0,1},{1,0},{2,3},{3,2},{4,5},{5,4},{6,7},{7,6},{8,9},{9,8},{10,11... | collective-permute-start | bytes 147464 | tf_op jit(solution)/shard_map/ppermute | solution.py:487
  121.4 1.5 %collective-permute-done.19.refs_3_ = bf16[32,768]{1,0:T(8,128)(2,1)S(1)} collective-permute-done((bf16[32,768]{1,0:T(8,128)(2,1)S(1)}, bf16[32,768]{1,0:T(8,128)(2,1)S(1)}, u32[]{:S(2)}, u32[]{:S(2)}) %collective-permute-start.19) | collective-permute-done | bytes 49184 | tf_op jit(solution)/shard_map/ppermute | solution.py:487
  122.9 1.1 collective-permute-done.18.refs_2_
  124.0 3.9 %collective-permute-start.24 = (bf16[4,32,768]{2,1,0:T(8,128)(2,1)S(1)}, bf16[4,32,768]{2,1,0:T(8,128)(2,1)S(1)}, u32[]{:S(2)}, u32[]{:S(2)}) collective-permute-start(bf16[4,32,768]{2,1,0:T(8,128)(2,1)S(1)} %line_place.1.refs_0_), channel_id=1, source_target_pairs={{0,24},{4,28},{8,16},{12,20},{16,8},{20,12},{24,0},{28,4},{1,25},{... | collective-permute-start | bytes 589832 | tf_op jit(solution)/shard_map/ppermute | solution.py:491
  127.9 3.6 %collective-permute-start.23 = (bf16[4,32,768]{2,1,0:T(8,128)(2,1)S(1)}, bf16[4,32,768]{2,1,0:T(8,128)(2,1)S(1)}, u32[]{:S(2)}, u32[]{:S(2)}) collective-permute-start(bf16[4,32,768]{2,1,0:T(8,128)(2,1)S(1)} %line_place.1.refs_0_), channel_id=1, source_target_pairs={{0,16},{4,20},{8,24},{12,28},{16,0},{20,4},{24,8},{28,12},{1,17},{... | collective-permute-start | bytes 589832 | tf_op jit(solution)/shard_map/ppermute | solution.py:491
  131.5 4.9 %temporal_forward.1 = bf16[8,8,64,256]{3,2,1,0:T(8,128)(2,1)} custom-call(s32[2]{0:T(128)S(1)} %copy-done.6, s32[2]{0:T(128)S(1)} %copy-done.7, bf16[8,512,256]{2,1,0:T(8,128)(2,1)S(1)} %get-tuple-element.82.act_ref.own, bf16[8,512,256]{2,1,0:T(8,128)(2,1)S(1)} %collective-permute-done.20.nxt, bf16[8,512,256]{2,1,0:T(8,128)(2,1)S(1)} %collective-permute-done.21.prv, ...), custom_call_target="tpu_custom_call" | custom-call | flops 1610612736 | bytes 10485760 | tf_op jit(solution)/shard_map/temporal_forward/pallas_call | solution.py:20
  136.4 1.0 collective-permute-done.22.refs_1_
  137.4 0.1 plane_place.1.mine_ref
  137.5 0.1 collective-permute-start.25
  137.5 2.3 %collective-permute-done.25.got_ref = bf16[4,4,32,768]{3,2,1,0:T(8,128)(2,1)S(1)} collective-permute-done((bf16[4,4,32,768]{3,2,1,0:T(8,128)(2,1)S(1)}, bf16[4,4,32,768]{3,2,1,0:T(8,128)(2,1)S(1)}, u32[]{:S(2)}, u32[]{:S(2)}) %collective-permute-start.25) | collective-permute-done | bytes 786464 | tf_op jit(solution)/shard_map/ppermute | solution.py:503
  139.8 1.9 %finish.1 = (f32[3,3,256,256]{3,2,1,0:T(8,128)}, f32[3,256,256]{2,1,0:T(8,128)}) custom-call(bf16[4,4,32,768]{3,2,1,0:T(8,128)(2,1)S(1)} %plane_place.1.mine_ref, bf16[4,4,32,768]{3,2,1,0:T(8,128)(2,1)S(1)} %collective-permute-done.25.got_ref), custom_call_target="tpu_custom_call" | custom-call | bytes 4194304 | tf_op jit(solution)/shard_map/finish/pallas_call | solution.py:20
  (28 shorter events, 0.1 us)
Async XLA Ops:
  0.6 21.5 %copy-start = (bf16[8,8,64,256]{3,2,1,0:T(8,128)(2,1)S(1)}, bf16[8,8,64,256]{3,2,1,0:T(8,128)(2,1)}, u32[]{:S(2)}) copy-start(bf16[8,8,64,256]{3,2,1,0:T(8,128)(2,1)} %x_ref.5) | copy-start | bytes 6291460
  0.6 42.8 %collective-permute-start.5 = (bf16[8,512,256]{2,1,0:T(8,128)(2,1)}, bf16[8,512,256]{2,1,0:T(8,128)(2,1)S(1)}, u32[]{:S(2)}, u32[]{:S(2)}) collective-permute-start(bf16[8,512,256]{2,1,0:T(8,128)(2,1)} %bitcast.4), channel_id=1, source_target_pairs={{4,0},{8,4},{12,8},{16,12},{20,16},{24,20},{28,24},{5,1},{9,5},{13... | collective-permute-start | bytes 6291464 | tf_op jit(solution)/shard_map/ppermute | solution.py:372
  2.1 41.4 %collective-permute-start.4 = (bf16[8,512,256]{2,1,0:T(8,128)(2,1)}, bf16[8,512,256]{2,1,0:T(8,128)(2,1)S(1)}, u32[]{:S(2)}, u32[]{:S(2)}) collective-permute-start(bf16[8,512,256]{2,1,0:T(8,128)(2,1)} %bitcast.5), channel_id=1, source_target_pairs={{0,4},{4,8},{8,12},{12,16},{16,20},{20,24},{24,28},{1,5},{5,9},{9,... | collective-permute-start | bytes 6291464 | tf_op jit(solution)/shard_map/ppermute | solution.py:372
  6.3 11.6 %collective-permute-start = (bf16[8,1,64,256]{3,2,1,0:T(8,128)(2,1)S(1)}, bf16[8,1,64,256]{3,2,1,0:T(8,128)(2,1)S(1)}, u32[]{:S(2)}, u32[]{:S(2)}) collective-permute-start(bf16[8,1,64,256]{3,2,1,0:T(8,128)(2,1)S(1)} %get-tuple-element.89), channel_id=1, source_target_pairs={{0,1},{1,2},{2,3},{4,5},{5,6},{6,7},{8,9},{9,10},{10,11},{12,13},{... | collective-permute-start | bytes 786440 | tf_op jit(solution)/shard_map/ppermute | solution.py:372
  11.3 10.8 %collective-permute-start.1 = (bf16[8,1,64,256]{3,2,1,0:T(8,128)(2,1)S(1)}, bf16[8,1,64,256]{3,2,1,0:T(8,128)(2,1)S(1)}, u32[]{:S(2)}, u32[]{:S(2)}) collective-permute-start(bf16[8,1,64,256]{3,2,1,0:T(8,128)(2,1)S(1)} %get-tuple-element.88), channel_id=1, source_target_pairs={{1,0},{2,1},{3,2},{5,4},{6,5},{7,6},{9,8},{10,9},{11,10},{13,12},{... | collective-permute-start | bytes 786440 | tf_op jit(solution)/shard_map/ppermute | solution.py:372
  12.6 1.0 copy-start.2
  13.6 1.3 copy-start.4
  22.1 1.3 copy-start.5
  29.0 3.8 %collective-permute-start.2 = (f32[8,2,256]{2,1,0:T(2,128)S(1)}, f32[8,2,256]{2,1,0:T(2,128)S(1)}, u32[]{:S(2)}, u32[]{:S(2)}) collective-permute-start(f32[8,2,256]{2,1,0:T(2,128)S(1)} %get-tuple-element.49), channel_id=1, source_target_pairs={{0,1},{1,0},{2,3},{3,2},{4,5},{5,4},{6,7},{7,6},{8,9},{9,8},{10,11... | collective-permute-start | bytes 49160 | tf_op jit(solution)/shard_map/ppermute | solution.py:381
  32.8 4.9 %copy-start.6 = (s32[2]{0:T(128)S(1)}, s32[2]{0:T(128)}, u32[]{:S(2)}) copy-start(s32[2]{0:T(128)} %clip_ref.5) | copy-start | bytes 28
  32.8 4.9 %copy-start.8 = (f32[256]{0:T(256)S(1)}, f32[256]{0:T(256)}, u32[]{:S(2)}) copy-start(f32[256]{0:T(256)} %param.12) | copy-start | bytes 3076
  32.8 4.9 %copy-start.9 = (f32[256]{0:T(256)S(1)}, f32[256]{0:T(256)}, u32[]{:S(2)}) copy-start(f32[256]{0:T(256)} %param.13) | copy-start | bytes 3076
  32.9 4.8 %collective-permute-start.3 = (f32[8,2,256]{2,1,0:T(2,128)S(1)}, f32[8,2,256]{2,1,0:T(2,128)S(1)}, u32[]{:S(2)}, u32[]{:S(2)}) collective-permute-start(f32[8,2,256]{2,1,0:T(2,128)S(1)} %add.6.refs_0_), channel_id=1, source_target_pairs={{0,2},{1,3},{2,0},{3,1},{4,6},{5,7},{6,4},{7,5},{8,10},{9,11},{10,... | collective-permute-start | bytes 49160 | tf_op jit(solution)/shard_map/ppermute | solution.py:381
  37.7 14.0 %copy-start.1 = (bf16[8,8,64,256]{3,2,1,0:T(8,128)(2,1)S(1)}, bf16[8,8,64,256]{3,2,1,0:T(8,128)(2,1)}, u32[]{:S(2)}) copy-start(bf16[8,8,64,256]{3,2,1,0:T(8,128)(2,1)} %cot_ref.1) | copy-start | bytes 6291460
  37.7 14.0 %copy-start.7 = (s32[2]{0:T(128)S(1)}, s32[2]{0:T(128)}, u32[]{:S(2)}) copy-start(s32[2]{0:T(128)} %dil_ref.3) | copy-start | bytes 28
  43.5 88.0 %collective-permute-start.21 = (bf16[8,512,256]{2,1,0:T(8,128)(2,1)S(1)}, bf16[8,512,256]{2,1,0:T(8,128)(2,1)S(1)}, u32[]{:S(2)}, u32[]{:S(2)}) collective-permute-start(bf16[8,512,256]{2,1,0:T(8,128)(2,1)S(1)} %get-tuple-element.82.act_ref.own), channel_id=1, source_target_pairs={{0,4},{4,8},{8,12},{12,16},{16,20},{20,24},{24,28},{1,5},{5,9},{9,... | collective-permute-start | bytes 6291464 | tf_op jit(solution)/shard_map/ppermute | solution.py:372
  50.4 81.0 %collective-permute-start.20 = (bf16[8,512,256]{2,1,0:T(8,128)(2,1)S(1)}, bf16[8,512,256]{2,1,0:T(8,128)(2,1)S(1)}, u32[]{:S(2)}, u32[]{:S(2)}) collective-permute-start(bf16[8,512,256]{2,1,0:T(8,128)(2,1)S(1)} %get-tuple-element.82.act_ref.own), channel_id=1, source_target_pairs={{4,0},{8,4},{12,8},{16,12},{20,16},{24,20},{28,24},{5,1},{9,5},{13... | collective-permute-start | bytes 6291464 | tf_op jit(solution)/shard_map/ppermute | solution.py:372
  55.6 3.8 %collective-permute-start.6 = (f32[8,2,256]{2,1,0:T(2,128)S(1)}, f32[8,2,256]{2,1,0:T(2,128)S(1)}, u32[]{:S(2)}, u32[]{:S(2)}) collective-permute-start(f32[8,2,256]{2,1,0:T(2,128)S(1)} %get-tuple-element.61), channel_id=1, source_target_pairs={{0,1},{1,0},{2,3},{3,2},{4,5},{5,4},{6,7},{7,6},{8,9},{9,8},{10,11... | collective-permute-start | bytes 49160 | tf_op jit(solution)/shard_map/ppermute | solution.py:381
  59.5 4.7 %collective-permute-start.7 = (f32[8,2,256]{2,1,0:T(2,128)S(1)}, f32[8,2,256]{2,1,0:T(2,128)S(1)}, u32[]{:S(2)}, u32[]{:S(2)}) collective-permute-start(f32[8,2,256]{2,1,0:T(2,128)S(1)} %add.7.refs_2_), channel_id=1, source_target_pairs={{0,2},{1,3},{2,0},{3,1},{4,6},{5,7},{6,4},{7,5},{8,10},{9,11},{10,... | collective-permute-start | bytes 49160 | tf_op jit(solution)/shard_map/ppermute | solution.py:381
  68.8 8.9 %collective-permute-start.8 = (bf16[8,1,64,256]{3,2,1,0:T(8,128)(2,1)S(1)}, bf16[8,1,64,256]{3,2,1,0:T(8,128)(2,1)S(1)}, u32[]{:S(2)}, u32[]{:S(2)}) collective-permute-start(bf16[8,1,64,256]{3,2,1,0:T(8,128)(2,1)S(1)} %get-tuple-element.63), channel_id=1, source_target_pairs={{0,1},{1,2},{2,3},{4,5},{5,6},{6,7},{8,9},{9,10},{10,11},{12,13},{... | collective-permute-start | bytes 786440 | tf_op jit(solution)/shard_map/ppermute | solution.py:372
  72.3 9.5 %collective-permute-start.9 = (bf16[8,1,64,256]{3,2,1,0:T(8,128)(2,1)S(1)}, bf16[8,1,64,256]{3,2,1,0:T(8,128)(2,1)S(1)}, u32[]{:S(2)}, u32[]{:S(2)}) collective-permute-start(bf16[8,1,64,256]{3,2,1,0:T(8,128)(2,1)S(1)} %get-tuple-element.64), channel_id=1, source_target_pairs={{1,0},{2,1},{3,2},{5,4},{6,5},{7,6},{9,8},{10,9},{11,10},{13,12},{... | collective-permute-start | bytes 786440 | tf_op jit(solution)/shard_map/ppermute | solution.py:372
  84.0 2.4 %collective-permute-start.10 = (bf16[4,4,32,768]{3,2,1,0:T(8,128)(2,1)S(1)}, bf16[4,4,32,768]{3,2,1,0:T(8,128)(2,1)S(1)}, u32[]{:S(2)}, u32[]{:S(2)}) collective-permute-start(bf16[4,4,32,768]{3,2,1,0:T(8,128)(2,1)S(1)} %get-tuple-element.68), channel_id=1, source_target_pairs={{0,4},{4,0},{8,12},{12,8},{16,20},{20,16},{24,28},{28,24},{1,5},{5... | collective-permute-start | bytes 2359304 | tf_op jit(solution)/shard_map/ppermute | solution.py:466
  86.5 20.2 %collective-permute-start.11 = (bf16[4,32,768]{2,1,0:T(8,128)(2,1)S(1)}, bf16[4,32,768]{2,1,0:T(8,128)(2,1)S(1)}, u32[]{:S(2)}, u32[]{:S(2)}) collective-permute-start(bf16[4,32,768]{2,1,0:T(8,128)(2,1)S(1)} %get-tuple-element.75), channel_id=1, source_target_pairs={{0,8},{4,12},{8,0},{12,4},{16,24},{20,28},{24,16},{28,20},{1,9},{5... | collective-permute-start | bytes 589832 | tf_op jit(solution)/shard_map/ppermute | solution.py:471
  92.4 14.2 %collective-permute-start.12 = (bf16[4,32,768]{2,1,0:T(8,128)(2,1)S(1)}, bf16[4,32,768]{2,1,0:T(8,128)(2,1)S(1)}, u32[]{:S(2)}, u32[]{:S(2)}) collective-permute-start(bf16[4,32,768]{2,1,0:T(8,128)(2,1)S(1)} %get-tuple-element.76), channel_id=1, source_target_pairs={{0,16},{4,20},{8,24},{12,28},{16,0},{20,4},{24,8},{28,12},{1,17},{... | collective-permute-start | bytes 589832 | tf_op jit(solution)/shard_map/ppermute | solution.py:471
  94.4 12.3 %collective-permute-start.13 = (bf16[4,32,768]{2,1,0:T(8,128)(2,1)S(1)}, bf16[4,32,768]{2,1,0:T(8,128)(2,1)S(1)}, u32[]{:S(2)}, u32[]{:S(2)}) collective-permute-start(bf16[4,32,768]{2,1,0:T(8,128)(2,1)S(1)} %get-tuple-element.77), channel_id=1, source_target_pairs={{0,24},{4,28},{8,16},{12,20},{16,8},{20,12},{24,0},{28,4},{1,25},{... | collective-permute-start | bytes 589832 | tf_op jit(solution)/shard_map/ppermute | solution.py:471
  95.3 36.1 %copy-start.3 = (bf16[3,256,256]{2,1,0:T(8,128)(2,1)S(1)}, bf16[3,256,256]{2,1,0:T(8,128)(2,1)}, u32[]{:S(2)}) copy-start(bf16[3,256,256]{2,1,0:T(8,128)(2,1)} %temporal_ref.1) | copy-start | bytes 1179652
  106.8 4.5 %collective-permute-start.14 = (bf16[32,768]{1,0:T(8,128)(2,1)S(1)}, bf16[32,768]{1,0:T(8,128)(2,1)S(1)}, u32[]{:S(2)}, u32[]{:S(2)}) collective-permute-start(bf16[32,768]{1,0:T(8,128)(2,1)S(1)} %get-tuple-element.79), channel_id=1, source_target_pairs={{0,1},{1,0},{2,3},{3,2},{4,5},{5,4},{6,7},{7,6},{8,9},{9,8},{10,11... | collective-permute-start | bytes 147464 | tf_op jit(solution)/shard_map/ppermute | solution.py:483
  108.4 6.1 %collective-permute-start.15 = (bf16[32,768]{1,0:T(8,128)(2,1)S(1)}, bf16[32,768]{1,0:T(8,128)(2,1)S(1)}, u32[]{:S(2)}, u32[]{:S(2)}) collective-permute-start(bf16[32,768]{1,0:T(8,128)(2,1)S(1)} %get-tuple-element.80), channel_id=1, source_target_pairs={{0,2},{1,3},{2,0},{3,1},{4,6},{5,7},{6,4},{7,5},{8,10},{9,11},{10,... | collective-permute-start | bytes 147464 | tf_op jit(solution)/shard_map/ppermute | solution.py:483
  111.0 5.9 %collective-permute-start.16 = (bf16[32,768]{1,0:T(8,128)(2,1)S(1)}, bf16[32,768]{1,0:T(8,128)(2,1)S(1)}, u32[]{:S(2)}, u32[]{:S(2)}) collective-permute-start(bf16[32,768]{1,0:T(8,128)(2,1)S(1)} %get-tuple-element.81), channel_id=1, source_target_pairs={{0,3},{1,2},{2,1},{3,0},{4,7},{5,6},{6,5},{7,4},{8,11},{9,10},{10,... | collective-permute-start | bytes 147464 | tf_op jit(solution)/shard_map/ppermute | solution.py:483
  116.9 6.0 %collective-permute-start.19 = (bf16[32,768]{1,0:T(8,128)(2,1)S(1)}, bf16[32,768]{1,0:T(8,128)(2,1)S(1)}, u32[]{:S(2)}, u32[]{:S(2)}) collective-permute-start(bf16[32,768]{1,0:T(8,128)(2,1)S(1)} %line_sum.1.refs_0_), channel_id=1, source_target_pairs={{0,3},{1,2},{2,1},{3,0},{4,7},{5,6},{6,5},{7,4},{8,11},{9,10},{10,... | collective-permute-start | bytes 147464 | tf_op jit(solution)/shard_map/ppermute | solution.py:487
  118.3 5.7 %collective-permute-start.18 = (bf16[32,768]{1,0:T(8,128)(2,1)S(1)}, bf16[32,768]{1,0:T(8,128)(2,1)S(1)}, u32[]{:S(2)}, u32[]{:S(2)}) collective-permute-start(bf16[32,768]{1,0:T(8,128)(2,1)S(1)} %line_sum.1.refs_0_), channel_id=1, source_target_pairs={{0,2},{1,3},{2,0},{3,1},{4,6},{5,7},{6,4},{7,5},{8,10},{9,11},{10,... | collective-permute-start | bytes 147464 | tf_op jit(solution)/shard_map/ppermute | solution.py:487
  118.3 5.7 %collective-permute-start.17 = (bf16[32,768]{1,0:T(8,128)(2,1)S(1)}, bf16[32,768]{1,0:T(8,128)(2,1)S(1)}, u32[]{:S(2)}, u32[]{:S(2)}) collective-permute-start(bf16[32,768]{1,0:T(8,128)(2,1)S(1)} %line_sum.1.refs_0_), channel_id=1, source_target_pairs={{0,1},{1,0},{2,3},{3,2},{4,5},{5,4},{6,7},{7,6},{8,9},{9,8},{10,11... | collective-permute-start | bytes 147464 | tf_op jit(solution)/shard_map/ppermute | solution.py:487
  124.0 12.4 %collective-permute-start.24 = (bf16[4,32,768]{2,1,0:T(8,128)(2,1)S(1)}, bf16[4,32,768]{2,1,0:T(8,128)(2,1)S(1)}, u32[]{:S(2)}, u32[]{:S(2)}) collective-permute-start(bf16[4,32,768]{2,1,0:T(8,128)(2,1)S(1)} %line_place.1.refs_0_), channel_id=1, source_target_pairs={{0,24},{4,28},{8,16},{12,20},{16,8},{20,12},{24,0},{28,4},{1,25},{... | collective-permute-start | bytes 589832 | tf_op jit(solution)/shard_map/ppermute | solution.py:491
  127.9 8.5 %collective-permute-start.23 = (bf16[4,32,768]{2,1,0:T(8,128)(2,1)S(1)}, bf16[4,32,768]{2,1,0:T(8,128)(2,1)S(1)}, u32[]{:S(2)}, u32[]{:S(2)}) collective-permute-start(bf16[4,32,768]{2,1,0:T(8,128)(2,1)S(1)} %line_place.1.refs_0_), channel_id=1, source_target_pairs={{0,16},{4,20},{8,24},{12,28},{16,0},{20,4},{24,8},{28,12},{1,17},{... | collective-permute-start | bytes 589832 | tf_op jit(solution)/shard_map/ppermute | solution.py:491
  131.4 6.0 %collective-permute-start.22 = (bf16[4,32,768]{2,1,0:T(8,128)(2,1)S(1)}, bf16[4,32,768]{2,1,0:T(8,128)(2,1)S(1)}, u32[]{:S(2)}, u32[]{:S(2)}) collective-permute-start(bf16[4,32,768]{2,1,0:T(8,128)(2,1)S(1)} %line_place.1.refs_0_), channel_id=1, source_target_pairs={{0,8},{4,12},{8,0},{12,4},{16,24},{20,28},{24,16},{28,20},{1,9},{5... | collective-permute-start | bytes 589832 | tf_op jit(solution)/shard_map/ppermute | solution.py:491
  137.5 2.4 %collective-permute-start.25 = (bf16[4,4,32,768]{3,2,1,0:T(8,128)(2,1)S(1)}, bf16[4,4,32,768]{3,2,1,0:T(8,128)(2,1)S(1)}, u32[]{:S(2)}, u32[]{:S(2)}) collective-permute-start(bf16[4,4,32,768]{3,2,1,0:T(8,128)(2,1)S(1)} %plane_place.1.mine_ref), channel_id=1, source_target_pairs={{0,4},{4,0},{8,12},{12,8},{16,20},{20,16},{24,28},{28,24},{1,5},{5... | collective-permute-start | bytes 2359304 | tf_op jit(solution)/shard_map/ppermute | solution.py:503

commit v2 on v1

--- a/solution.py
+++ b/solution.py
@@ -156,9 +156,12 @@
 
 
 def act_kernel(n, entries, group_size, clip_ref, *refs):
-    parts, (conv_ref, gain_ref, shift_ref, act_ref, normed_ref, slope_ref) = refs[:n], refs[n:]
-    frames = conv_ref.shape[0]
+    parts, refs = refs[:n], refs[n:]
+    conv_ref, gain_ref, shift_ref, act_ref, normed_ref, slope_ref, first_ref, last_ref = refs
+    frames, pixels, _ = conv_ref.shape
+    width = first_ref.shape[2]
     first = lax.axis_index("tm") * frames
+    top, bottom = slice(0, width), slice(pixels - width, pixels)
     filled = clip_ref[0] + clip_ref[1]
     half_gain, half_shift = 0.5 * gain_ref[...], 0.5 * shift_ref[...]
 
@@ -169,8 +172,11 @@
         t = jnp.tanh(h)
         rise = 1.0 + t
         act_ref[f] = jnp.where(first + f < filled, h * rise, 0.0).astype(BF16)
-        normed_ref[f] = normed.astype(BF16)
-        slope_ref[f] = (rise * (1.0 + h * (1.0 - t)) * half_gain).astype(BF16)
+        for k, (ref, value) in enumerate(((normed_ref, normed), (slope_ref, rise * (1.0 + h * (1.0 - t)) * half_gain))):
+            value = value.astype(BF16)
+            ref[f] = value
+            first_ref[f, k] = value[top]
+            last_ref[f, k] = value[bottom]
 
     loop(frames, body)
 
@@ -200,9 +206,10 @@
 
 
 def grad_act_kernel(
-    clip_ref, dil_ref, own, nxt, prv, tw_ref, normed_ref, slope_ref, ga_ref, cat_ref, sums_ref
+    clip_ref, dil_ref, own, nxt, prv, tw_ref, normed_ref, slope_ref, ga_ref, first_ref, last_ref, cat_ref, sums_ref
 ):
     frames, pixels, _ = own.shape
+    width = first_ref.shape[1]
 
     def body(pair):
         rows = pl.ds(pl.multiple_of(2 * pair * pixels, 2 * pixels), 2 * pixels)
@@ -214,6 +221,8 @@
             f = 2 * pair + b
             one = grad_act[b * pixels : (b + 1) * pixels]
             ga_ref[f] = one
+            first_ref[f] = one[:width]
+            last_ref[f] = one[pixels - width :]
             gn = one.astype(F32) * slope_ref[f].astype(F32)
             sums_ref[f] = column_sums(gn, gn * normed_ref[f].astype(F32))
 
@@ -225,21 +234,22 @@
     out_ref[...] = dot_rows(act_ref[...].reshape(frames * pixels, channels), cat_ref[...])
 
 
-def norm_back_kernel(n, m, entries, group_size, normed_ref, slope_ref, ga_ref, *refs):
+def norm_back(inv, means, normed, slope, grad_act):
+    gn = grad_act.astype(F32) * slope.astype(F32)
+    return inv * (gn - means[0:1] - normed.astype(F32) * means[1:2])
+
+
+def norm_back_kernel(width, n, m, entries, group_size, normed_ref, slope_ref, ga_ref, *refs):
     parts, grad_parts = refs[:n], refs[n : n + m]
-    g_ref, first_ref, last_ref, moved_ref = refs[n + m :]
+    g_ref, moved_ref = refs[n + m :]
     _, pixels, channels = normed_ref.shape
-    width = first_ref.shape[2]
 
     def body(f):
         _, inv = mean_and_inv(parts, f, entries, group_size)
         means = frame_stats(grad_parts, f, entries, group_size)
-        gn = ga_ref[f].astype(F32) * slope_ref[f].astype(F32)
-        wide = inv * (gn - means[0:1] - normed_ref[f].astype(F32) * means[1:2])
+        wide = norm_back(inv, means, normed_ref[f], slope_ref[f], ga_ref[f])
         grad = wide.astype(BF16)
         g_ref[f] = grad
-        first_ref[f, 0] = grad[:width]
-        last_ref[f, 0] = grad[pixels - width :]
         here = pl.ds(pl.multiple_of(f * pixels, pixels), pixels)
         moved_ref[here, :channels] = from_right(wide, width).astype(BF16)
         moved_ref[here, channels : 2 * channels] = grad
@@ -274,14 +284,23 @@
     pl.when(core == 1)(functools.partial(hand_out, half, 0))
 
 
-def conv_back_kernel(g_ref, above_ref, below_ref, cot_ref, w_ref, out_ref, lhs_ref):
+def conv_back_kernel(n, m, entries, group_size, g_ref, near_above, near_below, ga_above, ga_below, cot_ref, w_ref, *refs):
+    parts, grad_parts = refs[:n], refs[n : n + m]
+    out_ref, lhs_ref = refs[n + m :]
     frames, rows, width, channels = cot_ref.shape
     pixels = rows * width
+    place, size = lax.axis_index("space"), lax.axis_size("space")
 
     def body(pair):
         for b in range(2):
             f = 2 * pair + b
-            put_windows(above_ref[f, 0], g_ref[f], below_ref[f, 0], lhs_ref, b * pixels, (2, 1, 0))
+            _, inv = mean_and_inv(parts, f, entries, group_size)
+            means = frame_stats(grad_parts, f, entries, group_size)
+            above = norm_back(inv, means, near_above[f, 0], near_above[f, 1], ga_above[f])
+            below = norm_back(inv, means, near_below[f, 0], near_below[f, 1], ga_below[f])
+            above = jnp.where(place > 0, above, 0.0).astype(BF16)
+            below = jnp.where(place < size - 1, below, 0.0).astype(BF16)
+            put_windows(above, g_ref[f], below, lhs_ref, b * pixels, (2, 1, 0))
         lhs = lhs_ref[...]
         z = [dot(lhs, w_ref[j]) for j in range(3)]
         out = z[1] + from_right(z[0], width) + from_left(z[2], width)
@@ -416,39 +435,45 @@
         0, 8 * big, [pltpu.VMEM((pixels, 3 * channels), BF16)],
     )
     x_turned, *parts = lax.optimization_barrier((x_turned, *parts))
-    act, normed, slope = call(
+    edge = shape((frames, 2, width, channels), BF16)
+    act, normed, slope, near_first, near_last = call(
         functools.partial(act_kernel, len(parts), entries, group_size), "activation",
         [clip_frames, *parts, conv_out, gain, shift],
-        [shape(per_px, BF16)] * 3, 10 * big, 10 * big,
-    )
-    act_sent, cot_prev, cot_next = lax.optimization_barrier((act, cot_prev, cot_next))
-    act_prev, act_next = neighbours("tm", act_sent, act_sent)
-
-    grad_act, cot_cat, grad_sums = call(
+        [shape(per_px, BF16)] * 3 + [edge] * 2, 10 * big, 10 * big,
+    )
+    near_above, near_below = neighbours("space", near_first, near_last)
+
+    edge = shape((frames, width, channels), BF16)
+    grad_act, ga_first, ga_last, cot_cat, grad_sums = call(
         grad_act_kernel, "grad_activation",
         [clip_frames, dilation, cot, cot_next, cot_prev, back_taps, normed, slope],
-        [shape(per_px, BF16), shape((frames * pixels, 3 * channels), BF16), shape((frames, 2, channels), F32)],
+        [
+            shape(per_px, BF16), edge, edge, shape((frames * pixels, 3 * channels), BF16),
+            shape((frames, 2, channels), F32),
+        ],
         6 * big * channels, 16 * big,
     )
+    ga_above, ga_below = neighbours("space", ga_first, ga_last)
     grad_parts = spread_sums(grad_sums, "space")
+    grad_parts[0], act_sent = lax.optimization_barrier((grad_parts[0], act))
+    act_prev, act_next = neighbours("tm", act_sent, act_sent)
     temporal_part = call(
         temporal_grad_kernel, "temporal_grad", [act, cot_cat],
         shape((channels, 3 * channels), F32), 6 * big * channels, 8 * big,
     )
+    grad_parts[0], near_above, near_below = lax.optimization_barrier((grad_parts[0], near_above, near_below))
     lanes = 3 * channels
-    grad_conv, first_rows, last_rows, moved = call(
-        functools.partial(norm_back_kernel, len(parts), len(grad_parts), entries, group_size), "norm_backward",
+    grad_conv, moved = call(
+        functools.partial(norm_back_kernel, width, len(parts), len(grad_parts), entries, group_size), "norm_backward",
         [normed, slope, grad_act, *parts, *grad_parts],
-        [shape(per_px, BF16)] + [shape((frames, 1, width, channels), BF16)] * 2
-        + [shape((frames * pixels, lanes), BF16)],
+        [shape(per_px, BF16), shape((frames * pixels, lanes), BF16)],
         0, 12 * big,
     )
-    grad_above, grad_below = neighbours("space", first_rows, last_rows)
     part = call(
         weight_part_kernel, "weight_part", [x_turned, moved], shape((lanes, 2 * channels), F32),
         12 * big * channels, 8 * big,
     )
-    moved, grad_above, grad_below = lax.optimization_barrier((moved, grad_above, grad_below))
+    moved, ga_above, ga_below = lax.optimization_barrier((moved, ga_above, ga_below))
     block = 2 * channels // (chips * n)
     send, keep = call(
         weight_grad_kernel, "weight_grad", [x_turned, moved, part, temporal_part],
@@ -471,7 +496,8 @@
     gots = [lax.ppermute(x, "tm", other_chip(s)) for s, x in enumerate(sends, 1)]
 
     in_grad = call(
-        conv_back_kernel, "conv_backward", [grad_conv, grad_above, grad_below, cotangent, back_weights],
+        functools.partial(conv_back_kernel, len(parts), len(grad_parts), entries, group_size), "conv_backward",
+        [grad_conv, near_above, near_below, ga_above, ga_below, cotangent, back_weights, *parts, *grad_parts],
         shape(frames_in.shape, BF16), 18 * big * channels, 8 * big, [windows], 20,
     )
     own, in_grad = lax.optimization_barrier((own, in_grad))

time: 142 us -> 149 us (1.049)
  waiting for transfers between devices: 34.3 us -> 47.9 us
  starting transfers between devices: 57.7 us -> 50.2 us
    ppermute x3, waiting for transfers between devices: 4.4 us -> 17.8 us  [per_device(): lax.ppermute(x, 'tm', other_chip(s))]
    ppermute x3, starting transfers between devices: 8.83 us -> 3.85 us  [per_device(): lax.ppermute(x, 'tm', other_chip(s))]
    ppermute x4, waiting for transfers between devices: 4.52 us -> 8.89 us  [spread_sums(): got = lax.ppermute(part, axis, [(i, i ^ step) for i in range(size)])]
    ppermute x8 -> x10, waiting for transfers between devices: 11.6 us -> 7.58 us  [neighbours(): return (lax.ppermute(high, axis, up), lax.ppermute(low, axis, down))]
    ppermute x3, starting transfers between devices: 7.44 us -> 4.89 us  [per_device(): gots = [lax.ppermute(own, 'tm', other_chip(s)) for s in range(1, chips)]]
    ppermute x8 -> x10, starting transfers between devices: 23.8 us -> 22.8 us  [neighbours(): return (lax.ppermute(high, axis, up), lax.ppermute(low, axis, down))]
  transfers between devices with their start and end apart: 26 -> 28, of which waited for: 15 -> 14; matrix products, arithmetic and copies ran while one was open for 1% -> 1% of each run, Pallas kernels for 30% -> 29%
where the time goes in v2:
time: 149 us
  starting transfers between devices  50.2 us (34%)
  waiting for transfers between devices  47.9 us (32%)
  Pallas kernels  44.7 us (30%)
  local copies, waits for them, and re-layouts  4.65 us (3%)
    pallas_call x17, Pallas kernels, call(): pl.pallas_call(kernel, in_specs=[smem if x.dtype == jnp.int32 else vmem f...  44.7 us
    ppermute x10, starting transfers between devices, neighbours(): return (lax.ppermute(high, axis, up), lax.ppermute(low, axis, down))  22.8 us
    ppermute x3, waiting for transfers between devices, per_device(): lax.ppermute(x, 'tm', other_chip(s))  17.8 us
    ppermute x4, starting transfers between devices, spread_sums(): got = lax.ppermute(part, axis, [(i, i ^ step) for i in range(size)])  9.63 us
    ppermute x4, waiting for transfers between devices, spread_sums(): got = lax.ppermute(part, axis, [(i, i ^ step) for i in range(size)])  8.89 us
    ppermute x10, waiting for transfers between devices, neighbours(): return (lax.ppermute(high, axis, up), lax.ppermute(low, axis, down))  7.58 us
    ppermute x3, waiting for transfers between devices, per_device(): lax.ppermute(x, 'space', other_plane(s))  5.67 us
    ppermute x3, starting transfers between devices, per_device(): gots = [lax.ppermute(own, 'tm', other_chip(s)) for s in range(1, chips)]  4.89 us
  transfers between devices with their start and end apart: 28, of which 14 were waited for; matrix products, arithmetic and copies ran while one was open for 1% of the time, Pallas kernels for 29%

profile of v2, /device:TPU:0, one launch (start us, length us, event | category | flops | bytes accessed | tf_op | source)
XLA Modules:
  0.0 148.5 jit_solution(14947404037981164523)
XLA Ops:
  0.6 2.6 %collective-permute-start.5 = (bf16[8,512,256]{2,1,0:T(8,128)(2,1)}, bf16[8,512,256]{2,1,0:T(8,128)(2,1)S(1)}, u32[]{:S(2)}, u32[]{:S(2)}) collective-permute-start(bf16[8,512,256]{2,1,0:T(8,128)(2,1)} %bitcast.4), channel_id=1, source_target_pairs={{0,4},{4,8},{8,12},{12,16},{16,20},{20,24},{24,28},{1,5},{5,9},{9,... | collective-permute-start | bytes 6291464 | tf_op jit(solution)/shard_map/ppermute | solution.py:391
  3.3 1.3 collective-permute-start.4
  4.6 1.1 fusion
  5.7 4.3 %collective-permute-start = (bf16[8,1,64,256]{3,2,1,0:T(8,128)(2,1)S(1)}, bf16[8,1,64,256]{3,2,1,0:T(8,128)(2,1)S(1)}, u32[]{:S(2)}, u32[]{:S(2)}) collective-permute-start(bf16[8,1,64,256]{3,2,1,0:T(8,128)(2,1)S(1)} %get-tuple-element.97), channel_id=1, source_target_pairs={{0,1},{1,2},{2,3},{4,5},{5,6},{6,7},{8,9},{9,10},{10,11},{12,13},{... | collective-permute-start | bytes 786440 | tf_op jit(solution)/shard_map/ppermute | solution.py:391
  10.0 1.3 collective-permute-start.1
  11.3 0.0 copy-start.2
  11.3 1.0 copy-done.2
  12.3 1.3 copy-done.4
  13.6 0.5 turn_weights.1
  14.0 1.3 collective-permute-done.above_ref
  15.3 4.7 %collective-permute-done.1.below_ref = bf16[8,1,64,256]{3,2,1,0:T(8,128)(2,1)S(1)} collective-permute-done((bf16[8,1,64,256]{3,2,1,0:T(8,128)(2,1)S(1)}, bf16[8,1,64,256]{3,2,1,0:T(8,128)(2,1)S(1)}, u32[]{:S(2)}, u32[]{:S(2)}) %collective-permute-start.1) | collective-permute-done | bytes 262176 | tf_op jit(solution)/shard_map/ppermute | solution.py:391
  20.0 1.3 copy-done.5
  21.3 5.6 %conv_forward.1 = (f32[8,512,256]{2,1,0:T(8,128)S(1)}, f32[8,2,256]{2,1,0:T(2,128)S(1)}) custom-call(bf16[8,8,64,256]{3,2,1,0:T(8,128)(2,1)S(1)} %copy-done, bf16[8,1,64,256]{3,2,1,0:T(8,128)(2,1)S(1)} %collective-permute-done.above_ref, bf16[8,1,64,256]{3,2,1,0:T(8,128)(2,1)S(1)} %collective-permute-done.1.below_ref, bf16[3,3,256,256]{3,2,1,0:T(8,128)(2,1)S(1)} %copy-done.5), custom_call_target="tpu_custom_call" | custom-call | flops 4831838208 | bytes 8388608 | tf_op jit(solution)/shard_map/conv_forward/pallas_call | solution.py:20
  26.9 1.6 %collective-permute-start.2 = (f32[8,2,256]{2,1,0:T(2,128)S(1)}, f32[8,2,256]{2,1,0:T(2,128)S(1)}, u32[]{:S(2)}, u32[]{:S(2)}) collective-permute-start(f32[8,2,256]{2,1,0:T(2,128)S(1)} %get-tuple-element.53), channel_id=1, source_target_pairs={{0,1},{1,0},{2,3},{3,2},{4,5},{5,4},{6,7},{7,6},{8,9},{9,8},{10,11... | collective-permute-start | bytes 49160 | tf_op jit(solution)/shard_map/ppermute | solution.py:400
  28.6 2.2 %collective-permute-done.2 = f32[8,2,256]{2,1,0:T(2,128)S(1)} collective-permute-done((f32[8,2,256]{2,1,0:T(2,128)S(1)}, f32[8,2,256]{2,1,0:T(2,128)S(1)}, u32[]{:S(2)}, u32[]{:S(2)}) %collective-permute-start.2) | collective-permute-done | bytes 16416 | tf_op jit(solution)/shard_map/ppermute | solution.py:400
  30.8 0.0 copy-start.9
  30.8 2.6 %collective-permute-start.3 = (f32[8,2,256]{2,1,0:T(2,128)S(1)}, f32[8,2,256]{2,1,0:T(2,128)S(1)}, u32[]{:S(2)}, u32[]{:S(2)}) collective-permute-start(f32[8,2,256]{2,1,0:T(2,128)S(1)} %add.6.refs_0_), channel_id=1, source_target_pairs={{0,2},{1,3},{2,0},{3,1},{4,6},{5,7},{6,4},{7,5},{8,10},{9,11},{10,... | collective-permute-start | bytes 49160 | tf_op jit(solution)/shard_map/ppermute | solution.py:400
  33.5 2.2 %turned.1.xt_ref = bf16[768,4096]{1,0:T(8,128)(2,1)S(1)} custom-call(bf16[8,8,64,256]{3,2,1,0:T(8,128)(2,1)S(1)} %copy-done, bf16[8,1,64,256]{3,2,1,0:T(8,128)(2,1)S(1)} %collective-permute-done.above_ref, bf16[8,1,64,256]{3,2,1,0:T(8,128)(2,1)S(1)} %collective-permute-done.1.below_ref), custom_call_target="tpu_custom_call" | custom-call | bytes 8388608 | tf_op jit(solution)/shard_map/turned/pallas_call | solution.py:20
  35.7 0.1 collective-permute-done.3.refs_1_
  35.7 0.0 copy-start.1
  35.8 5.7 %activation.1 = (bf16[8,512,256]{2,1,0:T(8,128)(2,1)S(1)}, bf16[8,512,256]{2,1,0:T(8,128)(2,1)S(1)}, bf16[8,512,256]{2,1,0:T(8,128)(2,1)S(1)}, bf16[8,2,64,256]{...) custom-call(s32[2]{0:T(128)S(1)} %copy-done.6, f32[8,2,256]{2,1,0:T(2,128)S(1)} %add.6.refs_0_, ...), custom_call_target="tpu_custom_call" | custom-call | flops 10485760 | bytes 10485760 | tf_op jit(solution)/shard_map/activation/pallas_call | solution.py:20
  41.5 3.3 %collective-permute-start.7 = (bf16[8,2,64,256]{3,2,1,0:T(8,128)(2,1)S(1)}, bf16[8,2,64,256]{3,2,1,0:T(8,128)(2,1)S(1)}, u32[]{:S(2)}, u32[]{:S(2)}) collective-permute-start(bf16[8,2,64,256]{3,2,1,0:T(8,128)(2,1)S(1)} %get-tuple-element.65), channel_id=1, source_target_pairs={{0,1},{1,2},{2,3},{4,5},{5,6},{6,7},{8,9},{9,10},{10,11},{12,13},{... | collective-permute-start | bytes 1572872 | tf_op jit(solution)/shard_map/ppermute | solution.py:391
  44.8 1.3 collective-permute-start.8
  46.2 3.9 %grad_activation.1 = (bf16[8,512,256]{2,1,0:T(8,128)(2,1)S(1)}, bf16[8,64,256]{2,1,0:T(8,128)(2,1)S(1)}, bf16[8,64,256]{2,1,0:T(8,128)(2,1)S(1)}, bf16[4096,768]{1,0:T(8,128)(2,1)S(1)}, f32[8,2,256]{2,1,0:T(2,128)S(1)}) custom-call(s32[2]{0:T(128)S(1)} %copy-done.6, s32[2]{0:T(128)S(1)} %copy-done.7, bf16[8,512,256]{2,1,0:T(8,128)(2,1)S(1)} %bitcast.6, ...), custom_call_target="tpu_custom_call" | custom-call | flops 1610612736 | bytes 16777216 | tf_op jit(solution)/shard_map/grad_activation/pallas_call | solution.py:20
  50.1 2.7 %collective-permute-start.6 = (f32[8,2,256]{2,1,0:T(2,128)S(1)}, f32[8,2,256]{2,1,0:T(2,128)S(1)}, u32[]{:S(2)}, u32[]{:S(2)}) collective-permute-start(f32[8,2,256]{2,1,0:T(2,128)S(1)} %get-tuple-element.62), channel_id=1, source_target_pairs={{0,1},{1,0},{2,3},{3,2},{4,5},{5,4},{6,7},{7,6},{8,9},{9,8},{10,11... | collective-permute-start | bytes 49160 | tf_op jit(solution)/shard_map/ppermute | solution.py:400
  52.8 6.6 %collective-permute-done.6 = f32[8,2,256]{2,1,0:T(2,128)S(1)} collective-permute-done((f32[8,2,256]{2,1,0:T(2,128)S(1)}, f32[8,2,256]{2,1,0:T(2,128)S(1)}, u32[]{:S(2)}, u32[]{:S(2)}) %collective-permute-start.6) | collective-permute-done | bytes 16416 | tf_op jit(solution)/shard_map/ppermute | solution.py:400
  59.4 2.6 %collective-permute-start.23 = (bf16[8,512,256]{2,1,0:T(8,128)(2,1)S(1)}, bf16[8,512,256]{2,1,0:T(8,128)(2,1)S(1)}, u32[]{:S(2)}, u32[]{:S(2)}) collective-permute-start(bf16[8,512,256]{2,1,0:T(8,128)(2,1)S(1)} %get-tuple-element.90.act_ref.own), channel_id=1, source_target_pairs={{0,4},{4,8},{8,12},{12,16},{16,20},{20,24},{24,28},{1,5},{5,9},{9,... | collective-permute-start | bytes 6291464 | tf_op jit(solution)/shard_map/ppermute | solution.py:391
  62.0 1.3 collective-permute-start.22
  63.3 2.7 %collective-permute-start.9 = (f32[8,2,256]{2,1,0:T(2,128)S(1)}, f32[8,2,256]{2,1,0:T(2,128)S(1)}, u32[]{:S(2)}, u32[]{:S(2)}) collective-permute-start(f32[8,2,256]{2,1,0:T(2,128)S(1)} %add.7.refs_2_), channel_id=1, source_target_pairs={{0,2},{1,3},{2,0},{3,1},{4,6},{5,7},{6,4},{7,5},{8,10},{9,11},{10,... | collective-permute-start | bytes 49160 | tf_op jit(solution)/shard_map/ppermute | solution.py:400
  65.9 1.9 %temporal_grad.1.temporal_ref = f32[256,768]{1,0:T(8,128)S(1)} custom-call(bf16[8,512,256]{2,1,0:T(8,128)(2,1)S(1)} %get-tuple-element.90.act_ref.own, bf16[4096,768]{1,0:T(8,128)(2,1)S(1)} %get-tuple-element.72.cat_ref), custom_call_target="tpu_custom_call" | custom-call | flops 1610612736 | bytes 8388608 | tf_op jit(solution)/shard_map/temporal_grad/pallas_call | solution.py:20
  67.8 3.5 %collective-permute-start.10 = (bf16[8,64,256]{2,1,0:T(8,128)(2,1)S(1)}, bf16[8,64,256]{2,1,0:T(8,128)(2,1)S(1)}, u32[]{:S(2)}, u32[]{:S(2)}) collective-permute-start(bf16[8,64,256]{2,1,0:T(8,128)(2,1)S(1)} %get-tuple-element.69), channel_id=1, source_target_pairs={{0,1},{1,2},{2,3},{4,5},{5,6},{6,7},{8,9},{9,10},{10,11},{12,13},{... | collective-permute-start | bytes 786440 | tf_op jit(solution)/shard_map/ppermute | solution.py:391
  71.3 1.3 collective-permute-start.11
  72.6 4.6 %norm_backward.1 = (bf16[8,512,256]{2,1,0:T(8,128)(2,1)S(1)}, bf16[4096,768]{1,0:T(8,128)(2,1)S(1)}) custom-call(bf16[8,512,256]{2,1,0:T(8,128)(2,1)S(1)} %get-tuple-element.58.normed_ref, bf16[8,512,256]{2,1,0:T(8,128)(2,1)S(1)} %get-tuple-element.59.slope_ref, bf16[8,512,256]{2,1,0:T(8,128)(2,1)S(1)} %get-tuple-element.61.ga_ref, ...), custom_call_target="tpu_custom_call" | custom-call | bytes 12582912 | tf_op jit(solution)/shard_map/norm_backward/pallas_call | solution.py:20
  77.2 3.4 %weight_part.1.part_ref = f32[768,512]{1,0:T(8,128)S(1)} custom-call(bf16[768,4096]{1,0:T(8,128)(2,1)S(1)} %turned.1.xt_ref, bf16[4096,768]{1,0:T(8,128)(2,1)S(1)} %get-tuple-element.71.moved_ref), custom_call_target="tpu_custom_call" | custom-call | flops 3221225472 | bytes 8388608 | tf_op jit(solution)/shard_map/weight_part/pallas_call | solution.py:20
  80.6 1.5 %collective-permute-done.11.ga_below = bf16[8,64,256]{2,1,0:T(8,128)(2,1)S(1)} collective-permute-done((bf16[8,64,256]{2,1,0:T(8,128)(2,1)S(1)}, bf16[8,64,256]{2,1,0:T(8,128)(2,1)S(1)}, u32[]{:S(2)}, u32[]{:S(2)}) %collective-permute-start.11) | collective-permute-done | bytes 262176 | tf_op jit(solution)/shard_map/ppermute | solution.py:391
  82.2 2.2 %weight_grad.1 = (bf16[4,4,32,768]{3,2,1,0:T(8,128)(2,1)S(1)}, f32[4,4,32,768]{3,2,1,0:T(8,128)S(1)}) custom-call(bf16[768,4096]{1,0:T(8,128)(2,1)S(1)} %turned.1.xt_ref, bf16[4096,768]{1,0:T(8,128)(2,1)S(1)} %get-tuple-element.71.moved_ref, f32[768,512]{1,0:T(8,128)S(1)} %weight_part.1.part_ref, f32[256,768]{1,0:T(8,128)S(1)} %temporal_grad.1.temporal_ref), custom_call_target="tpu_custom_call" | custom-call | flops 1610612736 | bytes 8388608 | tf_op jit(solution)/shard_map/weight_grad/pallas_call | solution.py:20
  84.4 0.1 collective-permute-start.12
  84.5 2.3 %collective-permute-done.12.got_ref = bf16[4,4,32,768]{3,2,1,0:T(8,128)(2,1)S(1)} collective-permute-done((bf16[4,4,32,768]{3,2,1,0:T(8,128)(2,1)S(1)}, bf16[4,4,32,768]{3,2,1,0:T(8,128)(2,1)S(1)}, u32[]{:S(2)}, u32[]{:S(2)}) %collective-permute-start.12) | collective-permute-done | bytes 786464 | tf_op jit(solution)/shard_map/ppermute | solution.py:491
  86.8 0.1 core_sum.1
  86.9 1.6 %collective-permute-start.13 = (bf16[4,32,768]{2,1,0:T(8,128)(2,1)S(1)}, bf16[4,32,768]{2,1,0:T(8,128)(2,1)S(1)}, u32[]{:S(2)}, u32[]{:S(2)}) collective-permute-start(bf16[4,32,768]{2,1,0:T(8,128)(2,1)S(1)} %get-tuple-element.83), channel_id=1, source_target_pairs={{0,8},{4,12},{8,0},{12,4},{16,24},{20,28},{24,16},{28,20},{1,9},{5... | collective-permute-start | bytes 589832 | tf_op jit(solution)/shard_map/ppermute | solution.py:496
  88.4 0.9 collective-permute-start.14
  89.4 1.4 collective-permute-start.15
  90.7 7.7 %conv_backward.1 = bf16[8,8,64,256]{3,2,1,0:T(8,128)(2,1)} custom-call(bf16[8,512,256]{2,1,0:T(8,128)(2,1)S(1)} %get-tuple-element.76.g_ref, bf16[8,2,64,256]{3,2,1,0:T(8,128)(2,1)S(1)} %collective-permute-done.7.near_above, bf16[8,2,64,256]{3,2,1,0:T(8,128)(2,1)S(1)} %collective-permute-done.8.near_below, ...), custom_call_target="tpu_custom_call" | custom-call | flops 4831838208 | bytes 8388608 | tf_op jit(solution)/shard_map/conv_backward/pallas_call | solution.py:20
  98.4 17.8 %collective-permute-done.13.refs_0_ = bf16[4,32,768]{2,1,0:T(8,128)(2,1)S(1)} collective-permute-done((bf16[4,32,768]{2,1,0:T(8,128)(2,1)S(1)}, bf16[4,32,768]{2,1,0:T(8,128)(2,1)S(1)}, u32[]{:S(2)}, u32[]{:S(2)}) %collective-permute-start.13) | collective-permute-done | bytes 196640 | tf_op jit(solution)/shard_map/ppermute | solution.py:496
  116.2 0.1 plane_sum.1
  116.3 1.6 %collective-permute-start.16 = (bf16[32,768]{1,0:T(8,128)(2,1)S(1)}, bf16[32,768]{1,0:T(8,128)(2,1)S(1)}, u32[]{:S(2)}, u32[]{:S(2)}) collective-permute-start(bf16[32,768]{1,0:T(8,128)(2,1)S(1)} %get-tuple-element.87), channel_id=1, source_target_pairs={{0,1},{1,0},{2,3},{3,2},{4,5},{5,4},{6,7},{7,6},{8,9},{9,8},{10,11... | collective-permute-start | bytes 147464 | tf_op jit(solution)/shard_map/ppermute | solution.py:509
  118.0 2.6 %collective-permute-start.17 = (bf16[32,768]{1,0:T(8,128)(2,1)S(1)}, bf16[32,768]{1,0:T(8,128)(2,1)S(1)}, u32[]{:S(2)}, u32[]{:S(2)}) collective-permute-start(bf16[32,768]{1,0:T(8,128)(2,1)S(1)} %get-tuple-element.88), channel_id=1, source_target_pairs={{0,2},{1,3},{2,0},{3,1},{4,6},{5,7},{6,4},{7,5},{8,10},{9,11},{10,... | collective-permute-start | bytes 147464 | tf_op jit(solution)/shard_map/ppermute | solution.py:509
  120.5 0.2 collective-permute-start.18
  120.8 2.7 %collective-permute-done.17.refs_1_ = bf16[32,768]{1,0:T(8,128)(2,1)S(1)} collective-permute-done((bf16[32,768]{1,0:T(8,128)(2,1)S(1)}, bf16[32,768]{1,0:T(8,128)(2,1)S(1)}, u32[]{:S(2)}, u32[]{:S(2)}) %collective-permute-start.17) | collective-permute-done | bytes 49184 | tf_op jit(solution)/shard_map/ppermute | solution.py:509
  123.5 3.0 %collective-permute-done.18.refs_2_ = bf16[32,768]{1,0:T(8,128)(2,1)S(1)} collective-permute-done((bf16[32,768]{1,0:T(8,128)(2,1)S(1)}, bf16[32,768]{1,0:T(8,128)(2,1)S(1)}, u32[]{:S(2)}, u32[]{:S(2)}) %collective-permute-start.18) | collective-permute-done | bytes 49184 | tf_op jit(solution)/shard_map/ppermute | solution.py:509
  126.5 1.5 %collective-permute-start.21 = (bf16[32,768]{1,0:T(8,128)(2,1)S(1)}, bf16[32,768]{1,0:T(8,128)(2,1)S(1)}, u32[]{:S(2)}, u32[]{:S(2)}) collective-permute-start(bf16[32,768]{1,0:T(8,128)(2,1)S(1)} %line_sum.1.refs_0_), channel_id=1, source_target_pairs={{0,3},{1,2},{2,1},{3,0},{4,7},{5,6},{6,5},{7,4},{8,11},{9,10},{10,... | collective-permute-start | bytes 147464 | tf_op jit(solution)/shard_map/ppermute | solution.py:513
  128.0 0.0 collective-permute-start.20
  128.0 2.9 %collective-permute-start.19 = (bf16[32,768]{1,0:T(8,128)(2,1)S(1)}, bf16[32,768]{1,0:T(8,128)(2,1)S(1)}, u32[]{:S(2)}, u32[]{:S(2)}) collective-permute-start(bf16[32,768]{1,0:T(8,128)(2,1)S(1)} %line_sum.1.refs_0_), channel_id=1, source_target_pairs={{0,1},{1,0},{2,3},{3,2},{4,5},{5,4},{6,7},{7,6},{8,9},{9,8},{10,11... | collective-permute-start | bytes 147464 | tf_op jit(solution)/shard_map/ppermute | solution.py:513
  130.9 1.5 %collective-permute-done.21.refs_3_ = bf16[32,768]{1,0:T(8,128)(2,1)S(1)} collective-permute-done((bf16[32,768]{1,0:T(8,128)(2,1)S(1)}, bf16[32,768]{1,0:T(8,128)(2,1)S(1)}, u32[]{:S(2)}, u32[]{:S(2)}) %collective-permute-start.21) | collective-permute-done | bytes 49184 | tf_op jit(solution)/shard_map/ppermute | solution.py:513
  132.4 1.1 collective-permute-done.20.refs_2_
  133.5 0.1 collective-permute-start.26
  133.6 3.4 %collective-permute-start.25 = (bf16[4,32,768]{2,1,0:T(8,128)(2,1)S(1)}, bf16[4,32,768]{2,1,0:T(8,128)(2,1)S(1)}, u32[]{:S(2)}, u32[]{:S(2)}) collective-permute-start(bf16[4,32,768]{2,1,0:T(8,128)(2,1)S(1)} %line_place.1.refs_0_), channel_id=1, source_target_pairs={{0,16},{4,20},{8,24},{12,28},{16,0},{20,4},{24,8},{28,12},{1,17},{... | collective-permute-start | bytes 589832 | tf_op jit(solution)/shard_map/ppermute | solution.py:517
  137.1 1.4 collective-permute-start.24
  138.5 4.9 %temporal_forward.1 = bf16[8,8,64,256]{3,2,1,0:T(8,128)(2,1)} custom-call(s32[2]{0:T(128)S(1)} %copy-done.6, s32[2]{0:T(128)S(1)} %copy-done.7, bf16[8,512,256]{2,1,0:T(8,128)(2,1)S(1)} %get-tuple-element.90.act_ref.own, bf16[8,512,256]{2,1,0:T(8,128)(2,1)S(1)} %collective-permute-done.22.nxt, bf16[8,512,256]{2,1,0:T(8,128)(2,1)S(1)} %collective-permute-done.23.prv, ...), custom_call_target="tpu_custom_call" | custom-call | flops 1610612736 | bytes 10485760 | tf_op jit(solution)/shard_map/temporal_forward/pallas_call | solution.py:20
  143.4 0.8 collective-permute-done.24.refs_1_
  144.2 0.1 plane_place.1.mine_ref
  144.3 0.1 collective-permute-start.27
  144.4 2.3 %collective-permute-done.27.got_ref = bf16[4,4,32,768]{3,2,1,0:T(8,128)(2,1)S(1)} collective-permute-done((bf16[4,4,32,768]{3,2,1,0:T(8,128)(2,1)S(1)}, bf16[4,4,32,768]{3,2,1,0:T(8,128)(2,1)S(1)}, u32[]{:S(2)}, u32[]{:S(2)}) %collective-permute-start.27) | collective-permute-done | bytes 786464 | tf_op jit(solution)/shard_map/ppermute | solution.py:529
  146.7 1.9 %finish.1 = (f32[3,3,256,256]{3,2,1,0:T(8,128)}, f32[3,256,256]{2,1,0:T(8,128)}) custom-call(bf16[4,4,32,768]{3,2,1,0:T(8,128)(2,1)S(1)} %plane_place.1.mine_ref, bf16[4,4,32,768]{3,2,1,0:T(8,128)(2,1)S(1)} %collective-permute-done.27.got_ref), custom_call_target="tpu_custom_call" | custom-call | bytes 4194304 | tf_op jit(solution)/shard_map/finish/pallas_call | solution.py:20
  (32 shorter events, 0.1 us)
Async XLA Ops:
  0.6 19.4 %copy-start = (bf16[8,8,64,256]{3,2,1,0:T(8,128)(2,1)S(1)}, bf16[8,8,64,256]{3,2,1,0:T(8,128)(2,1)}, u32[]{:S(2)}) copy-start(bf16[8,8,64,256]{3,2,1,0:T(8,128)(2,1)} %x_ref.5) | copy-start | bytes 6291460
  0.6 45.5 %collective-permute-start.5 = (bf16[8,512,256]{2,1,0:T(8,128)(2,1)}, bf16[8,512,256]{2,1,0:T(8,128)(2,1)S(1)}, u32[]{:S(2)}, u32[]{:S(2)}) collective-permute-start(bf16[8,512,256]{2,1,0:T(8,128)(2,1)} %bitcast.4), channel_id=1, source_target_pairs={{0,4},{4,8},{8,12},{12,16},{16,20},{20,24},{24,28},{1,5},{5,9},{9,... | collective-permute-start | bytes 6291464 | tf_op jit(solution)/shard_map/ppermute | solution.py:391
  3.3 42.9 %collective-permute-start.4 = (bf16[8,512,256]{2,1,0:T(8,128)(2,1)}, bf16[8,512,256]{2,1,0:T(8,128)(2,1)S(1)}, u32[]{:S(2)}, u32[]{:S(2)}) collective-permute-start(bf16[8,512,256]{2,1,0:T(8,128)(2,1)} %bitcast.5), channel_id=1, source_target_pairs={{4,0},{8,4},{12,8},{16,12},{20,16},{24,20},{28,24},{5,1},{9,5},{13... | collective-permute-start | bytes 6291464 | tf_op jit(solution)/shard_map/ppermute | solution.py:391
  5.7 9.7 %collective-permute-start = (bf16[8,1,64,256]{3,2,1,0:T(8,128)(2,1)S(1)}, bf16[8,1,64,256]{3,2,1,0:T(8,128)(2,1)S(1)}, u32[]{:S(2)}, u32[]{:S(2)}) collective-permute-start(bf16[8,1,64,256]{3,2,1,0:T(8,128)(2,1)S(1)} %get-tuple-element.97), channel_id=1, source_target_pairs={{0,1},{1,2},{2,3},{4,5},{5,6},{6,7},{8,9},{9,10},{10,11},{12,13},{... | collective-permute-start | bytes 786440 | tf_op jit(solution)/shard_map/ppermute | solution.py:391
  10.0 10.0 %collective-permute-start.1 = (bf16[8,1,64,256]{3,2,1,0:T(8,128)(2,1)S(1)}, bf16[8,1,64,256]{3,2,1,0:T(8,128)(2,1)S(1)}, u32[]{:S(2)}, u32[]{:S(2)}) collective-permute-start(bf16[8,1,64,256]{3,2,1,0:T(8,128)(2,1)S(1)} %get-tuple-element.96), channel_id=1, source_target_pairs={{1,0},{2,1},{3,2},{5,4},{6,5},{7,6},{9,8},{10,9},{11,10},{13,12},{... | collective-permute-start | bytes 786440 | tf_op jit(solution)/shard_map/ppermute | solution.py:391
  11.3 1.0 copy-start.2
  12.3 1.3 copy-start.4
  20.0 1.3 copy-start.5
  26.9 3.9 %collective-permute-start.2 = (f32[8,2,256]{2,1,0:T(2,128)S(1)}, f32[8,2,256]{2,1,0:T(2,128)S(1)}, u32[]{:S(2)}, u32[]{:S(2)}) collective-permute-start(f32[8,2,256]{2,1,0:T(2,128)S(1)} %get-tuple-element.53), channel_id=1, source_target_pairs={{0,1},{1,0},{2,3},{3,2},{4,5},{5,4},{6,7},{7,6},{8,9},{9,8},{10,11... | collective-permute-start | bytes 49160 | tf_op jit(solution)/shard_map/ppermute | solution.py:400
  30.8 4.9 %copy-start.6 = (s32[2]{0:T(128)S(1)}, s32[2]{0:T(128)}, u32[]{:S(2)}) copy-start(s32[2]{0:T(128)} %clip_ref.5) | copy-start | bytes 28
  30.8 4.9 %copy-start.8 = (f32[256]{0:T(256)S(1)}, f32[256]{0:T(256)}, u32[]{:S(2)}) copy-start(f32[256]{0:T(256)} %param.12) | copy-start | bytes 3076
  30.8 4.9 %copy-start.9 = (f32[256]{0:T(256)S(1)}, f32[256]{0:T(256)}, u32[]{:S(2)}) copy-start(f32[256]{0:T(256)} %param.13) | copy-start | bytes 3076
  30.8 4.9 %collective-permute-start.3 = (f32[8,2,256]{2,1,0:T(2,128)S(1)}, f32[8,2,256]{2,1,0:T(2,128)S(1)}, u32[]{:S(2)}, u32[]{:S(2)}) collective-permute-start(f32[8,2,256]{2,1,0:T(2,128)S(1)} %add.6.refs_0_), channel_id=1, source_target_pairs={{0,2},{1,3},{2,0},{3,1},{4,6},{5,7},{6,4},{7,5},{8,10},{9,11},{10,... | collective-permute-start | bytes 49160 | tf_op jit(solution)/shard_map/ppermute | solution.py:400
  35.7 10.4 %copy-start.1 = (bf16[8,8,64,256]{3,2,1,0:T(8,128)(2,1)S(1)}, bf16[8,8,64,256]{3,2,1,0:T(8,128)(2,1)}, u32[]{:S(2)}) copy-start(bf16[8,8,64,256]{3,2,1,0:T(8,128)(2,1)} %cot_ref.1) | copy-start | bytes 6291460
  35.7 10.4 %copy-start.7 = (s32[2]{0:T(128)S(1)}, s32[2]{0:T(128)}, u32[]{:S(2)}) copy-start(s32[2]{0:T(128)} %dil_ref.3) | copy-start | bytes 28
  41.5 26.3 %collective-permute-start.7 = (bf16[8,2,64,256]{3,2,1,0:T(8,128)(2,1)S(1)}, bf16[8,2,64,256]{3,2,1,0:T(8,128)(2,1)S(1)}, u32[]{:S(2)}, u32[]{:S(2)}) collective-permute-start(bf16[8,2,64,256]{3,2,1,0:T(8,128)(2,1)S(1)} %get-tuple-element.65), channel_id=1, source_target_pairs={{0,1},{1,2},{2,3},{4,5},{5,6},{6,7},{8,9},{9,10},{10,11},{12,13},{... | collective-permute-start | bytes 1572872 | tf_op jit(solution)/shard_map/ppermute | solution.py:391
  44.8 26.5 %collective-permute-start.8 = (bf16[8,2,64,256]{3,2,1,0:T(8,128)(2,1)S(1)}, bf16[8,2,64,256]{3,2,1,0:T(8,128)(2,1)S(1)}, u32[]{:S(2)}, u32[]{:S(2)}) collective-permute-start(bf16[8,2,64,256]{3,2,1,0:T(8,128)(2,1)S(1)} %get-tuple-element.66), channel_id=1, source_target_pairs={{1,0},{2,1},{3,2},{5,4},{6,5},{7,6},{9,8},{10,9},{11,10},{13,12},{... | collective-permute-start | bytes 1572872 | tf_op jit(solution)/shard_map/ppermute | solution.py:391
  50.1 9.3 %collective-permute-start.6 = (f32[8,2,256]{2,1,0:T(2,128)S(1)}, f32[8,2,256]{2,1,0:T(2,128)S(1)}, u32[]{:S(2)}, u32[]{:S(2)}) collective-permute-start(f32[8,2,256]{2,1,0:T(2,128)S(1)} %get-tuple-element.62), channel_id=1, source_target_pairs={{0,1},{1,0},{2,3},{3,2},{4,5},{5,4},{6,7},{7,6},{8,9},{9,8},{10,11... | collective-permute-start | bytes 49160 | tf_op jit(solution)/shard_map/ppermute | solution.py:400
  59.4 79.1 %collective-permute-start.23 = (bf16[8,512,256]{2,1,0:T(8,128)(2,1)S(1)}, bf16[8,512,256]{2,1,0:T(8,128)(2,1)S(1)}, u32[]{:S(2)}, u32[]{:S(2)}) collective-permute-start(bf16[8,512,256]{2,1,0:T(8,128)(2,1)S(1)} %get-tuple-element.90.act_ref.own), channel_id=1, source_target_pairs={{0,4},{4,8},{8,12},{12,16},{16,20},{20,24},{24,28},{1,5},{5,9},{9,... | collective-permute-start | bytes 6291464 | tf_op jit(solution)/shard_map/ppermute | solution.py:391
  62.0 76.5 %collective-permute-start.22 = (bf16[8,512,256]{2,1,0:T(8,128)(2,1)S(1)}, bf16[8,512,256]{2,1,0:T(8,128)(2,1)S(1)}, u32[]{:S(2)}, u32[]{:S(2)}) collective-permute-start(bf16[8,512,256]{2,1,0:T(8,128)(2,1)S(1)} %get-tuple-element.90.act_ref.own), channel_id=1, source_target_pairs={{4,0},{8,4},{12,8},{16,12},{20,16},{24,20},{28,24},{5,1},{9,5},{13... | collective-permute-start | bytes 6291464 | tf_op jit(solution)/shard_map/ppermute | solution.py:391
  63.3 9.4 %collective-permute-start.9 = (f32[8,2,256]{2,1,0:T(2,128)S(1)}, f32[8,2,256]{2,1,0:T(2,128)S(1)}, u32[]{:S(2)}, u32[]{:S(2)}) collective-permute-start(f32[8,2,256]{2,1,0:T(2,128)S(1)} %add.7.refs_2_), channel_id=1, source_target_pairs={{0,2},{1,3},{2,0},{3,1},{4,6},{5,7},{6,4},{7,5},{8,10},{9,11},{10,... | collective-permute-start | bytes 49160 | tf_op jit(solution)/shard_map/ppermute | solution.py:400
  67.8 12.8 %collective-permute-start.10 = (bf16[8,64,256]{2,1,0:T(8,128)(2,1)S(1)}, bf16[8,64,256]{2,1,0:T(8,128)(2,1)S(1)}, u32[]{:S(2)}, u32[]{:S(2)}) collective-permute-start(bf16[8,64,256]{2,1,0:T(8,128)(2,1)S(1)} %get-tuple-element.69), channel_id=1, source_target_pairs={{0,1},{1,2},{2,3},{4,5},{5,6},{6,7},{8,9},{9,10},{10,11},{12,13},{... | collective-permute-start | bytes 786440 | tf_op jit(solution)/shard_map/ppermute | solution.py:391
  71.3 10.8 %collective-permute-start.11 = (bf16[8,64,256]{2,1,0:T(8,128)(2,1)S(1)}, bf16[8,64,256]{2,1,0:T(8,128)(2,1)S(1)}, u32[]{:S(2)}, u32[]{:S(2)}) collective-permute-start(bf16[8,64,256]{2,1,0:T(8,128)(2,1)S(1)} %get-tuple-element.70), channel_id=1, source_target_pairs={{1,0},{2,1},{3,2},{5,4},{6,5},{7,6},{9,8},{10,9},{11,10},{13,12},{... | collective-permute-start | bytes 786440 | tf_op jit(solution)/shard_map/ppermute | solution.py:391
  84.4 2.4 %collective-permute-start.12 = (bf16[4,4,32,768]{3,2,1,0:T(8,128)(2,1)S(1)}, bf16[4,4,32,768]{3,2,1,0:T(8,128)(2,1)S(1)}, u32[]{:S(2)}, u32[]{:S(2)}) collective-permute-start(bf16[4,4,32,768]{3,2,1,0:T(8,128)(2,1)S(1)} %get-tuple-element.74), channel_id=1, source_target_pairs={{0,4},{4,0},{8,12},{12,8},{16,20},{20,16},{24,28},{28,24},{1,5},{5... | collective-permute-start | bytes 2359304 | tf_op jit(solution)/shard_map/ppermute | solution.py:491
  86.9 29.3 %collective-permute-start.13 = (bf16[4,32,768]{2,1,0:T(8,128)(2,1)S(1)}, bf16[4,32,768]{2,1,0:T(8,128)(2,1)S(1)}, u32[]{:S(2)}, u32[]{:S(2)}) collective-permute-start(bf16[4,32,768]{2,1,0:T(8,128)(2,1)S(1)} %get-tuple-element.83), channel_id=1, source_target_pairs={{0,8},{4,12},{8,0},{12,4},{16,24},{20,28},{24,16},{28,20},{1,9},{5... | collective-permute-start | bytes 589832 | tf_op jit(solution)/shard_map/ppermute | solution.py:496
  88.4 27.8 %collective-permute-start.14 = (bf16[4,32,768]{2,1,0:T(8,128)(2,1)S(1)}, bf16[4,32,768]{2,1,0:T(8,128)(2,1)S(1)}, u32[]{:S(2)}, u32[]{:S(2)}) collective-permute-start(bf16[4,32,768]{2,1,0:T(8,128)(2,1)S(1)} %get-tuple-element.84), channel_id=1, source_target_pairs={{0,16},{4,20},{8,24},{12,28},{16,0},{20,4},{24,8},{28,12},{1,17},{... | collective-permute-start | bytes 589832 | tf_op jit(solution)/shard_map/ppermute | solution.py:496
  89.4 26.9 %collective-permute-start.15 = (bf16[4,32,768]{2,1,0:T(8,128)(2,1)S(1)}, bf16[4,32,768]{2,1,0:T(8,128)(2,1)S(1)}, u32[]{:S(2)}, u32[]{:S(2)}) collective-permute-start(bf16[4,32,768]{2,1,0:T(8,128)(2,1)S(1)} %get-tuple-element.85), channel_id=1, source_target_pairs={{0,24},{4,28},{8,16},{12,20},{16,8},{20,12},{24,0},{28,4},{1,25},{... | collective-permute-start | bytes 589832 | tf_op jit(solution)/shard_map/ppermute | solution.py:496
  90.7 47.7 %copy-start.3 = (bf16[3,256,256]{2,1,0:T(8,128)(2,1)S(1)}, bf16[3,256,256]{2,1,0:T(8,128)(2,1)}, u32[]{:S(2)}) copy-start(bf16[3,256,256]{2,1,0:T(8,128)(2,1)} %temporal_ref.1) | copy-start | bytes 1179652
  116.3 4.5 %collective-permute-start.16 = (bf16[32,768]{1,0:T(8,128)(2,1)S(1)}, bf16[32,768]{1,0:T(8,128)(2,1)S(1)}, u32[]{:S(2)}, u32[]{:S(2)}) collective-permute-start(bf16[32,768]{1,0:T(8,128)(2,1)S(1)} %get-tuple-element.87), channel_id=1, source_target_pairs={{0,1},{1,0},{2,3},{3,2},{4,5},{5,4},{6,7},{7,6},{8,9},{9,8},{10,11... | collective-permute-start | bytes 147464 | tf_op jit(solution)/shard_map/ppermute | solution.py:509
  118.0 5.5 %collective-permute-start.17 = (bf16[32,768]{1,0:T(8,128)(2,1)S(1)}, bf16[32,768]{1,0:T(8,128)(2,1)S(1)}, u32[]{:S(2)}, u32[]{:S(2)}) collective-permute-start(bf16[32,768]{1,0:T(8,128)(2,1)S(1)} %get-tuple-element.88), channel_id=1, source_target_pairs={{0,2},{1,3},{2,0},{3,1},{4,6},{5,7},{6,4},{7,5},{8,10},{9,11},{10,... | collective-permute-start | bytes 147464 | tf_op jit(solution)/shard_map/ppermute | solution.py:509
  120.5 5.9 %collective-permute-start.18 = (bf16[32,768]{1,0:T(8,128)(2,1)S(1)}, bf16[32,768]{1,0:T(8,128)(2,1)S(1)}, u32[]{:S(2)}, u32[]{:S(2)}) collective-permute-start(bf16[32,768]{1,0:T(8,128)(2,1)S(1)} %get-tuple-element.89), channel_id=1, source_target_pairs={{0,3},{1,2},{2,1},{3,0},{4,7},{5,6},{6,5},{7,4},{8,11},{9,10},{10,... | collective-permute-start | bytes 147464 | tf_op jit(solution)/shard_map/ppermute | solution.py:509
  126.5 6.0 %collective-permute-start.21 = (bf16[32,768]{1,0:T(8,128)(2,1)S(1)}, bf16[32,768]{1,0:T(8,128)(2,1)S(1)}, u32[]{:S(2)}, u32[]{:S(2)}) collective-permute-start(bf16[32,768]{1,0:T(8,128)(2,1)S(1)} %line_sum.1.refs_0_), channel_id=1, source_target_pairs={{0,3},{1,2},{2,1},{3,0},{4,7},{5,6},{6,5},{7,4},{8,11},{9,10},{10,... | collective-permute-start | bytes 147464 | tf_op jit(solution)/shard_map/ppermute | solution.py:513
  128.0 5.5 %collective-permute-start.20 = (bf16[32,768]{1,0:T(8,128)(2,1)S(1)}, bf16[32,768]{1,0:T(8,128)(2,1)S(1)}, u32[]{:S(2)}, u32[]{:S(2)}) collective-permute-start(bf16[32,768]{1,0:T(8,128)(2,1)S(1)} %line_sum.1.refs_0_), channel_id=1, source_target_pairs={{0,2},{1,3},{2,0},{3,1},{4,6},{5,7},{6,4},{7,5},{8,10},{9,11},{10,... | collective-permute-start | bytes 147464 | tf_op jit(solution)/shard_map/ppermute | solution.py:513
  128.0 5.5 %collective-permute-start.19 = (bf16[32,768]{1,0:T(8,128)(2,1)S(1)}, bf16[32,768]{1,0:T(8,128)(2,1)S(1)}, u32[]{:S(2)}, u32[]{:S(2)}) collective-permute-start(bf16[32,768]{1,0:T(8,128)(2,1)S(1)} %line_sum.1.refs_0_), channel_id=1, source_target_pairs={{0,1},{1,0},{2,3},{3,2},{4,5},{5,4},{6,7},{7,6},{8,9},{9,8},{10,11... | collective-permute-start | bytes 147464 | tf_op jit(solution)/shard_map/ppermute | solution.py:513
  133.5 9.9 %collective-permute-start.26 = (bf16[4,32,768]{2,1,0:T(8,128)(2,1)S(1)}, bf16[4,32,768]{2,1,0:T(8,128)(2,1)S(1)}, u32[]{:S(2)}, u32[]{:S(2)}) collective-permute-start(bf16[4,32,768]{2,1,0:T(8,128)(2,1)S(1)} %line_place.1.refs_0_), channel_id=1, source_target_pairs={{0,24},{4,28},{8,16},{12,20},{16,8},{20,12},{24,0},{28,4},{1,25},{... | collective-permute-start | bytes 589832 | tf_op jit(solution)/shard_map/ppermute | solution.py:517
  133.6 9.8 %collective-permute-start.25 = (bf16[4,32,768]{2,1,0:T(8,128)(2,1)S(1)}, bf16[4,32,768]{2,1,0:T(8,128)(2,1)S(1)}, u32[]{:S(2)}, u32[]{:S(2)}) collective-permute-start(bf16[4,32,768]{2,1,0:T(8,128)(2,1)S(1)} %line_place.1.refs_0_), channel_id=1, source_target_pairs={{0,16},{4,20},{8,24},{12,28},{16,0},{20,4},{24,8},{28,12},{1,17},{... | collective-permute-start | bytes 589832 | tf_op jit(solution)/shard_map/ppermute | solution.py:517
  137.1 7.2 %collective-permute-start.24 = (bf16[4,32,768]{2,1,0:T(8,128)(2,1)S(1)}, bf16[4,32,768]{2,1,0:T(8,128)(2,1)S(1)}, u32[]{:S(2)}, u32[]{:S(2)}) collective-permute-start(bf16[4,32,768]{2,1,0:T(8,128)(2,1)S(1)} %line_place.1.refs_0_), channel_id=1, source_target_pairs={{0,8},{4,12},{8,0},{12,4},{16,24},{20,28},{24,16},{28,20},{1,9},{5... | collective-permute-start | bytes 589832 | tf_op jit(solution)/shard_map/ppermute | solution.py:517
  144.3 2.4 %collective-permute-start.27 = (bf16[4,4,32,768]{3,2,1,0:T(8,128)(2,1)S(1)}, bf16[4,4,32,768]{3,2,1,0:T(8,128)(2,1)S(1)}, u32[]{:S(2)}, u32[]{:S(2)}) collective-permute-start(bf16[4,4,32,768]{3,2,1,0:T(8,128)(2,1)S(1)} %plane_place.1.mine_ref), channel_id=1, source_target_pairs={{0,4},{4,0},{8,12},{12,8},{16,20},{20,16},{24,28},{28,24},{1,5},{5... | collective-permute-start | bytes 2359304 | tf_op jit(solution)/shard_map/ppermute | solution.py:529

commit v3 on v2

--- a/solution.py
+++ b/solution.py
@@ -106,9 +106,10 @@
     return (later, later_which), (earlier, earlier_which), used
 
 
-def gather_taps(clip_ref, dil_ref, local, own, nxt, prv, cat_ref, at, up_slot):
+def gather_taps(clip_ref, dil_ref, local, own, nxt, prv, corner, cat_ref, at, up_slot):
     frames, pixels, channels = own.shape
     later, earlier, used = slot_sources(clip_ref, dil_ref, local, frames)
+    me, half = lax.axis_index("tm"), frames // 2
 
     def put(slot, ref, index):
         cat_ref[pl.ds(at, pixels), slot * channels : (slot + 1) * channels] = ref[index]
@@ -116,13 +117,21 @@
     def clear(slot):
         cat_ref[pl.ds(at, pixels), slot * channels : (slot + 1) * channels] = jnp.zeros((pixels, channels), BF16)
 
-    for slot, (index, which), other, shift in (
-        (up_slot, later, nxt, -frames),
-        (2 - up_slot, earlier, prv, frames),
+    for slot, (index, which), other, shift, turn in (
+        (up_slot, later, nxt, -frames, 3),
+        (2 - up_slot, earlier, prv, frames, 4),
     ):
+        beyond = which == 2
+        there = jnp.clip(index + shift, 0, frames - 1)
         pl.when(which == 0)(functools.partial(clear, slot))
         pl.when(which == 1)(functools.partial(put, slot, own, jnp.clip(index, 0, frames - 1)))
-        pl.when(which == 2)(functools.partial(put, slot, other, jnp.clip(index + shift, 0, frames - 1)))
+        if corner:
+            by_corner = beyond & (me == turn)
+            low, high = by_corner & (there < half), by_corner & (there >= half)
+            pl.when(low)(functools.partial(put, slot, corner[0], jnp.minimum(there, half - 1)))
+            pl.when(high)(functools.partial(put, slot, corner[1], jnp.maximum(there - half, 0)))
+            beyond = beyond & (me != turn)
+        pl.when(beyond)(functools.partial(put, slot, other, there))
     pl.when(used)(functools.partial(put, 1, own, local))
     pl.when(jnp.logical_not(used))(functools.partial(clear, 1))
 
@@ -155,28 +164,41 @@
     loop(frames // 2, body)
 
 
+def edge_kernel(n, entries, group_size, *refs):
+    parts, (conv_ref, first_ref, last_ref) = refs[:n], refs[n:]
+    frames, pixels, _ = conv_ref.shape
+    width = first_ref.shape[1]
+
+    def body(f):
+        mean, inv = mean_and_inv(parts, f, entries, group_size)
+        first_ref[f] = ((conv_ref[f, :width] - mean) * inv).astype(BF16)
+        last_ref[f] = ((conv_ref[f, pixels - width :] - mean) * inv).astype(BF16)
+
+    loop(frames, body)
+
+
+def silu_parts(normed, half_gain, half_shift):
+    h = normed * half_gain + half_shift
+    t = jnp.tanh(h)
+    rise = 1.0 + t
+    return h, rise, rise * (1.0 + h * (1.0 - t)) * half_gain
+
+
 def act_kernel(n, entries, group_size, clip_ref, *refs):
     parts, refs = refs[:n], refs[n:]
-    conv_ref, gain_ref, shift_ref, act_ref, normed_ref, slope_ref, first_ref, last_ref = refs
-    frames, pixels, _ = conv_ref.shape
-    width = first_ref.shape[2]
+    conv_ref, gain_ref, shift_ref, act_ref, normed_ref, slope_ref = refs
+    frames = conv_ref.shape[0]
     first = lax.axis_index("tm") * frames
-    top, bottom = slice(0, width), slice(pixels - width, pixels)
     filled = clip_ref[0] + clip_ref[1]
     half_gain, half_shift = 0.5 * gain_ref[...], 0.5 * shift_ref[...]
 
     def body(f):
         mean, inv = mean_and_inv(parts, f, entries, group_size)
         normed = (conv_ref[f] - mean) * inv
-        h = normed * half_gain + half_shift
-        t = jnp.tanh(h)
-        rise = 1.0 + t
+        h, rise, slope = silu_parts(normed, half_gain, half_shift)
         act_ref[f] = jnp.where(first + f < filled, h * rise, 0.0).astype(BF16)
-        for k, (ref, value) in enumerate(((normed_ref, normed), (slope_ref, rise * (1.0 + h * (1.0 - t)) * half_gain))):
-            value = value.astype(BF16)
-            ref[f] = value
-            first_ref[f, k] = value[top]
-            last_ref[f, k] = value[bottom]
+        normed_ref[f] = normed.astype(BF16)
+        slope_ref[f] = slope.astype(BF16)
 
     loop(frames, body)
 
@@ -205,9 +227,9 @@
             back_ref[j, rows] = spatial_ref[i, j].T
 
 
-def grad_act_kernel(
-    clip_ref, dil_ref, own, nxt, prv, tw_ref, normed_ref, slope_ref, ga_ref, first_ref, last_ref, cat_ref, sums_ref
-):
+def grad_act_kernel(corners, clip_ref, dil_ref, own, nxt, prv, *refs):
+    corner, refs = refs[:corners], refs[corners:]
+    tw_ref, normed_ref, slope_ref, ga_ref, first_ref, last_ref, cat_ref, sums_ref = refs
     frames, pixels, _ = own.shape
     width = first_ref.shape[1]
 
@@ -215,7 +237,7 @@
         rows = pl.ds(pl.multiple_of(2 * pair * pixels, 2 * pixels), 2 * pixels)
         for b in range(2):
             at = pl.multiple_of((2 * pair + b) * pixels, pixels)
-            gather_taps(clip_ref, dil_ref, 2 * pair + b, own, nxt, prv, cat_ref, at, 0)
+            gather_taps(clip_ref, dil_ref, 2 * pair + b, own, nxt, prv, corner, cat_ref, at, 0)
         grad_act = dot(cat_ref[rows], tw_ref[...]).astype(BF16)
         for b in range(2):
             f = 2 * pair + b
@@ -284,22 +306,27 @@
     pl.when(core == 1)(functools.partial(hand_out, half, 0))
 
 
-def conv_back_kernel(n, m, entries, group_size, g_ref, near_above, near_below, ga_above, ga_below, cot_ref, w_ref, *refs):
+def conv_back_kernel(
+    n, m, entries, group_size, g_ref, near_above, near_below, ga_above, ga_below, gain_ref, shift_ref, cot_ref, w_ref, *refs
+):
     parts, grad_parts = refs[:n], refs[n : n + m]
     out_ref, lhs_ref = refs[n + m :]
     frames, rows, width, channels = cot_ref.shape
     pixels = rows * width
     place, size = lax.axis_index("space"), lax.axis_size("space")
+    half_gain, half_shift = 0.5 * gain_ref[...], 0.5 * shift_ref[...]
+
+    def edge(inv, means, normed, grad_act, there):
+        _, _, slope = silu_parts(normed.astype(F32), half_gain, half_shift)
+        return jnp.where(there, norm_back(inv, means, normed, slope, grad_act), 0.0).astype(BF16)
 
     def body(pair):
         for b in range(2):
             f = 2 * pair + b
             _, inv = mean_and_inv(parts, f, entries, group_size)
             means = frame_stats(grad_parts, f, entries, group_size)
-            above = norm_back(inv, means, near_above[f, 0], near_above[f, 1], ga_above[f])
-            below = norm_back(inv, means, near_below[f, 0], near_below[f, 1], ga_below[f])
-            above = jnp.where(place > 0, above, 0.0).astype(BF16)
-            below = jnp.where(place < size - 1, below, 0.0).astype(BF16)
+            above = edge(inv, means, near_above[f], ga_above[f], place > 0)
+            below = edge(inv, means, near_below[f], ga_below[f], place < size - 1)
             put_windows(above, g_ref[f], below, lhs_ref, b * pixels, (2, 1, 0))
         lhs = lhs_ref[...]
         z = [dot(lhs, w_ref[j]) for j in range(3)]
@@ -311,13 +338,14 @@
     loop(frames // 2, body)
 
 
-def out_kernel(clip_ref, dil_ref, own, nxt, prv, tw_ref, x_ref, out_ref, cat_ref):
+def out_kernel(corners, clip_ref, dil_ref, own, nxt, prv, *refs):
+    corner, (tw_ref, x_ref, out_ref, cat_ref) = refs[:corners], refs[corners:]
     frames, rows, width, channels = x_ref.shape
     pixels = rows * width
 
     def body(pair):
         for b in range(2):
-            gather_taps(clip_ref, dil_ref, 2 * pair + b, own, nxt, prv, cat_ref, b * pixels, 2)
+            gather_taps(clip_ref, dil_ref, 2 * pair + b, own, nxt, prv, corner, cat_ref, b * pixels, 2)
         temporal_out = dot(cat_ref[...], tw_ref[...]).astype(BF16).astype(F32)
         for b in range(2):
             one = temporal_out[b * pixels : (b + 1) * pixels].reshape(rows, width, channels)
@@ -333,16 +361,9 @@
         ref[...] = (keep_ref[chip ^ s] + got_ref[chip ^ s].astype(F32)).astype(BF16)
 
 
-def sum_kernel(count, own_ref, *refs):
-    total = own_ref[...]
-    for ref in refs[:count]:
-        total = total + ref[...].astype(F32)
-    refs[count][...] = total.astype(BF16)
-
-
-def sum_split_kernel(count, own_ref, *refs):
-    got, (mine_ref, *send_refs) = refs[:count], refs[count:]
-    deep = lax.axis_index("space")
+def sum_split_kernel(count, bit, own_ref, *refs):
+    got, (keep_ref, send_ref) = refs[:count], refs[count:]
+    mine = (lax.axis_index("space") >> bit) & 1
 
     def block(k):
         total = own_ref[k]
@@ -350,9 +371,20 @@
             total = total + ref[k].astype(F32)
         return total
 
-    mine_ref[...] = block(deep)
-    for s, ref in enumerate(send_refs, 1):
-        ref[...] = block(deep ^ s).astype(BF16)
+    for k in range(keep_ref.shape[0]):
+        keep_ref[k] = block(2 * k + mine)
+        send_ref[k] = block(2 * k + 1 - mine).astype(BF16)
+
+
+def sum_kernel(own_ref, got_ref, out_ref):
+    out_ref[...] = (own_ref[...] + got_ref[...].astype(F32)).astype(BF16)
+
+
+def weave_kernel(bit, mine_ref, got_ref, out_ref):
+    mine = (lax.axis_index("space") >> bit) & 1
+    for k in range(mine_ref.shape[0]):
+        out_ref[2 * k + mine] = mine_ref[k]
+        out_ref[2 * k + 1 - mine] = got_ref[k]
 
 
 def place_kernel(axis, shift, *refs):
@@ -384,9 +416,9 @@
     pl.when(core == 1)(functools.partial(write, (got_ref, mine_ref)))
 
 
-def neighbours(axis, low, high):
+def neighbours(axis, low, high, but=None):
     size = lax.axis_size(axis)
-    up = [(i, i + 1) for i in range(size - 1)]
+    up = [(i, i + 1) for i in range(size - 1) if i != but]
     down = [(j, i) for i, j in up]
     return lax.ppermute(high, axis, up), lax.ppermute(low, axis, down)
 
@@ -416,37 +448,51 @@
     windows = pltpu.VMEM((2 * pixels, 3 * channels), BF16)
 
     cot = cotangent.reshape(per_px)
-    cot_prev, cot_next = neighbours("tm", cot, cot)
+    by_corner = tm == 8
+    but = 3 if by_corner else None
+    cot_prev, cot_next = neighbours("tm", cot, cot, but)
     above, below = neighbours("space", frames_in[:, :1], frames_in[:, rows - 1 :])
-
     back_weights, back_taps = call(
         turn_weights_kernel, "turn_weights", [spatial, temporal],
         [shape((3, 3 * channels, channels), BF16), shape((3 * channels, channels), BF16)], 0, big,
     )
-    above, back_weights, back_taps = lax.optimization_barrier((above, back_weights, back_taps))
+    if by_corner:
+        above, below, cot_late = lax.optimization_barrier((above, below, cot))
+        cot_low, cot_high = cot_late[: frames // 2], cot_late[frames // 2 :]
+        cot_relayed = lax.ppermute(cot_high, "tm", [(3, 7), (4, 0)])
     conv_out, sums = call(
         conv_kernel, "conv_forward", [frames_in, above, below, spatial],
         [shape(per_px, F32), shape((frames, 2, channels), F32)],
         18 * big * channels, 8 * big, [windows], 18,
     )
+    cot_corner = []
+    if by_corner:
+        sums, cot_low = lax.optimization_barrier((sums, cot_low))
+        cot_corner.append(lax.ppermute(cot_low, "tm", [(3, 4), (4, 3)]))
     parts = spread_sums(sums, "space")
+    if by_corner:
+        parts[0], cot_relayed = lax.optimization_barrier((parts[0], cot_relayed))
+        cot_corner.append(lax.ppermute(cot_relayed, "tm", [(7, 4), (0, 3)]))
     x_turned = call(
         turn_kernel, "turned", [frames_in, above, below], shape((3 * channels, frames * pixels), BF16),
         0, 8 * big, [pltpu.VMEM((pixels, 3 * channels), BF16)],
     )
     x_turned, *parts = lax.optimization_barrier((x_turned, *parts))
-    edge = shape((frames, 2, width, channels), BF16)
-    act, normed, slope, near_first, near_last = call(
+    edge = shape((frames, width, channels), BF16)
+    near_first, near_last = call(
+        functools.partial(edge_kernel, len(parts), entries, group_size), "edges", [*parts, conv_out], [edge] * 2, 0, big,
+    )
+    near_first, near_last, cot_prev, cot_next = lax.optimization_barrier((near_first, near_last, cot_prev, cot_next))
+    near_above, near_below = neighbours("space", near_first, near_last)
+    act, normed, slope = call(
         functools.partial(act_kernel, len(parts), entries, group_size), "activation",
-        [clip_frames, *parts, conv_out, gain, shift],
-        [shape(per_px, BF16)] * 3 + [edge] * 2, 10 * big, 10 * big,
-    )
-    near_above, near_below = neighbours("space", near_first, near_last)
-
-    edge = shape((frames, width, channels), BF16)
+        [clip_frames, *parts, conv_out, gain, shift], [shape(per_px, BF16)] * 3, 0, big,
+    )
+    normed, near_above, near_below = lax.optimization_barrier((normed, near_above, near_below))
+
     grad_act, ga_first, ga_last, cot_cat, grad_sums = call(
-        grad_act_kernel, "grad_activation",
-        [clip_frames, dilation, cot, cot_next, cot_prev, back_taps, normed, slope],
+        functools.partial(grad_act_kernel, len(cot_corner)), "grad_activation",
+        [clip_frames, dilation, cot, cot_next, cot_prev, *cot_corner, back_taps, normed, slope],
         [
             shape(per_px, BF16), edge, edge, shape((frames * pixels, 3 * channels), BF16),
             shape((frames, 2, channels), F32),
@@ -454,14 +500,16 @@
         6 * big * channels, 16 * big,
     )
     ga_above, ga_below = neighbours("space", ga_first, ga_last)
+    grad_sums, act_sent = lax.optimization_barrier((grad_sums, act))
+    act_prev, act_next = neighbours("tm", act_sent, act_sent, but)
     grad_parts = spread_sums(grad_sums, "space")
-    grad_parts[0], act_sent = lax.optimization_barrier((grad_parts[0], act))
-    act_prev, act_next = neighbours("tm", act_sent, act_sent)
+    if by_corner:
+        grad_parts[0], act_late = lax.optimization_barrier((grad_parts[0], act))
+        act_relayed = lax.ppermute(act_late[frames // 2 :], "tm", [(3, 7), (4, 0)])
     temporal_part = call(
         temporal_grad_kernel, "temporal_grad", [act, cot_cat],
         shape((channels, 3 * channels), F32), 6 * big * channels, 8 * big,
     )
-    grad_parts[0], near_above, near_below = lax.optimization_barrier((grad_parts[0], near_above, near_below))
     lanes = 3 * channels
     grad_conv, moved = call(
         functools.partial(norm_back_kernel, width, len(parts), len(grad_parts), entries, group_size), "norm_backward",
@@ -497,28 +545,40 @@
 
     in_grad = call(
         functools.partial(conv_back_kernel, len(parts), len(grad_parts), entries, group_size), "conv_backward",
-        [grad_conv, near_above, near_below, ga_above, ga_below, cotangent, back_weights, *parts, *grad_parts],
+        [grad_conv, near_above, near_below, ga_above, ga_below, gain, shift, cotangent, back_weights, *parts, *grad_parts],
         shape(frames_in.shape, BF16), 18 * big * channels, 8 * big, [windows], 20,
     )
-    own, in_grad = lax.optimization_barrier((own, in_grad))
-
-    own, *sends = call(
-        functools.partial(sum_split_kernel, chips - 1), "plane_sum", [own, *gots],
-        [shape((block, lanes), F32)] + [shape((block, lanes), BF16)] * (n - 1), 0, big,
-    )
-    gots = [lax.ppermute(x, "space", other_plane(s)) for s, x in enumerate(sends, 1)]
-    own = call(
-        functools.partial(sum_kernel, n - 1), "line_sum", [own, *gots], shape((block, lanes), BF16), 0, big
-    )
-    gots = [lax.ppermute(own, "space", other_plane(s)) for s in range(1, n)]
-    own = call(
-        functools.partial(place_kernel, "space", 0), "line_place", [own, *gots], shape((n, block, lanes), BF16), 0, big
-    )
+    own, in_grad, act_prev, act_next = lax.optimization_barrier((own, in_grad, act_prev, act_next))
+    if by_corner:
+        own, act_relayed = lax.optimization_barrier((own, act_relayed))
+
+    act_corner = []
+    bits = range(n.bit_length() - 1)
+    for bit in bits:
+        m = n >> bit
+        own, send = call(
+            functools.partial(sum_split_kernel, len(gots), bit), "plane_sum" if bit == 0 else "line_sum", [own, *gots],
+            [shape((m // 2, block, lanes), F32), shape((m // 2, block, lanes), BF16)], 0, big,
+        )
+        if by_corner and bit == 0:
+            own, low, high = lax.optimization_barrier((own, act_sent, act_relayed))
+            act_corner = [
+                lax.ppermute(low[: frames // 2], "tm", [(3, 4), (4, 3)]),
+                lax.ppermute(high, "tm", [(7, 4), (0, 3)]),
+            ]
+        gots = [lax.ppermute(send, "space", other_plane(1 << bit))]
+    own = call(sum_kernel, "line_total", [own, *gots], shape((1, block, lanes), BF16), 0, big)
+    for bit in reversed(bits):
+        got = lax.ppermute(own, "space", other_plane(1 << bit))
+        own = call(
+            functools.partial(weave_kernel, bit), "line_weave", [own, got],
+            shape((n >> bit, block, lanes), BF16), 0, big,
+        )
     gots = [lax.ppermute(own, "tm", other_chip(s)) for s in range(1, chips)]
 
     out_frames = call(
-        out_kernel, "temporal_forward",
-        [clip_frames, dilation, act, act_next, act_prev, temporal.reshape(3 * channels, channels), frames_in],
+        functools.partial(out_kernel, len(act_corner)), "temporal_forward",
+        [clip_frames, dilation, act, act_next, act_prev, *act_corner, temporal.reshape(3 * channels, channels), frames_in],
         shape(frames_in.shape, BF16), 6 * big * channels, 10 * big, [windows],
     )
     own, out_frames = lax.optimization_barrier((own, out_frames))

time: 149 us -> 155 us (1.040)
  starting transfers between devices: 50.2 us -> 57.3 us
  Pallas kernels: 44.7 us -> 47.5 us
  waiting for transfers between devices: 47.9 us -> 46 us
  local copies, waits for them, and re-layouts: 4.65 us -> 2.94 us
    ppermute x6 -> x10, waiting for transfers between devices: 8.26 us -> 31.3 us  [the longest x2 8.94 us: per_device(): gots = [lax.ppermute(send, 'space', other_plane(1 << bit))]]
    ppermute x3, waiting for transfers between devices: 17.8 us -> 2.11 us  [per_device(): lax.ppermute(x, 'tm', other_chip(s))]
    ppermute x10, waiting for transfers between devices: 7.58 us -> 3.69 us  [neighbours(): return (lax.ppermute(high, axis, up), lax.ppermute(low, axis, down))]
    ppermute x6 -> x10, starting transfers between devices: 8.9 us -> 12.7 us  [the longest x1 4.03 us: per_device(): lax.ppermute(high, 'tm', [(7, 4), (0, 3)])]
    unnamed x20 -> x16, local copies, waits for them, and re-layouts: 3.57 us -> 0.05 us
    ppermute x4, waiting for transfers between devices: 8.89 us -> 5.8 us  [spread_sums(): got = lax.ppermute(part, axis, [(i, i ^ step) for i in range(size)])]
    ppermute x10, starting transfers between devices: 22.8 us -> 25.8 us  [neighbours(): return (lax.ppermute(high, axis, up), lax.ppermute(low, axis, down))]
    pallas_call x17 -> x20, Pallas kernels: 44.7 us -> 47.5 us  [call(): pl.pallas_call(kernel, in_specs=[smem if x.dtype == jnp.int32 else vmem f...]
  transfers between devices with their start and end apart: 28 -> 32, of which waited for: 14 -> 13; matrix products, arithmetic and copies ran while one was open for 1% -> 1% of each run, Pallas kernels for 29% -> 27%
where the time goes in v3:
time: 155 us
  starting transfers between devices  57.3 us (37%)
  Pallas kernels  47.5 us (31%)
  waiting for transfers between devices  46 us (30%)
  local copies, waits for them, and re-layouts  2.94 us (2%)
    pallas_call x20, Pallas kernels, call(): pl.pallas_call(kernel, in_specs=[smem if x.dtype == jnp.int32 else vmem f...  47.5 us
    ppermute x10, starting transfers between devices, neighbours(): return (lax.ppermute(high, axis, up), lax.ppermute(low, axis, down))  25.8 us
    ppermute x4, starting transfers between devices, spread_sums(): got = lax.ppermute(part, axis, [(i, i ^ step) for i in range(size)])  9.5 us
    ppermute x2, waiting for transfers between devices, per_device(): gots = [lax.ppermute(send, 'space', other_plane(1 << bit))]  8.94 us
    ppermute x1, waiting for transfers between devices, per_device(): act_relayed = lax.ppermute(act_late[frames // 2:], 'tm', [(3, 7), (4, 0)])  8.82 us
    ppermute x2, waiting for transfers between devices, per_device(): got = lax.ppermute(own, 'space', other_plane(1 << bit))  8.05 us
    ppermute x4, waiting for transfers between devices, spread_sums(): got = lax.ppermute(part, axis, [(i, i ^ step) for i in range(size)])  5.8 us
    ppermute x3, starting transfers between devices, per_device(): lax.ppermute(x, 'tm', other_chip(s))  5.68 us
  transfers between devices with their start and end apart: 32, of which 13 were waited for; matrix products, arithmetic and copies ran while one was open for 1% of the time, Pallas kernels for 27%

profile of v3, /device:TPU:0, one launch (start us, length us, event | category | flops | bytes accessed | tf_op | source)
XLA Modules:
  0.0 155.0 jit_solution(15931455139516264089)
XLA Ops:
  0.6 1.1 fusion.1
  1.7 1.3 collective-permute-start.1
  3.0 5.6 %collective-permute-start = (bf16[8,1,64,256]{3,2,1,0:T(8,128)(2,1)S(1)}, bf16[8,1,64,256]{3,2,1,0:T(8,128)(2,1)S(1)}, u32[]{:S(2)}, u32[]{:S(2)}) collective-permute-start(bf16[8,1,64,256]{3,2,1,0:T(8,128)(2,1)S(1)} %get-tuple-element.133), channel_id=1, source_target_pairs={{0,1},{1,2},{2,3},{4,5},{5,6},{6,7},{8,9},{9,10},{10,11},{12,13},{... | collective-permute-start | bytes 786440 | tf_op jit(solution)/shard_map/ppermute | solution.py:423
  8.6 1.6 %collective-permute-start.6 = (bf16[8,512,256]{2,1,0:T(8,128)(2,1)}, bf16[8,512,256]{2,1,0:T(8,128)(2,1)S(1)}, u32[]{:S(2)}, u32[]{:S(2)}) collective-permute-start(bf16[8,512,256]{2,1,0:T(8,128)(2,1)} %bitcast.4), channel_id=1, source_target_pairs={{4,0},{8,4},{12,8},{20,16},{24,20},{28,24},{5,1},{9,5},{13,9},{21,... | collective-permute-start | bytes 6291464 | tf_op jit(solution)/shard_map/ppermute | solution.py:423
  10.2 3.2 %collective-permute-start.5 = (bf16[8,512,256]{2,1,0:T(8,128)(2,1)}, bf16[8,512,256]{2,1,0:T(8,128)(2,1)S(1)}, u32[]{:S(2)}, u32[]{:S(2)}) collective-permute-start(bf16[8,512,256]{2,1,0:T(8,128)(2,1)} %bitcast.5), channel_id=1, source_target_pairs={{0,4},{4,8},{8,12},{16,20},{20,24},{24,28},{1,5},{5,9},{9,13},{17,... | collective-permute-start | bytes 6291464 | tf_op jit(solution)/shard_map/ppermute | solution.py:423
  13.4 0.8 collective-permute-done.above_ref
  14.1 1.7 %fusion = (bf16[4,512,256]{2,1,0:T(8,128)(2,1)S(1)}, bf16[4,512,256]{2,1,0:T(8,128)(2,1)S(1)}) fusion(bf16[8,512,256]{2,1,0:T(8,128)(2,1)} %bitcast.6), kind=kLoop, calls=%fused_computation | loop fusion | bytes 4194304 | tf_op jit(solution)/shard_map/slice | solution.py:461
  15.8 1.3 collective-permute-start.3
  17.1 5.6 %conv_forward.1 = (f32[8,512,256]{2,1,0:T(8,128)S(1)}, f32[8,2,256]{2,1,0:T(2,128)S(1)}) custom-call(bf16[8,8,64,256]{3,2,1,0:T(8,128)(2,1)S(1)} %copy-done, bf16[8,1,64,256]{3,2,1,0:T(8,128)(2,1)S(1)} %collective-permute-done.above_ref, bf16[8,1,64,256]{3,2,1,0:T(8,128)(2,1)S(1)} %collective-permute-done.1.below_ref, bf16[3,3,256,256]{3,2,1,0:T(8,128)(2,1)S(1)} %copy-done.3), custom_call_target="tpu_custom_call" | custom-call | flops 4831838208 | bytes 8388608 | tf_op jit(solution)/shard_map/conv_forward/pallas_call | solution.py:20
  22.8 2.5 %collective-permute-start.2 = (f32[8,2,256]{2,1,0:T(2,128)S(1)}, f32[8,2,256]{2,1,0:T(2,128)S(1)}, u32[]{:S(2)}, u32[]{:S(2)}) collective-permute-start(f32[8,2,256]{2,1,0:T(2,128)S(1)} %get-tuple-element.71), channel_id=1, source_target_pairs={{0,1},{1,0},{2,3},{3,2},{4,5},{5,4},{6,7},{7,6},{8,9},{9,8},{10,11... | collective-permute-start | bytes 49160 | tf_op jit(solution)/shard_map/ppermute | solution.py:432
  25.3 0.7 collective-permute-start.9
  26.0 1.0 collective-permute-done.2
  27.0 5.5 %collective-permute-done.3 = bf16[4,512,256]{2,1,0:T(8,128)(2,1)S(1)} collective-permute-done((bf16[4,512,256]{2,1,0:T(8,128)(2,1)S(1)}, bf16[4,512,256]{2,1,0:T(8,128)(2,1)S(1)}, u32[]{:S(2)}, u32[]{:S(2)}) %collective-permute-start.3) | collective-permute-done | bytes 1048608 | tf_op jit(solution)/shard_map/ppermute | solution.py:462
  32.5 1.3 collective-permute-start.10
  33.8 3.7 %collective-permute-start.4 = (f32[8,2,256]{2,1,0:T(2,128)S(1)}, f32[8,2,256]{2,1,0:T(2,128)S(1)}, u32[]{:S(2)}, u32[]{:S(2)}) collective-permute-start(f32[8,2,256]{2,1,0:T(2,128)S(1)} %add.6.refs_0_), channel_id=1, source_target_pairs={{0,2},{1,3},{2,0},{3,1},{4,6},{5,7},{6,4},{7,5},{8,10},{9,11},{10,... | collective-permute-start | bytes 49160 | tf_op jit(solution)/shard_map/ppermute | solution.py:432
  37.6 2.2 %turned.1.xt_ref = bf16[768,4096]{1,0:T(8,128)(2,1)S(1)} custom-call(bf16[8,8,64,256]{3,2,1,0:T(8,128)(2,1)S(1)} %copy-done, bf16[8,1,64,256]{3,2,1,0:T(8,128)(2,1)S(1)} %collective-permute-done.above_ref, bf16[8,1,64,256]{3,2,1,0:T(8,128)(2,1)S(1)} %collective-permute-done.1.below_ref), custom_call_target="tpu_custom_call" | custom-call | bytes 8388608 | tf_op jit(solution)/shard_map/turned/pallas_call | solution.py:20
  39.8 2.0 %edges.1 = (bf16[8,64,256]{2,1,0:T(8,128)(2,1)S(1)}, bf16[8,64,256]{2,1,0:T(8,128)(2,1)S(1)}) custom-call(f32[8,2,256]{2,1,0:T(2,128)S(1)} %add.6.refs_0_, f32[8,2,256]{2,1,0:T(2,128)S(1)} %collective-permute-done.4.refs_1_, f32[8,512,256]{2,1,0:T(8,128)S(1)} %get-tuple-element.76.refs_2_), custom_call_target="tpu_custom_call" | custom-call | bytes 1048576 | tf_op jit(solution)/shard_map/edges/pallas_call | solution.py:20
  41.8 3.5 %collective-permute-start.7 = (bf16[8,64,256]{2,1,0:T(8,128)(2,1)S(1)}, bf16[8,64,256]{2,1,0:T(8,128)(2,1)S(1)}, u32[]{:S(2)}, u32[]{:S(2)}) collective-permute-start(bf16[8,64,256]{2,1,0:T(8,128)(2,1)S(1)} %get-tuple-element.80), channel_id=1, source_target_pairs={{0,1},{1,2},{2,3},{4,5},{5,6},{6,7},{8,9},{9,10},{10,11},{12,13},{... | collective-permute-start | bytes 786440 | tf_op jit(solution)/shard_map/ppermute | solution.py:423
  45.4 1.3 collective-permute-start.8
  46.7 0.5 turn_weights.1
  47.2 6.0 %activation.1 = (bf16[8,512,256]{2,1,0:T(8,128)(2,1)S(1)}, bf16[8,512,256]{2,1,0:T(8,128)(2,1)S(1)}, bf16[8,512,256]{2,1,0:T(8,128)(2,1)S(1)}) custom-call(s32[2]{0:T(128)S(1)} %copy-done.4, f32[8,2,256]{2,1,0:T(2,128)S(1)} %add.6.refs_0_, f32[8,2,256]{2,1,0:T(2,128)S(1)} %collective-permute-done.4.refs_1_, f32[8,512,256]{2,1,0:T(8,128)S(1)} %get-tuple-element.76.refs_2_, ...), custom_call_target="tpu_custom_call" | custom-call | bytes 1048576 | tf_op jit(solution)/shard_map/activation/pallas_call | solution.py:20
  53.2 2.9 %collective-permute-done.8.near_below = bf16[8,64,256]{2,1,0:T(8,128)(2,1)S(1)} collective-permute-done((bf16[8,64,256]{2,1,0:T(8,128)(2,1)S(1)}, bf16[8,64,256]{2,1,0:T(8,128)(2,1)S(1)}, u32[]{:S(2)}, u32[]{:S(2)}) %collective-permute-start.8) | collective-permute-done | bytes 262176 | tf_op jit(solution)/shard_map/ppermute | solution.py:423
  56.2 4.1 %grad_activation.1 = (bf16[8,512,256]{2,1,0:T(8,128)(2,1)S(1)}, bf16[8,64,256]{2,1,0:T(8,128)(2,1)S(1)}, bf16[8,64,256]{2,1,0:T(8,128)(2,1)S(1)}, bf16[4096,768]{1,0:T(8,128)(2,1)S(1)}, f32[8,2,256]{2,1,0:T(2,128)S(1)}) custom-call(s32[2]{0:T(128)S(1)} %copy-done.4, s32[2]{0:T(128)S(1)} %copy-done.5, bf16[8,512,256]{2,1,0:T(8,128)(2,1)S(1)} %bitcast.7, ...), custom_call_target="tpu_custom_call" | custom-call | flops 1610612736 | bytes 16777216 | tf_op jit(solution)/shard_map/grad_activation/pallas_call | solution.py:20
  60.3 1.3 collective-permute-start.17
  61.6 3.2 %collective-permute-start.16 = (bf16[8,512,256]{2,1,0:T(8,128)(2,1)S(1)}, bf16[8,512,256]{2,1,0:T(8,128)(2,1)S(1)}, u32[]{:S(2)}, u32[]{:S(2)}) collective-permute-start(bf16[8,512,256]{2,1,0:T(8,128)(2,1)S(1)} %get-tuple-element.123.act_ref.own), channel_id=1, source_target_pairs={{0,4},{4,8},{8,12},{16,20},{20,24},{24,28},{1,5},{5,9},{9,13},{17,... | collective-permute-start | bytes 6291464 | tf_op jit(solution)/shard_map/ppermute | solution.py:423
  64.8 0.3 collective-permute-start.11
  65.1 3.7 %collective-permute-start.13 = (bf16[8,64,256]{2,1,0:T(8,128)(2,1)S(1)}, bf16[8,64,256]{2,1,0:T(8,128)(2,1)S(1)}, u32[]{:S(2)}, u32[]{:S(2)}) collective-permute-start(bf16[8,64,256]{2,1,0:T(8,128)(2,1)S(1)} %get-tuple-element.95), channel_id=1, source_target_pairs={{0,1},{1,2},{2,3},{4,5},{5,6},{6,7},{8,9},{9,10},{10,11},{12,13},{... | collective-permute-start | bytes 786440 | tf_op jit(solution)/shard_map/ppermute | solution.py:423
  68.8 1.3 collective-permute-start.14
  70.1 2.9 %collective-permute-start.12 = (f32[8,2,256]{2,1,0:T(2,128)S(1)}, f32[8,2,256]{2,1,0:T(2,128)S(1)}, u32[]{:S(2)}, u32[]{:S(2)}) collective-permute-start(f32[8,2,256]{2,1,0:T(2,128)S(1)} %add.7.refs_2_), channel_id=1, source_target_pairs={{0,2},{1,3},{2,0},{3,1},{4,6},{5,7},{6,4},{7,5},{8,10},{9,11},{10,... | collective-permute-start | bytes 49160 | tf_op jit(solution)/shard_map/ppermute | solution.py:432
  73.0 1.9 %temporal_grad.1.temporal_ref = f32[256,768]{1,0:T(8,128)S(1)} custom-call(bf16[8,512,256]{2,1,0:T(8,128)(2,1)S(1)} %get-tuple-element.123.act_ref.own, bf16[4096,768]{1,0:T(8,128)(2,1)S(1)} %get-tuple-element.98.cat_ref), custom_call_target="tpu_custom_call" | custom-call | flops 1610612736 | bytes 8388608 | tf_op jit(solution)/shard_map/temporal_grad/pallas_call | solution.py:20
  74.9 4.8 %collective-permute-done.12.refs_3_ = f32[8,2,256]{2,1,0:T(2,128)S(1)} collective-permute-done((f32[8,2,256]{2,1,0:T(2,128)S(1)}, f32[8,2,256]{2,1,0:T(2,128)S(1)}, u32[]{:S(2)}, u32[]{:S(2)}) %collective-permute-start.12) | collective-permute-done | bytes 16416 | tf_op jit(solution)/shard_map/ppermute | solution.py:432
  79.7 4.5 %norm_backward.1 = (bf16[8,512,256]{2,1,0:T(8,128)(2,1)S(1)}, bf16[4096,768]{1,0:T(8,128)(2,1)S(1)}) custom-call(bf16[8,512,256]{2,1,0:T(8,128)(2,1)S(1)} %get-tuple-element.82.refs_3_.normed_ref, bf16[8,512,256]{2,1,0:T(8,128)(2,1)S(1)} %get-tuple-element.83.refs_4_.slope_ref, bf16[8,512,256]{2,1,0:T(8,128)(2,1)S(1)} %get-tuple-element.89.ga_ref, ...), custom_call_target="tpu_custom_call" | custom-call | bytes 12582912 | tf_op jit(solution)/shard_map/norm_backward/pallas_call | solution.py:20
  84.2 3.4 %weight_part.1.part_ref = f32[768,512]{1,0:T(8,128)S(1)} custom-call(bf16[768,4096]{1,0:T(8,128)(2,1)S(1)} %turned.1.xt_ref, bf16[4096,768]{1,0:T(8,128)(2,1)S(1)} %get-tuple-element.97.moved_ref), custom_call_target="tpu_custom_call" | custom-call | flops 3221225472 | bytes 8388608 | tf_op jit(solution)/shard_map/weight_part/pallas_call | solution.py:20
  87.7 2.2 %weight_grad.1 = (bf16[4,4,32,768]{3,2,1,0:T(8,128)(2,1)S(1)}, f32[4,4,32,768]{3,2,1,0:T(8,128)S(1)}) custom-call(bf16[768,4096]{1,0:T(8,128)(2,1)S(1)} %turned.1.xt_ref, bf16[4096,768]{1,0:T(8,128)(2,1)S(1)} %get-tuple-element.97.moved_ref, f32[768,512]{1,0:T(8,128)S(1)} %weight_part.1.part_ref, f32[256,768]{1,0:T(8,128)S(1)} %temporal_grad.1.temporal_ref), custom_call_target="tpu_custom_call" | custom-call | flops 1610612736 | bytes 8388608 | tf_op jit(solution)/shard_map/weight_grad/pallas_call | solution.py:20
  89.9 0.1 collective-permute-start.15
  90.0 0.1 slice.22
  90.1 1.3 collective-permute-start.18
  91.4 0.9 collective-permute-done.15.got_ref
  92.2 0.1 core_sum.1
  92.4 0.1 collective-permute-start.19
  92.5 5.6 %collective-permute-start.20 = (bf16[4,32,768]{2,1,0:T(8,128)(2,1)S(1)}, bf16[4,32,768]{2,1,0:T(8,128)(2,1)S(1)}, u32[]{:S(2)}, u32[]{:S(2)}) collective-permute-start(bf16[4,32,768]{2,1,0:T(8,128)(2,1)S(1)} %get-tuple-element.113), channel_id=1, source_target_pairs={{0,16},{4,20},{8,24},{12,28},{16,0},{20,4},{24,8},{28,12},{1,17},{... | collective-permute-start | bytes 589832 | tf_op jit(solution)/shard_map/ppermute | solution.py:544
  98.1 7.7 %conv_backward.1 = bf16[8,8,64,256]{3,2,1,0:T(8,128)(2,1)} custom-call(bf16[8,512,256]{2,1,0:T(8,128)(2,1)S(1)} %get-tuple-element.102.g_ref, bf16[8,64,256]{2,1,0:T(8,128)(2,1)S(1)} %collective-permute-done.7.near_above, bf16[8,64,256]{2,1,0:T(8,128)(2,1)S(1)} %collective-permute-done.8.near_below, ...), custom_call_target="tpu_custom_call" | custom-call | flops 4831838208 | bytes 8388608 | tf_op jit(solution)/shard_map/conv_backward/pallas_call | solution.py:20
  105.8 8.8 %collective-permute-done.18 = bf16[4,512,256]{2,1,0:T(8,128)(2,1)S(1)} collective-permute-done((bf16[4,512,256]{2,1,0:T(8,128)(2,1)S(1)}, bf16[4,512,256]{2,1,0:T(8,128)(2,1)S(1)}, u32[]{:S(2)}, u32[]{:S(2)}) %collective-permute-start.18) | collective-permute-done | bytes 1048608 | tf_op jit(solution)/shard_map/ppermute | solution.py:508
  114.6 2.1 %collective-permute-done.20.refs_1_ = bf16[4,32,768]{2,1,0:T(8,128)(2,1)S(1)} collective-permute-done((bf16[4,32,768]{2,1,0:T(8,128)(2,1)S(1)}, bf16[4,32,768]{2,1,0:T(8,128)(2,1)S(1)}, u32[]{:S(2)}, u32[]{:S(2)}) %collective-permute-start.20) | collective-permute-done | bytes 196640 | tf_op jit(solution)/shard_map/ppermute | solution.py:544
  116.7 0.1 plane_sum.1
  116.8 0.1 slice.23
  116.9 0.7 collective-permute-start.26
  117.6 4.0 %collective-permute-start.27 = (bf16[4,512,256]{2,1,0:T(8,128)(2,1)S(1)}, bf16[4,512,256]{2,1,0:T(8,128)(2,1)S(1)}, u32[]{:S(2)}, u32[]{:S(2)}) collective-permute-start(bf16[4,512,256]{2,1,0:T(8,128)(2,1)S(1)} %collective-permute-done.18), channel_id=1, source_target_pairs={{28,16},{0,12},{29,17},{1,13},{30,18},{2,14},{31,19},{3,15}} | collective-permute-start | bytes 3145736 | tf_op jit(solution)/shard_map/ppermute | solution.py:567
  121.6 1.5 collective-permute-start.22
  123.1 4.0 %collective-permute-done.22.refs_0_ = bf16[2,32,768]{2,1,0:T(8,128)(2,1)S(1)} collective-permute-done((bf16[2,32,768]{2,1,0:T(8,128)(2,1)S(1)}, bf16[2,32,768]{2,1,0:T(8,128)(2,1)S(1)}, u32[]{:S(2)}, u32[]{:S(2)}) %collective-permute-start.22) | collective-permute-done | bytes 98336 | tf_op jit(solution)/shard_map/ppermute | solution.py:569
  127.1 0.1 collective-permute-start.23
  127.2 5.0 %collective-permute-done.23.got_ref = bf16[1,32,768]{2,1,0:T(8,128)(2,1)S(1)} collective-permute-done((bf16[1,32,768]{2,1,0:T(8,128)(2,1)S(1)}, bf16[1,32,768]{2,1,0:T(8,128)(2,1)S(1)}, u32[]{:S(2)}, u32[]{:S(2)}) %collective-permute-start.23) | collective-permute-done | bytes 49184 | tf_op jit(solution)/shard_map/ppermute | solution.py:569
  132.2 0.2 collective-permute-start.24
  132.4 4.9 %collective-permute-done.24.got_ref = bf16[1,32,768]{2,1,0:T(8,128)(2,1)S(1)} collective-permute-done((bf16[1,32,768]{2,1,0:T(8,128)(2,1)S(1)}, bf16[1,32,768]{2,1,0:T(8,128)(2,1)S(1)}, u32[]{:S(2)}, u32[]{:S(2)}) %collective-permute-start.24) | collective-permute-done | bytes 49184 | tf_op jit(solution)/shard_map/ppermute | solution.py:572
  137.3 1.5 collective-permute-start.25
  138.8 3.2 %collective-permute-done.25.got_ref = bf16[2,32,768]{2,1,0:T(8,128)(2,1)S(1)} collective-permute-done((bf16[2,32,768]{2,1,0:T(8,128)(2,1)S(1)}, bf16[2,32,768]{2,1,0:T(8,128)(2,1)S(1)}, u32[]{:S(2)}, u32[]{:S(2)}) %collective-permute-start.25) | collective-permute-done | bytes 98336 | tf_op jit(solution)/shard_map/ppermute | solution.py:572
  142.0 0.1 collective-permute-start.30
  142.1 0.1 collective-permute-start.29
  142.1 3.4 %collective-permute-start.28 = (bf16[4,32,768]{2,1,0:T(8,128)(2,1)S(1)}, bf16[4,32,768]{2,1,0:T(8,128)(2,1)S(1)}, u32[]{:S(2)}, u32[]{:S(2)}) collective-permute-start(bf16[4,32,768]{2,1,0:T(8,128)(2,1)S(1)} %line_weave.3.refs_0_), channel_id=1, source_target_pairs={{0,8},{4,12},{8,0},{12,4},{16,24},{20,28},{24,16},{28,20},{1,9},{5... | collective-permute-start | bytes 589832 | tf_op jit(solution)/shard_map/ppermute | solution.py:577
  145.5 5.1 %temporal_forward.1 = bf16[8,8,64,256]{3,2,1,0:T(8,128)(2,1)} custom-call(s32[2]{0:T(128)S(1)} %copy-done.4, s32[2]{0:T(128)S(1)} %copy-done.5, bf16[8,512,256]{2,1,0:T(8,128)(2,1)S(1)} %get-tuple-element.123.act_ref.own, bf16[8,512,256]{2,1,0:T(8,128)(2,1)S(1)} %collective-permute-done.17.nxt, bf16[8,512,256]{2,1,0:T(8,128)(2,1)S(1)} %collective-permute-done.16.prv, ...), custom_call_target="tpu_custom_call" | custom-call | flops 1610612736 | bytes 10485760 | tf_op jit(solution)/shard_map/temporal_forward/pallas_call | solution.py:20
  150.7 0.1 plane_place.1.mine_ref
  150.8 0.1 collective-permute-start.31
  150.8 2.3 %collective-permute-done.31.got_ref = bf16[4,4,32,768]{3,2,1,0:T(8,128)(2,1)S(1)} collective-permute-done((bf16[4,4,32,768]{3,2,1,0:T(8,128)(2,1)S(1)}, bf16[4,4,32,768]{3,2,1,0:T(8,128)(2,1)S(1)}, u32[]{:S(2)}, u32[]{:S(2)}) %collective-permute-start.31) | collective-permute-done | bytes 786464 | tf_op jit(solution)/shard_map/ppermute | solution.py:589
  153.1 1.9 %finish.1 = (f32[3,3,256,256]{3,2,1,0:T(8,128)}, f32[3,256,256]{2,1,0:T(8,128)}) custom-call(bf16[4,4,32,768]{3,2,1,0:T(8,128)(2,1)S(1)} %plane_place.1.mine_ref, bf16[4,4,32,768]{3,2,1,0:T(8,128)(2,1)S(1)} %collective-permute-done.31.got_ref), custom_call_target="tpu_custom_call" | custom-call | bytes 4194304 | tf_op jit(solution)/shard_map/finish/pallas_call | solution.py:20
  (42 shorter events, 0.2 us)
Async XLA Ops:
  1.7 11.6 %collective-permute-start.1 = (bf16[8,1,64,256]{3,2,1,0:T(8,128)(2,1)S(1)}, bf16[8,1,64,256]{3,2,1,0:T(8,128)(2,1)S(1)}, u32[]{:S(2)}, u32[]{:S(2)}) collective-permute-start(bf16[8,1,64,256]{3,2,1,0:T(8,128)(2,1)S(1)} %get-tuple-element.132), channel_id=1, source_target_pairs={{1,0},{2,1},{3,2},{5,4},{6,5},{7,6},{9,8},{10,9},{11,10},{13,12},{... | collective-permute-start | bytes 786440 | tf_op jit(solution)/shard_map/ppermute | solution.py:423
  3.0 11.1 %collective-permute-start = (bf16[8,1,64,256]{3,2,1,0:T(8,128)(2,1)S(1)}, bf16[8,1,64,256]{3,2,1,0:T(8,128)(2,1)S(1)}, u32[]{:S(2)}, u32[]{:S(2)}) collective-permute-start(bf16[8,1,64,256]{3,2,1,0:T(8,128)(2,1)S(1)} %get-tuple-element.133), channel_id=1, source_target_pairs={{0,1},{1,2},{2,3},{4,5},{5,6},{6,7},{8,9},{9,10},{10,11},{12,13},{... | collective-permute-start | bytes 786440 | tf_op jit(solution)/shard_map/ppermute | solution.py:423
  8.6 8.5 %copy-start = (bf16[8,8,64,256]{3,2,1,0:T(8,128)(2,1)S(1)}, bf16[8,8,64,256]{3,2,1,0:T(8,128)(2,1)}, u32[]{:S(2)}) copy-start(bf16[8,8,64,256]{3,2,1,0:T(8,128)(2,1)} %refs_3_.1) | copy-start | bytes 6291460
  8.6 8.5 %copy-start.3 = (bf16[3,3,256,256]{3,2,1,0:T(8,128)(2,1)S(1)}, bf16[3,3,256,256]{3,2,1,0:T(8,128)(2,1)}, u32[]{:S(2)}) copy-start(bf16[3,3,256,256]{3,2,1,0:T(8,128)(2,1)} %spatial_ref.1) | copy-start | bytes 3538948
  8.6 33.2 %collective-permute-start.6 = (bf16[8,512,256]{2,1,0:T(8,128)(2,1)}, bf16[8,512,256]{2,1,0:T(8,128)(2,1)S(1)}, u32[]{:S(2)}, u32[]{:S(2)}) collective-permute-start(bf16[8,512,256]{2,1,0:T(8,128)(2,1)} %bitcast.4), channel_id=1, source_target_pairs={{4,0},{8,4},{12,8},{20,16},{24,20},{28,24},{5,1},{9,5},{13,9},{21,... | collective-permute-start | bytes 6291464 | tf_op jit(solution)/shard_map/ppermute | solution.py:423
  10.2 31.7 %collective-permute-start.5 = (bf16[8,512,256]{2,1,0:T(8,128)(2,1)}, bf16[8,512,256]{2,1,0:T(8,128)(2,1)S(1)}, u32[]{:S(2)}, u32[]{:S(2)}) collective-permute-start(bf16[8,512,256]{2,1,0:T(8,128)(2,1)} %bitcast.5), channel_id=1, source_target_pairs={{0,4},{4,8},{8,12},{16,20},{20,24},{24,28},{1,5},{5,9},{9,13},{17,... | collective-permute-start | bytes 6291464 | tf_op jit(solution)/shard_map/ppermute | solution.py:423
  15.8 16.7 %collective-permute-start.3 = (bf16[4,512,256]{2,1,0:T(8,128)(2,1)S(1)}, bf16[4,512,256]{2,1,0:T(8,128)(2,1)S(1)}, u32[]{:S(2)}, u32[]{:S(2)}) collective-permute-start(bf16[4,512,256]{2,1,0:T(8,128)(2,1)S(1)} %get-tuple-element.130), channel_id=1, source_target_pairs={{12,28},{16,0},{13,29},{17,1},{14,30},{18,2},{15,31},{19,3}} | collective-permute-start | bytes 3145736 | tf_op jit(solution)/shard_map/ppermute | solution.py:462
  22.8 4.3 %collective-permute-start.2 = (f32[8,2,256]{2,1,0:T(2,128)S(1)}, f32[8,2,256]{2,1,0:T(2,128)S(1)}, u32[]{:S(2)}, u32[]{:S(2)}) collective-permute-start(f32[8,2,256]{2,1,0:T(2,128)S(1)} %get-tuple-element.71), channel_id=1, source_target_pairs={{0,1},{1,0},{2,3},{3,2},{4,5},{5,4},{6,7},{7,6},{8,9},{9,8},{10,11... | collective-permute-start | bytes 49160 | tf_op jit(solution)/shard_map/ppermute | solution.py:432
  25.3 30.8 %collective-permute-start.9 = (bf16[4,512,256]{2,1,0:T(8,128)(2,1)S(1)}, bf16[4,512,256]{2,1,0:T(8,128)(2,1)S(1)}, u32[]{:S(2)}, u32[]{:S(2)}) collective-permute-start(bf16[4,512,256]{2,1,0:T(8,128)(2,1)S(1)} %get-tuple-element.86), channel_id=1, source_target_pairs={{12,16},{16,12},{13,17},{17,13},{14,18},{18,14},{15,19},{19,15}} | collective-permute-start | bytes 3145736 | tf_op jit(solution)/shard_map/ppermute | solution.py:471
  32.5 23.7 %collective-permute-start.10 = (bf16[4,512,256]{2,1,0:T(8,128)(2,1)S(1)}, bf16[4,512,256]{2,1,0:T(8,128)(2,1)S(1)}, u32[]{:S(2)}, u32[]{:S(2)}) collective-permute-start(bf16[4,512,256]{2,1,0:T(8,128)(2,1)S(1)} %collective-permute-done.3), channel_id=1, source_target_pairs={{28,16},{0,12},{29,17},{1,13},{30,18},{2,14},{31,19},{3,15}} | collective-permute-start | bytes 3145736 | tf_op jit(solution)/shard_map/ppermute | solution.py:475
  33.8 5.9 %collective-permute-start.4 = (f32[8,2,256]{2,1,0:T(2,128)S(1)}, f32[8,2,256]{2,1,0:T(2,128)S(1)}, u32[]{:S(2)}, u32[]{:S(2)}) collective-permute-start(f32[8,2,256]{2,1,0:T(2,128)S(1)} %add.6.refs_0_), channel_id=1, source_target_pairs={{0,2},{1,3},{2,0},{3,1},{4,6},{5,7},{6,4},{7,5},{8,10},{9,11},{10,... | collective-permute-start | bytes 49160 | tf_op jit(solution)/shard_map/ppermute | solution.py:432
  39.8 6.9 %copy-start.2 = (bf16[3,256,256]{2,1,0:T(8,128)(2,1)S(1)}, bf16[3,256,256]{2,1,0:T(8,128)(2,1)}, u32[]{:S(2)}) copy-start(bf16[3,256,256]{2,1,0:T(8,128)(2,1)} %temporal_ref.1) | copy-start | bytes 1179652
  39.8 7.4 %copy-start.4 = (s32[2]{0:T(128)S(1)}, s32[2]{0:T(128)}, u32[]{:S(2)}) copy-start(s32[2]{0:T(128)} %clip_ref.5) | copy-start | bytes 28
  39.8 7.4 %copy-start.6 = (f32[256]{0:T(256)S(1)}, f32[256]{0:T(256)}, u32[]{:S(2)}) copy-start(f32[256]{0:T(256)} %param.12) | copy-start | bytes 3076
  39.8 7.4 %copy-start.7 = (f32[256]{0:T(256)S(1)}, f32[256]{0:T(256)}, u32[]{:S(2)}) copy-start(f32[256]{0:T(256)} %param.13) | copy-start | bytes 3076
  41.8 11.4 %collective-permute-start.7 = (bf16[8,64,256]{2,1,0:T(8,128)(2,1)S(1)}, bf16[8,64,256]{2,1,0:T(8,128)(2,1)S(1)}, u32[]{:S(2)}, u32[]{:S(2)}) collective-permute-start(bf16[8,64,256]{2,1,0:T(8,128)(2,1)S(1)} %get-tuple-element.80), channel_id=1, source_target_pairs={{0,1},{1,2},{2,3},{4,5},{5,6},{6,7},{8,9},{9,10},{10,11},{12,13},{... | collective-permute-start | bytes 786440 | tf_op jit(solution)/shard_map/ppermute | solution.py:423
  45.4 10.8 %collective-permute-start.8 = (bf16[8,64,256]{2,1,0:T(8,128)(2,1)S(1)}, bf16[8,64,256]{2,1,0:T(8,128)(2,1)S(1)}, u32[]{:S(2)}, u32[]{:S(2)}) collective-permute-start(bf16[8,64,256]{2,1,0:T(8,128)(2,1)S(1)} %get-tuple-element.81), channel_id=1, source_target_pairs={{1,0},{2,1},{3,2},{5,4},{6,5},{7,6},{9,8},{10,9},{11,10},{13,12},{... | collective-permute-start | bytes 786440 | tf_op jit(solution)/shard_map/ppermute | solution.py:423
  47.2 9.0 %copy-start.1 = (bf16[8,8,64,256]{3,2,1,0:T(8,128)(2,1)S(1)}, bf16[8,8,64,256]{3,2,1,0:T(8,128)(2,1)}, u32[]{:S(2)}) copy-start(bf16[8,8,64,256]{3,2,1,0:T(8,128)(2,1)} %cot_ref.1) | copy-start | bytes 6291460
  47.2 9.0 %copy-start.5 = (s32[2]{0:T(128)S(1)}, s32[2]{0:T(128)}, u32[]{:S(2)}) copy-start(s32[2]{0:T(128)} %dil_ref.3) | copy-start | bytes 28
  60.3 37.8 %collective-permute-start.17 = (bf16[8,512,256]{2,1,0:T(8,128)(2,1)S(1)}, bf16[8,512,256]{2,1,0:T(8,128)(2,1)S(1)}, u32[]{:S(2)}, u32[]{:S(2)}) collective-permute-start(bf16[8,512,256]{2,1,0:T(8,128)(2,1)S(1)} %get-tuple-element.123.act_ref.own), channel_id=1, source_target_pairs={{4,0},{8,4},{12,8},{20,16},{24,20},{28,24},{5,1},{9,5},{13,9},{21,... | collective-permute-start | bytes 6291464 | tf_op jit(solution)/shard_map/ppermute | solution.py:423
  61.6 44.2 %collective-permute-start.16 = (bf16[8,512,256]{2,1,0:T(8,128)(2,1)S(1)}, bf16[8,512,256]{2,1,0:T(8,128)(2,1)S(1)}, u32[]{:S(2)}, u32[]{:S(2)}) collective-permute-start(bf16[8,512,256]{2,1,0:T(8,128)(2,1)S(1)} %get-tuple-element.123.act_ref.own), channel_id=1, source_target_pairs={{0,4},{4,8},{8,12},{16,20},{20,24},{24,28},{1,5},{5,9},{9,13},{17,... | collective-permute-start | bytes 6291464 | tf_op jit(solution)/shard_map/ppermute | solution.py:423
  64.8 5.3 %collective-permute-start.11 = (f32[8,2,256]{2,1,0:T(2,128)S(1)}, f32[8,2,256]{2,1,0:T(2,128)S(1)}, u32[]{:S(2)}, u32[]{:S(2)}) collective-permute-start(f32[8,2,256]{2,1,0:T(2,128)S(1)} %get-tuple-element.92), channel_id=1, source_target_pairs={{0,1},{1,0},{2,3},{3,2},{4,5},{5,4},{6,7},{7,6},{8,9},{9,8},{10,11... | collective-permute-start | bytes 49160 | tf_op jit(solution)/shard_map/ppermute | solution.py:432
  65.1 22.5 %collective-permute-start.13 = (bf16[8,64,256]{2,1,0:T(8,128)(2,1)S(1)}, bf16[8,64,256]{2,1,0:T(8,128)(2,1)S(1)}, u32[]{:S(2)}, u32[]{:S(2)}) collective-permute-start(bf16[8,64,256]{2,1,0:T(8,128)(2,1)S(1)} %get-tuple-element.95), channel_id=1, source_target_pairs={{0,1},{1,2},{2,3},{4,5},{5,6},{6,7},{8,9},{9,10},{10,11},{12,13},{... | collective-permute-start | bytes 786440 | tf_op jit(solution)/shard_map/ppermute | solution.py:423
  68.8 18.9 %collective-permute-start.14 = (bf16[8,64,256]{2,1,0:T(8,128)(2,1)S(1)}, bf16[8,64,256]{2,1,0:T(8,128)(2,1)S(1)}, u32[]{:S(2)}, u32[]{:S(2)}) collective-permute-start(bf16[8,64,256]{2,1,0:T(8,128)(2,1)S(1)} %get-tuple-element.96), channel_id=1, source_target_pairs={{1,0},{2,1},{3,2},{5,4},{6,5},{7,6},{9,8},{10,9},{11,10},{13,12},{... | collective-permute-start | bytes 786440 | tf_op jit(solution)/shard_map/ppermute | solution.py:423
  70.1 9.6 %collective-permute-start.12 = (f32[8,2,256]{2,1,0:T(2,128)S(1)}, f32[8,2,256]{2,1,0:T(2,128)S(1)}, u32[]{:S(2)}, u32[]{:S(2)}) collective-permute-start(f32[8,2,256]{2,1,0:T(2,128)S(1)} %add.7.refs_2_), channel_id=1, source_target_pairs={{0,2},{1,3},{2,0},{3,1},{4,6},{5,7},{6,4},{7,5},{8,10},{9,11},{10,... | collective-permute-start | bytes 49160 | tf_op jit(solution)/shard_map/ppermute | solution.py:432
  89.9 2.4 %collective-permute-start.15 = (bf16[4,4,32,768]{3,2,1,0:T(8,128)(2,1)S(1)}, bf16[4,4,32,768]{3,2,1,0:T(8,128)(2,1)S(1)}, u32[]{:S(2)}, u32[]{:S(2)}) collective-permute-start(bf16[4,4,32,768]{3,2,1,0:T(8,128)(2,1)S(1)} %get-tuple-element.100), channel_id=1, source_target_pairs={{0,4},{4,0},{8,12},{12,8},{16,20},{20,16},{24,28},{28,24},{1,5},{5... | collective-permute-start | bytes 2359304 | tf_op jit(solution)/shard_map/ppermute | solution.py:539
  90.1 24.5 %collective-permute-start.18 = (bf16[4,512,256]{2,1,0:T(8,128)(2,1)S(1)}, bf16[4,512,256]{2,1,0:T(8,128)(2,1)S(1)}, u32[]{:S(2)}, u32[]{:S(2)}) collective-permute-start(bf16[4,512,256]{2,1,0:T(8,128)(2,1)S(1)} %slice.22), channel_id=1, source_target_pairs={{12,28},{16,0},{13,29},{17,1},{14,30},{18,2},{15,31},{19,3}} | collective-permute-start | bytes 3145736 | tf_op jit(solution)/shard_map/ppermute | solution.py:508
  92.4 22.2 %collective-permute-start.19 = (bf16[4,32,768]{2,1,0:T(8,128)(2,1)S(1)}, bf16[4,32,768]{2,1,0:T(8,128)(2,1)S(1)}, u32[]{:S(2)}, u32[]{:S(2)}) collective-permute-start(bf16[4,32,768]{2,1,0:T(8,128)(2,1)S(1)} %get-tuple-element.112), channel_id=1, source_target_pairs={{0,8},{4,12},{8,0},{12,4},{16,24},{20,28},{24,16},{28,20},{1,9},{5... | collective-permute-start | bytes 589832 | tf_op jit(solution)/shard_map/ppermute | solution.py:544
  92.5 24.2 %collective-permute-start.20 = (bf16[4,32,768]{2,1,0:T(8,128)(2,1)S(1)}, bf16[4,32,768]{2,1,0:T(8,128)(2,1)S(1)}, u32[]{:S(2)}, u32[]{:S(2)}) collective-permute-start(bf16[4,32,768]{2,1,0:T(8,128)(2,1)S(1)} %get-tuple-element.113), channel_id=1, source_target_pairs={{0,16},{4,20},{8,24},{12,28},{16,0},{20,4},{24,8},{28,12},{1,17},{... | collective-permute-start | bytes 589832 | tf_op jit(solution)/shard_map/ppermute | solution.py:544
  98.1 18.6 %collective-permute-start.21 = (bf16[4,32,768]{2,1,0:T(8,128)(2,1)S(1)}, bf16[4,32,768]{2,1,0:T(8,128)(2,1)S(1)}, u32[]{:S(2)}, u32[]{:S(2)}) collective-permute-start(bf16[4,32,768]{2,1,0:T(8,128)(2,1)S(1)} %get-tuple-element.114), channel_id=1, source_target_pairs={{0,24},{4,28},{8,16},{12,20},{16,8},{20,12},{24,0},{28,4},{1,25},{... | collective-permute-start | bytes 589832 | tf_op jit(solution)/shard_map/ppermute | solution.py:544
  116.9 28.7 %collective-permute-start.26 = (bf16[4,512,256]{2,1,0:T(8,128)(2,1)S(1)}, bf16[4,512,256]{2,1,0:T(8,128)(2,1)S(1)}, u32[]{:S(2)}, u32[]{:S(2)}) collective-permute-start(bf16[4,512,256]{2,1,0:T(8,128)(2,1)S(1)} %slice.23), channel_id=1, source_target_pairs={{12,16},{16,12},{13,17},{17,13},{14,18},{18,14},{15,19},{19,15}} | collective-permute-start | bytes 3145736 | tf_op jit(solution)/shard_map/ppermute | solution.py:566
  117.6 27.9 %collective-permute-start.27 = (bf16[4,512,256]{2,1,0:T(8,128)(2,1)S(1)}, bf16[4,512,256]{2,1,0:T(8,128)(2,1)S(1)}, u32[]{:S(2)}, u32[]{:S(2)}) collective-permute-start(bf16[4,512,256]{2,1,0:T(8,128)(2,1)S(1)} %collective-permute-done.18), channel_id=1, source_target_pairs={{28,16},{0,12},{29,17},{1,13},{30,18},{2,14},{31,19},{3,15}} | collective-permute-start | bytes 3145736 | tf_op jit(solution)/shard_map/ppermute | solution.py:567
  121.6 5.5 %collective-permute-start.22 = (bf16[2,32,768]{2,1,0:T(8,128)(2,1)S(1)}, bf16[2,32,768]{2,1,0:T(8,128)(2,1)S(1)}, u32[]{:S(2)}, u32[]{:S(2)}) collective-permute-start(bf16[2,32,768]{2,1,0:T(8,128)(2,1)S(1)} %get-tuple-element.118), channel_id=1, source_target_pairs={{0,1},{1,0},{2,3},{3,2},{4,5},{5,4},{6,7},{7,6},{8,9},{9,8},{10,11... | collective-permute-start | bytes 294920 | tf_op jit(solution)/shard_map/ppermute | solution.py:569
  127.1 5.1 %collective-permute-start.23 = (bf16[1,32,768]{2,1,0:T(8,128)(2,1)S(1)}, bf16[1,32,768]{2,1,0:T(8,128)(2,1)S(1)}, u32[]{:S(2)}, u32[]{:S(2)}) collective-permute-start(bf16[1,32,768]{2,1,0:T(8,128)(2,1)S(1)} %get-tuple-element.120), channel_id=1, source_target_pairs={{0,2},{1,3},{2,0},{3,1},{4,6},{5,7},{6,4},{7,5},{8,10},{9,11},{10,... | collective-permute-start | bytes 147464 | tf_op jit(solution)/shard_map/ppermute | solution.py:569
  132.2 5.1 %collective-permute-start.24 = (bf16[1,32,768]{2,1,0:T(8,128)(2,1)S(1)}, bf16[1,32,768]{2,1,0:T(8,128)(2,1)S(1)}, u32[]{:S(2)}, u32[]{:S(2)}) collective-permute-start(bf16[1,32,768]{2,1,0:T(8,128)(2,1)S(1)} %line_total.1.mine_ref), channel_id=1, source_target_pairs={{0,2},{1,3},{2,0},{3,1},{4,6},{5,7},{6,4},{7,5},{8,10},{9,11},{10,... | collective-permute-start | bytes 147464 | tf_op jit(solution)/shard_map/ppermute | solution.py:572
  137.3 4.7 %collective-permute-start.25 = (bf16[2,32,768]{2,1,0:T(8,128)(2,1)S(1)}, bf16[2,32,768]{2,1,0:T(8,128)(2,1)S(1)}, u32[]{:S(2)}, u32[]{:S(2)}) collective-permute-start(bf16[2,32,768]{2,1,0:T(8,128)(2,1)S(1)} %line_weave.2.mine_ref), channel_id=1, source_target_pairs={{0,1},{1,0},{2,3},{3,2},{4,5},{5,4},{6,7},{7,6},{8,9},{9,8},{10,11... | collective-permute-start | bytes 294920 | tf_op jit(solution)/shard_map/ppermute | solution.py:572
  142.0 8.7 %collective-permute-start.30 = (bf16[4,32,768]{2,1,0:T(8,128)(2,1)S(1)}, bf16[4,32,768]{2,1,0:T(8,128)(2,1)S(1)}, u32[]{:S(2)}, u32[]{:S(2)}) collective-permute-start(bf16[4,32,768]{2,1,0:T(8,128)(2,1)S(1)} %line_weave.3.refs_0_), channel_id=1, source_target_pairs={{0,24},{4,28},{8,16},{12,20},{16,8},{20,12},{24,0},{28,4},{1,25},{... | collective-permute-start | bytes 589832 | tf_op jit(solution)/shard_map/ppermute | solution.py:577
  142.1 8.6 %collective-permute-start.29 = (bf16[4,32,768]{2,1,0:T(8,128)(2,1)S(1)}, bf16[4,32,768]{2,1,0:T(8,128)(2,1)S(1)}, u32[]{:S(2)}, u32[]{:S(2)}) collective-permute-start(bf16[4,32,768]{2,1,0:T(8,128)(2,1)S(1)} %line_weave.3.refs_0_), channel_id=1, source_target_pairs={{0,16},{4,20},{8,24},{12,28},{16,0},{20,4},{24,8},{28,12},{1,17},{... | collective-permute-start | bytes 589832 | tf_op jit(solution)/shard_map/ppermute | solution.py:577
  142.1 8.6 %collective-permute-start.28 = (bf16[4,32,768]{2,1,0:T(8,128)(2,1)S(1)}, bf16[4,32,768]{2,1,0:T(8,128)(2,1)S(1)}, u32[]{:S(2)}, u32[]{:S(2)}) collective-permute-start(bf16[4,32,768]{2,1,0:T(8,128)(2,1)S(1)} %line_weave.3.refs_0_), channel_id=1, source_target_pairs={{0,8},{4,12},{8,0},{12,4},{16,24},{20,28},{24,16},{28,20},{1,9},{5... | collective-permute-start | bytes 589832 | tf_op jit(solution)/shard_map/ppermute | solution.py:577
  150.8 2.4 %collective-permute-start.31 = (bf16[4,4,32,768]{3,2,1,0:T(8,128)(2,1)S(1)}, bf16[4,4,32,768]{3,2,1,0:T(8,128)(2,1)S(1)}, u32[]{:S(2)}, u32[]{:S(2)}) collective-permute-start(bf16[4,4,32,768]{3,2,1,0:T(8,128)(2,1)S(1)} %plane_place.1.mine_ref), channel_id=1, source_target_pairs={{0,4},{4,0},{8,12},{12,8},{16,20},{20,16},{24,28},{28,24},{1,5},{5... | collective-permute-start | bytes 2359304 | tf_op jit(solution)/shard_map/ppermute | solution.py:589
